TPU v7x, 256 devices: a whole 4x4x8 slice. The times are simulated.
256 devices in a mesh: replica: 32 (over z_hi, x, core), tensor: 8 (over z_lo, y).
Axes of the slice: x: 4, y: 4, z: 8 (z_hi: 4, z_lo: 2; z = z_hi * 2 + z_lo), core: 2. Of those that a mesh axis runs over, the one named last changes fastest.
Arguments:
- activations: bfloat16 [24576, 2048], P('replica'), may hold values from -6 to 6
- out_grads: bfloat16 [24576, 10240], P('replica', 'tensor'), may hold values from -0.21875 to 0.21875
- exponents: int32 [2048, 40], P(None, 'tensor'), may hold values from -6 to -3
- signs: int32 [10240], P('tensor'), may hold values from -1 to 1, as said below
- master: float32 [2048, 10240], P('replica', 'tensor'), may hold values from -0.006 to 0.006
- moment: float32 [2048, 10240], P('replica', 'tensor'), may hold values from -0.06 to 0.06
- second: float32 [2048, 10240], P('replica', 'tensor'), may hold values from 0.01 to 0.03
Outputs:
- grad_mean: float32 [2048, 10240], P('replica', 'tensor')
- moment_new: float32 [2048, 10240], P('replica', 'tensor')
- second_new: float32 [2048, 10240], P('replica', 'tensor')
- master_new: float32 [2048, 10240], P('replica', 'tensor')
- weights: bfloat16 [2048, 10240], P(None, 'tensor')
Inputs may be any that keep to these rules, and one draw needn't show every extreme that they name: `signs`: every entry is -1 or +1.
All inputs are finite; a program needn't handle non-finite values.
Results may differ from a plain program's by a relative error of at most 0.018.
Values may be sent and summed in bfloat16 or wider, within the bound.
No kernel may reach another device: no remote copies, remote signals or barrier semaphores. Data moves between devices by JAX's collectives and lax.ppermute only.
A program may use at most 64 MiB of HBM per device.

v0:
```python
import math

import jax
import jax.numpy as jnp
import numpy as np
from jax import lax
from jax.sharding import PartitionSpec as P

TILE = 256


beta_one = 0.9
beta_two = 0.95
epsilon = 1e-08
decay_rate = 0.1
learn_rate = 0.001
step_number = 100.0


def hadamard_table(order):
    positions = np.arange(order)
    intersection = positions[:, None] & positions[None, :]
    parity = np.zeros((order, order))
    for level in range(order.bit_length()):
        parity = parity + intersection // 2**level % 2
    return np.where(parity % 2 == 0, 1.0, -1.0) / math.sqrt(order)


def on_device(activations, out_grads, exponents, signs, master, moment, second):
    replicas = lax.axis_size("replica")
    rows_owned = master.shape[0]
    columns = master.shape[1]
    tile_count = columns // TILE
    table = jnp.asarray(hadamard_table(TILE), jnp.bfloat16)
    table_float = jnp.asarray(hadamard_table(TILE), jnp.float32)
    sign_bf = signs.astype(jnp.bfloat16)
    sign_float = signs.astype(jnp.float32)
    partial_value = lax.dot_general(
        activations, out_grads, (((0,), (0,)), ((), ())), preferred_element_type=jnp.float32
    ).astype(jnp.bfloat16)
    flipped = partial_value * sign_bf
    rotated = jnp.einsum(
        "rtk,kj->rtj",
        flipped.reshape(rows_owned * lax.axis_size("replica"), tile_count, TILE),
        table,
        preferred_element_type=jnp.float32,
    ).reshape(rows_owned * lax.axis_size("replica"), columns)
    tile_exps = exponents.astype(jnp.float32)
    shrink = jnp.exp2(-jnp.repeat(tile_exps, TILE, axis=1))
    summed = lax.psum_scatter(
        jnp.clip(rotated * shrink, -127.0, 127.0).astype(jnp.bfloat16),
        "replica",
        scatter_dimension=0,
        tiled=True,
    ).astype(jnp.float32)
    owner = lax.axis_index("replica")
    own_exps = lax.dynamic_slice_in_dim(exponents, owner * rows_owned, rows_owned, 0).astype(
        jnp.float32
    )
    decoded = summed * jnp.exp2(jnp.repeat(own_exps, TILE, axis=1))
    restored = jnp.einsum(
        "rtk,kj->rtj",
        decoded.reshape(rows_owned, tile_count, TILE),
        table_float,
        precision=lax.Precision.HIGHEST,
    ).reshape(rows_owned, columns)
    grad_mean = restored * sign_float / replicas
    moment_new = beta_one * moment + (1.0 - beta_one) * grad_mean
    second_new = beta_two * second + (1.0 - beta_two) * grad_mean * grad_mean
    first_fix = 1.0 - beta_one**step_number
    second_fix = 1.0 - beta_two**step_number
    update = (
        moment_new / first_fix / (jnp.sqrt(second_new / second_fix) + epsilon) + decay_rate * master
    )
    master_new = master - learn_rate * update
    gathered = lax.all_gather(master_new.astype(jnp.bfloat16), "replica", axis=0, tiled=True)
    return (grad_mean, moment_new, second_new, master_new, gathered)


def solution(mesh):
    in_specs = (
        P("replica", None),
        P("replica", "tensor"),
        P(None, "tensor"),
        P("tensor"),
        P("replica", "tensor"),
        P("replica", "tensor"),
        P("replica", "tensor"),
    )
    out_specs = (
        P("replica", "tensor"),
        P("replica", "tensor"),
        P("replica", "tensor"),
        P("replica", "tensor"),
        P(None, "tensor"),
    )
    return jax.shard_map(
        on_device, mesh=mesh, in_specs=in_specs, out_specs=out_specs, check_vma=False
    )
```

profile of v0, /device:TPU:1, one launch (start us, length us, event | category | flops | bytes accessed | tf_op | source)
XLA Modules:
  0.0 214.8 jit_solution(8873477375073386631)
XLA Ops:
  7.2 0.0 copy-start
  7.2 0.0 reduce-scatter.2.cloned.1.call-start
  7.2 0.9 fusion.4
  8.1 0.9 multiply_exponential_fusion
  9.0 0.1 copy-done
  9.1 0.0 copy-start.1
  9.1 6.1 %fusion = bf16[2048,1280]{0,1:T(8,128)(2,1)S(1)} fusion(bf16[768,2048]{1,0:T(8,128)(2,1)S(1)} %copy-done, bf16[768,1280]{1,0:T(8,128)(2,1)} %param.10, bf16[1280]{0:T(1024)(128)(2,1)S(1)} %get-tuple-element.11), kind=kOutput, calls=%fused_computation.2 | convolution fusion | flops 4031774720 | bytes 10357248 | tf_op jit(solution)/shard_map/dot_general | solution.py:38
  15.2 0.0 copy-done.1
  15.2 3.9 %clamp_convert_fusion = bf16[2048,5,256]{0,2,1:T(8,128)(2,1)} fusion(f32[2048,5]{0,1:T(8,128)S(1)} %multiply_exponential_fusion, bf16[256,256,1]{0,1,2:T(8,128)(2,1)S(1)} %copy-done.1, bf16[2048,5,256]{0,2,1:T(8,128)(2,1)S(1)} %bitcast.23), kind=kOutput, calls=%fused_computation | convolution fusion | flops 1350041600 | bytes 10657792 | tf_op jit(solution)/shard_map/rtk,kj->rtj/dot_general | solution.py:42
  19.1 7.9 %copy.21 = bf16[2048,1280]{1,0:T(8,128)(2,1)} copy(bf16[2048,1280]{0,1:T(8,128)(2,1)} %bitcast.18) | data formatting | bytes 10485760 | tf_op jit(solution)/shard_map/convert_element_type | solution.py:51
  27.0 0.0 reduce-scatter.2.cloned.1.call-update
  27.0 0.0 all-gather.2.cloned.1.call-start
  27.1 0.8 multiply_exponential_fusion.1
  27.8 0.1 copy.22
  27.9 0.1 broadcast_in_dim.9
  28.1 0.1 copy.28
  28.2 105.9 %reduce-scatter.2.cloned.1.call-done = bf16[64,1280]{1,0:T(8,128)(2,1)} async-done(((bf16[2048,1280]{1,0:T(8,128)(2,1)}), bf16[64,1280]{1,0:T(8,128)(2,1)}) %reduce-scatter.2.cloned.1.call-update) | async-done | bytes 163856 | tf_op jit(solution)/shard_map/reduce_scatter | solution.py:50
  134.1 0.9 convert_multiply_fusion
  135.0 1.4 convolution_bitcast_fusion
  136.4 2.5 %fusion.3 = (bf16[64,1280]{1,0:T(8,128)(2,1)}, f32[64,1280]{1,0:T(8,128)}, f32[64,1280]{1,0:T(8,128)}, f32[64,1280]{1,0:T(8,128)}, f32[64,1280]{1,0:T(8,128)}) fusion(f32[64,1280]{1,0:T(8,128)} %param.13, f32[64,1280]{1,0:T(8,128)S(1)} %bitcast.22, f32[1280]{0:T(1024)S(1)} %get-tuple-element.10, f32[64,1280]{1,0:T(8,128)} %param.15, f32[64,1280]{1,0:T(8,128)} %param.14), kind=kLoop, calls=%fused_computation.13 | loop fusion | flops 1474560 | bytes 2790400 | tf_op jit(solution)/shard_map/convert_element_type | solution.py:76
  138.9 0.0 all-gather.2.cloned.1.call-update
  138.9 63.9 %all-gather.2.cloned.1.call-done = bf16[2048,1280]{1,0:T(8,128)(2,1)} async-done(((bf16[64,1280]{1,0:T(8,128)(2,1)}), bf16[2048,1280]{1,0:T(8,128)(2,1)}) %all-gather.2.cloned.1.call-update) | async-done | bytes 5242896 | tf_op jit(solution)/shard_map/all_gather | solution.py:76
  202.8 5.2 %copy.34 = bf16[2048,1280]{1,0:T(8,128)(2,1)} copy(bf16[2048,1280]{1,0:T(8,128)(2,1)} %all-gather.2.cloned.1.call-done) | data formatting | bytes 10485760
  (1 shorter events, 0.0 us)
Async XLA Ops:
  7.2 1.9 copy-start
  7.2 126.9 %reduce-scatter.2.cloned.1.call-start = ((), (), s32[]{:S(2)}) async-start(), calls=%async_computation.1 | async-start | bytes 5406720 | tf_op jit(solution)/shard_map/reduce_scatter | solution.py:50
  9.1 6.1 %copy-start.1 = (bf16[256,256,1]{0,1,2:T(8,128)(2,1)S(1)}, bf16[256,256,1]{0,1,2:T(8,128)(2,1)}, u32[]{:S(2)}) copy-start(bf16[256,256,1]{0,1,2:T(8,128)(2,1)} %constant.50) | copy-start | bytes 393220
  27.0 175.7 %all-gather.2.cloned.1.call-start = ((), (), s32[]{:S(2)}) async-start(), calls=%async_computation.2 | async-start | bytes 5406720 | tf_op jit(solution)/shard_map/all_gather | solution.py:76
Sparse Core Ops, SparseCore 0:
  27.1 106.8 reduce-scatter.1
  139.0 63.7 all-gather.1
where the time goes:
time: 215 us
  waiting for transfers between devices  170 us (79%)
  between operations  14.1 us (7%)
  local copies, waits for them, and re-layouts  13.5 us (6%)
  matrix products  11.4 us (5%)
  other arithmetic  5.94 us (3%)
    reduce_scatter x1, waiting for transfers between devices, on_device(): lax.psum_scatter(jnp.clip(rotated * shrink, -127.0, 127.0).astype(jnp.bfl...  106 us
    all_gather x1, waiting for transfers between devices, on_device(): lax.all_gather(master_new.astype(jnp.bfloat16), 'replica', axis=0, tiled=...  63.9 us
    convert_element_type x1, local copies, waits for them, and re-layouts, on_device(): jnp.clip(rotated * shrink, -127.0, 127.0).astype(jnp.bfloat16)  7.88 us
    dot_general x1, matrix products, on_device(): lax.dot_general(activations, out_grads, (((0,), (0,)), ((), ())), preferr...  6.1 us
    unnamed x6, local copies, waits for them, and re-layouts  5.38 us
  transfers between devices with their start and end apart: 2, of which 2 were waited for; matrix products, arithmetic and copies ran while one was open for 1% of the time, Pallas kernels for 0%

commit v1 on v0

v1 whole, which is shorter than its diff:
```python
import functools
import math

import jax
import jax.numpy as jnp
import numpy as np
from jax import lax
from jax.experimental import pallas as pl
from jax.experimental.pallas import tpu as pltpu
from jax.sharding import PartitionSpec as P

TILE = 256
NZ, NX, NC = 4, 4, 2
ROW = 64
COLS = 1280
COLS_A = 896
COLS_B = COLS - COLS_A
TOK = 768

beta_one = 0.9
beta_two = 0.95
epsilon = 1e-08
decay_rate = 0.1
learn_rate = 0.001
step_number = 100.0

F32 = jnp.float32
BF = jnp.bfloat16


def hadamard_table(order):
    positions = np.arange(order)
    intersection = positions[:, None] & positions[None, :]
    parity = np.zeros((order, order))
    for level in range(order.bit_length()):
        parity = parity + intersection // 2**level % 2
    return np.where(parity % 2 == 0, 1.0, -1.0) / math.sqrt(order)


def replica_perm(dz=0, dx=0, dc=0):
    pairs = []
    for z in range(NZ):
        for x in range(NX):
            for c in range(NC):
                to = (((z + dz) % NZ) * NX + (x + dx) % NX) * NC + (c + dc) % NC
                pairs.append(((z * NX + x) * NC + c, to))
    return pairs


def send(value, **shift):
    return lax.ppermute(value, "replica", replica_perm(**shift))


def quant_kernel(first, width, meta, act, grads, exps, signs, table, mine, theirs, rotated):
    @pl.when(pl.program_id(0) == 0)
    def _():
        lo = first // TILE
        for tile in range(lo, -(-(first + width) // TILE)):
            flipped = grads[:, tile * TILE : (tile + 1) * TILE] * signs[
                :, tile * TILE : (tile + 1) * TILE
            ].astype(BF)
            turned = jnp.dot(flipped, table[...], preferred_element_type=F32).astype(BF)
            a = max(first, tile * TILE)
            b = min(first + width, (tile + 1) * TILE)
            rotated[:, a - first : b - first] = turned[:, a - tile * TILE : b - tile * TILE]

    total = lax.dot_general(
        act[...], rotated[...], (((0,), (0,)), ((), ())), preferred_element_type=F32
    )
    shrink = jnp.exp2(-exps[...].astype(F32))
    core = meta[2]
    for tile in range(first // TILE, -(-(first + width) // TILE)):
        a = max(first, tile * TILE) - first
        b = min(first + width, (tile + 1) * TILE) - first
        part = jnp.clip(total[:, a:b] * shrink[:, tile : tile + 1], -127.0, 127.0).astype(BF)
        top, bottom = part[:ROW], part[ROW:]
        mine[0, 0, :, a:b] = jnp.where(core == 0, top, bottom)
        theirs[0, 0, :, a:b] = jnp.where(core == 0, bottom, top)


def quantized(first, width, x_outer, meta, act, grads, exps, signs, table):
    def group(i, meta):
        if x_outer:
            dx, dz = i // NZ, lax.rem(i, NZ)
        else:
            dz, dx = i // NX, lax.rem(i, NX)
        return lax.rem(meta[0] + dz, NZ) * NX + lax.rem(meta[1] + dx, NX)

    out = jax.ShapeDtypeStruct((4, 4, ROW, width), BF)
    out_spec = pl.BlockSpec((1, 1, ROW, width), lambda i, meta: (i // 4, lax.rem(i, 4), 0, 0))
    return pl.pallas_call(
        functools.partial(quant_kernel, first, width),
        grid_spec=pltpu.PrefetchScalarGridSpec(
            num_scalar_prefetch=1,
            grid=(NZ * NX,),
            in_specs=[
                pl.BlockSpec((TOK, 2 * ROW), lambda i, meta: (0, group(i, meta))),
                pl.BlockSpec((TOK, COLS), lambda i, meta: (0, 0)),
                pl.BlockSpec((2 * ROW, COLS // TILE), lambda i, meta: (group(i, meta), 0)),
                pl.BlockSpec((1, COLS), lambda i, meta: (0, 0)),
                pl.BlockSpec((TILE, TILE), lambda i, meta: (0, 0)),
            ],
            out_specs=[out_spec, out_spec],
            scratch_shapes=[pltpu.VMEM((TOK, width), BF)],
        ),
        out_shape=[out, out],
        compiler_params=pltpu.CompilerParams(vmem_limit_bytes=32 * 1024 * 1024),
        name="quantize",
    )(meta, act, grads, exps, signs, table)


def pair_kernel(mine, other, *outs):
    for k, out in enumerate(outs):
        out[...] = (mine[k].astype(F32) + other[k].astype(F32)).astype(BF)


def pair_sum(mine, other):
    width = mine.shape[-1]
    spec = pl.BlockSpec((4, 1, ROW, width), lambda i: (0, i, 0, 0))
    return pl.pallas_call(
        pair_kernel,
        grid=(4,),
        in_specs=[spec, spec],
        out_specs=[pl.BlockSpec((1, ROW, width), lambda i: (i, 0, 0))] * 4,
        out_shape=[jax.ShapeDtypeStruct((4, ROW, width), BF)] * 4,
        name="pair_sum",
    )(mine, other)


def quad_kernel(a, b, c, d, *outs):
    for k, out in enumerate(outs):
        out[...] = (
            (a[k].astype(F32) + b[k].astype(F32)) + (c[k].astype(F32) + d[k].astype(F32))
        ).astype(BF)


def quad_sum(parts):
    width = parts[0].shape[-1]
    return pl.pallas_call(
        quad_kernel,
        out_shape=[jax.ShapeDtypeStruct((ROW, width), BF)] * 4,
        name="quad_sum",
    )(*parts)


def update_kernel(*refs):
    a = refs[0:4]
    b = refs[4:8]
    exps, signs, table, master, moment, second = refs[8:14]
    grad_out, moment_out, second_out, master_out, weights_a, weights_b = refs[14:20]
    total_a = (a[0][...].astype(F32) + a[1][...].astype(F32)) + (
        a[2][...].astype(F32) + a[3][...].astype(F32)
    )
    total_b = (b[0][...].astype(F32) + b[1][...].astype(F32)) + (
        b[2][...].astype(F32) + b[3][...].astype(F32)
    )
    total = jnp.concatenate([total_a, total_b], axis=1)
    growth = jnp.exp2(exps[...].astype(F32))
    first_fix = 1.0 - beta_one**step_number
    second_fix = 1.0 - beta_two**step_number
    for tile in range(COLS // TILE):
        cut = slice(tile * TILE, (tile + 1) * TILE)
        decoded = total[:, cut] * growth[:, tile : tile + 1]
        high = decoded.astype(BF)
        rest = decoded - high.astype(F32)
        middle = rest.astype(BF)
        low = (rest - middle.astype(F32)).astype(BF)
        restored = jnp.dot(high, table[...], preferred_element_type=F32) + (
            jnp.dot(middle, table[...], preferred_element_type=F32)
            + jnp.dot(low, table[...], preferred_element_type=F32)
        )
        grad = restored * (signs[:, cut].astype(F32) * (1.0 / (NZ * NX * NC)))
        moment_new = beta_one * moment[:, cut] + (1.0 - beta_one) * grad
        second_new = beta_two * second[:, cut] + (1.0 - beta_two) * grad * grad
        update = (
            moment_new / first_fix / (jnp.sqrt(second_new / second_fix) + epsilon)
            + decay_rate * master[:, cut]
        )
        master_new = master[:, cut] - learn_rate * update
        grad_out[:, cut] = grad
        moment_out[:, cut] = moment_new
        second_out[:, cut] = second_new
        master_out[:, cut] = master_new
        weights = master_new.astype(BF)
        if (tile + 1) * TILE <= COLS_A:
            weights_a[:, cut] = weights
        elif tile * TILE >= COLS_A:
            weights_b[:, tile * TILE - COLS_A : (tile + 1) * TILE - COLS_A] = weights
        else:
            weights_a[:, tile * TILE : COLS_A] = weights[:, : COLS_A - tile * TILE]
            weights_b[:, : (tile + 1) * TILE - COLS_A] = weights[:, COLS_A - tile * TILE :]


def updated(parts_a, parts_b, exps, signs, table, master, moment, second):
    full = jax.ShapeDtypeStruct((ROW, COLS), F32)
    return pl.pallas_call(
        update_kernel,
        out_shape=[
            full,
            full,
            full,
            full,
            jax.ShapeDtypeStruct((ROW, COLS_A), BF),
            jax.ShapeDtypeStruct((ROW, COLS_B), BF),
        ],
        compiler_params=pltpu.CompilerParams(vmem_limit_bytes=32 * 1024 * 1024),
        name="update",
    )(*parts_a, *parts_b, exps, signs, table, master, moment, second)


def place_kernel(meta, *refs):
    pieces, out, sems = refs[:-2], refs[-2], refs[-1]
    zh, x, core = meta[0], meta[1], meta[2]
    copies = []
    for k, piece in enumerate(pieces):
        other, rest = k // 8, k % 8
        is_b, outer = rest // 4, rest % 4
        row_core = jnp.where(other == 1, 1 - core, core)
        for inner in range(4):
            dx, dz = (inner, outer) if is_b else (outer, inner)
            z_from = lax.rem(zh + NZ - dz, NZ)
            x_from = lax.rem(x + NX - dx, NX)
            row = pl.multiple_of(((z_from * NX + x_from) * NC + row_core) * ROW, ROW)
            cut = pl.ds(COLS_A, COLS_B) if is_b else pl.ds(0, COLS_A)
            copies.append(
                pltpu.make_async_copy(
                    piece.at[inner], out.at[pl.ds(row, ROW), cut], sems.at[len(copies)]
                )
            )
    for copy in copies:
        copy.start()
    for copy in copies:
        copy.wait()


def placed(meta, pieces):
    return pl.pallas_call(
        place_kernel,
        in_specs=[pl.BlockSpec(memory_space=pltpu.SMEM)]
        + [pl.BlockSpec(memory_space=pl.ANY)] * len(pieces),
        out_specs=pl.BlockSpec(memory_space=pl.ANY),
        out_shape=jax.ShapeDtypeStruct((NZ * NX * NC * ROW, COLS), BF),
        scratch_shapes=[pltpu.SemaphoreType.DMA((4 * len(pieces),))],
        name="place",
    )(meta, *pieces)


def on_device(activations, out_grads, exponents, signs, master, moment, second):
    table = jnp.asarray(hadamard_table(TILE), BF)
    replica = lax.axis_index("replica")
    zh, x, core = replica // (NX * NC), lax.rem(replica // NC, NX), lax.rem(replica, NC)
    meta = jnp.stack([zh, x, core]).astype(jnp.int32)
    sign_row = signs.reshape(1, COLS)
    own_exps = lax.dynamic_slice_in_dim(exponents, replica * ROW, ROW, 0)

    args = (meta, activations, out_grads, exponents, sign_row, table)
    mine_a, theirs_a = quantized(0, COLS_A, True, *args)
    other_a = send(theirs_a, dc=1)
    mine_b, theirs_b = quantized(COLS_A, COLS_B, False, *args)
    other_b = send(theirs_b, dc=1)
    a = pair_sum(mine_a, other_a)
    a = quad_sum([a[0], send(a[1], dx=1), send(a[3], dx=3), send(a[2], dx=2)])
    b = pair_sum(mine_b, other_b)
    b = quad_sum([b[0], send(b[1], dz=1), send(b[3], dz=3), send(b[2], dz=2)])
    a = [a[0], send(a[1], dz=1), send(a[3], dz=3), send(a[2], dz=2)]
    b = [b[0], send(b[1], dx=1), send(b[3], dx=3), send(b[2], dx=2)]
    grad_mean, moment_new, second_new, master_new, wa, wb = updated(
        a, b, own_exps, sign_row, table, master, moment, second
    )
    wa = jnp.stack([wa] + [send(wa, dz=k) for k in (1, 2, 3)])
    wb = jnp.stack([wb] + [send(wb, dx=k) for k in (1, 2, 3)])
    ga = [wa] + [send(wa, dx=k) for k in (1, 2, 3)]
    gb = [wb] + [send(wb, dz=k) for k in (1, 2, 3)]
    own = ga + gb
    other = [send(piece, dc=1) for piece in own]
    weights = placed(meta, own + other)
    return (grad_mean, moment_new, second_new, master_new, weights)


def solution(mesh):
    in_specs = (
        P("replica", None),
        P("replica", "tensor"),
        P(None, "tensor"),
        P("tensor"),
        P("replica", "tensor"),
        P("replica", "tensor"),
        P("replica", "tensor"),
    )
    out_specs = (
        P("replica", "tensor"),
        P("replica", "tensor"),
        P("replica", "tensor"),
        P("replica", "tensor"),
        P(None, "tensor"),
    )
    return jax.shard_map(
        on_device, mesh=mesh, in_specs=in_specs, out_specs=out_specs, check_vma=False
    )
```

time: 215 us -> 315 us (1.47)
  Pallas kernels: 0 us -> 192 us
  waiting for transfers between devices: 170 us -> 50.7 us
  starting transfers between devices: 0.08 us -> 56.5 us
  between operations: 14.1 us -> 1.11 us
  matrix products: 11.4 us -> 0 us
  other arithmetic: 5.94 us -> 0.18 us
    pallas_call x0 -> x8, Pallas kernels: none -> 192 us  [the longest x1 161 us: placed(): pl.pallas_call(place_kernel, in_specs=[pl.BlockSpec(memory_space=pltpu.SM...]
    reduce_scatter x1 -> x0, waiting for transfers between devices: 106 us -> none  [on_device(): lax.psum_scatter(jnp.clip(rotated * shrink, -127.0, 127.0).astype(jnp.bfl...]
    all_gather x1 -> x0, waiting for transfers between devices: 63.9 us -> none  [on_device(): lax.all_gather(master_new.astype(jnp.bfloat16), 'replica', axis=0, tiled=...]
    ppermute x0 -> x34, starting transfers between devices: none -> 56.5 us  [send(): return lax.ppermute(value, 'replica', replica_perm(**shift))]
    ppermute x0 -> x34, waiting for transfers between devices: none -> 50.7 us  [send(): return lax.ppermute(value, 'replica', replica_perm(**shift))]
    dot_general x3 -> x0, matrix products: 11.4 us -> none  [the longest x1 6.1 us: on_device(): lax.dot_general(activations, out_grads, (((0,), (0,)), ((), ())), preferr...]
    unnamed x6 -> x65, local copies, waits for them, and re-layouts: 5.38 us -> 13.6 us
    convert_element_type x1 -> x0, local copies, waits for them, and re-layouts: 7.88 us -> none  [on_device(): jnp.clip(rotated * shrink, -127.0, 127.0).astype(jnp.bfloat16)]
  transfers between devices with their start and end apart: 2 -> 34, of which waited for: 2 -> 10; matrix products, arithmetic and copies ran while one was open for 1% -> 0% of each run, Pallas kernels for 0% -> 6%
where the time goes in v1:
time: 315 us; the launch traced here: 314 us
  Pallas kernels  192 us (61%)
  starting transfers between devices  56.5 us (18%)
  waiting for transfers between devices  50.7 us (16%)
  local copies, waits for them, and re-layouts  14.3 us (5%)
    pallas_call x1, Pallas kernels, placed(): pl.pallas_call(place_kernel, in_specs=[pl.BlockSpec(memory_space=pltpu.SM...  161 us
    ppermute x34, starting transfers between devices, send(): return lax.ppermute(value, 'replica', replica_perm(**shift))  56.5 us
    ppermute x34, waiting for transfers between devices, send(): return lax.ppermute(value, 'replica', replica_perm(**shift))  50.7 us
    pallas_call x2, Pallas kernels, quantized(): pl.pallas_call(functools.partial(quant_kernel, first, width), grid_spec=p...  17 us
    unnamed x65, local copies, waits for them, and re-layouts  13.6 us
    pallas_call x2, Pallas kernels, pair_sum(): pl.pallas_call(pair_kernel, grid=(4,), in_specs=[spec, spec], out_specs=[...  7.63 us
  transfers between devices with their start and end apart: 34, of which 10 were waited for; matrix products, arithmetic and copies ran while one was open for 0% of the time, Pallas kernels for 6%

profile of v1, /device:TPU:1, one launch (start us, length us, event | category | flops | bytes accessed | tf_op | source)
XLA Modules:
  0.0 314.5 jit_solution(17989183830753946729)
XLA Ops:
  2.7 1.9 copy-done
  7.0 9.5 %quantize.2 = (bf16[4,4,64,896]{3,2,1,0:T(8,128)(2,1)S(1)}, bf16[4,4,64,896]{3,2,1,0:T(8,128)(2,1)S(1)}) custom-call(s32[3]{0:T(128)S(1)} %pad_add_fusion.meta, bf16[768,2048]{1,0:T(8,128)(2,1)S(1)} %copy-done, bf16[768,1280]{1,0:T(8,128)(2,1)S(1)} %copy-done.1, s32[2048,5]{1,0:T(8,128)S(1)} %copy.13.exps, s32[1,1280]{1,0:T(1,128)S(1)} %reshape.13.signs.refs_9_, ...), custom_call_target="tpu_custom_call" | custom-call | tf_op jit(solution)/shard_map/quantize/pallas_call | solution.py:91
  17.8 3.3 %collective-permute-start = (bf16[4,4,64,896]{3,2,1,0:T(8,128)(2,1)S(1)}, bf16[4,4,64,896]{3,2,1,0:T(8,128)(2,1)S(1)}, u32[]{:S(2)}, u32[]{:S(2)}) collective-permute-start(bf16[4,4,64,896]{3,2,1,0:T(8,128)(2,1)S(1)} %get-tuple-element.32), channel_id=1, source_target_pairs={{0,8},{8,0},{16,24},{24,16},{32,40},{40,32},{48,56},{56,48},{64,72... | collective-permute-start | bytes 5505032 | tf_op jit(solution)/shard_map/ppermute | solution.py:51
  21.0 7.5 %quantize.3 = (bf16[4,4,64,384]{3,2,1,0:T(8,128)(2,1)S(1)}, bf16[4,4,64,384]{3,2,1,0:T(8,128)(2,1)S(1)}) custom-call(s32[3]{0:T(128)S(1)} %pad_add_fusion.meta, bf16[768,2048]{1,0:T(8,128)(2,1)S(1)} %copy-done, bf16[768,1280]{1,0:T(8,128)(2,1)S(1)} %copy-done.1, s32[2048,5]{1,0:T(8,128)S(1)} %copy.13.exps, s32[1,1280]{1,0:T(1,128)S(1)} %reshape.13.signs.refs_9_, ...), custom_call_target="tpu_custom_call" | custom-call | tf_op jit(solution)/shard_map/quantize/pallas_call | solution.py:91
  30.7 4.1 %pair_sum.2 = (bf16[4,64,896]{2,1,0:T(8,128)(2,1)}, bf16[4,64,896]{2,1,0:T(8,128)(2,1)}, bf16[4,64,896]{2,1,0:T(8,128)(2,1)}, bf16[4,64,896]{2,1,0:T(8,128)(2,1)}) custom-call(bf16[4,4,64,896]{3,2,1,0:T(8,128)(2,1)} %copy-done.2, bf16[4,4,64,896]{3,2,1,0:T(8,128)(2,1)} %copy-done.12), custom_call_target="tpu_custom_call" | custom-call | tf_op jit(solution)/shard_map/pair_sum/pallas_call | solution.py:120
  34.8 2.7 collective-permute-start.2
  38.4 3.6 %pair_sum.3 = (bf16[4,64,384]{2,1,0:T(8,128)(2,1)}, bf16[4,64,384]{2,1,0:T(8,128)(2,1)}, bf16[4,64,384]{2,1,0:T(8,128)(2,1)}, bf16[4,64,384]{2,1,0:T(8,128)(2,1)}) custom-call(bf16[4,4,64,384]{3,2,1,0:T(8,128)(2,1)} %copy-done.5, bf16[4,4,64,384]{3,2,1,0:T(8,128)(2,1)} %copy-done.14), custom_call_target="tpu_custom_call" | custom-call | tf_op jit(solution)/shard_map/pair_sum/pallas_call | solution.py:120
  41.9 2.8 collective-permute-start.8
  44.8 3.1 collective-permute-start.9
  47.9 4.8 %collective-permute-done.8.b = bf16[4,64,384]{2,1,0:T(8,128)(2,1)S(1)} collective-permute-done((bf16[4,64,384]{2,1,0:T(8,128)(2,1)}, bf16[4,64,384]{2,1,0:T(8,128)(2,1)S(1)}, u32[]{:S(2)}, u32[]{:S(2)}) %collective-permute-start.8) | collective-permute-done | bytes 196640 | tf_op jit(solution)/shard_map/ppermute | solution.py:51
  52.7 8.2 %collective-permute-start.10 = (bf16[4,64,384]{2,1,0:T(8,128)(2,1)}, bf16[4,64,384]{2,1,0:T(8,128)(2,1)S(1)}, u32[]{:S(2)}, u32[]{:S(2)}) collective-permute-start(bf16[4,64,384]{2,1,0:T(8,128)(2,1)} %get-tuple-element.46), channel_id=1, source_target_pairs={{0,128},{8,136},{16,144},{24,152},{32,160},{40,168},{48,176},{56,1... | collective-permute-start | bytes 589832 | tf_op jit(solution)/shard_map/ppermute | solution.py:51
  60.9 8.8 %collective-permute-done.10.d = bf16[4,64,384]{2,1,0:T(8,128)(2,1)S(1)} collective-permute-done((bf16[4,64,384]{2,1,0:T(8,128)(2,1)}, bf16[4,64,384]{2,1,0:T(8,128)(2,1)S(1)}, u32[]{:S(2)}, u32[]{:S(2)}) %collective-permute-start.10) | collective-permute-done | bytes 196640 | tf_op jit(solution)/shard_map/ppermute | solution.py:51
  70.4 1.9 quad_sum.3
  72.3 2.3 quad_sum.2
  74.7 3.6 %collective-permute-start.5 = (bf16[64,896]{1,0:T(8,128)(2,1)}, bf16[64,896]{1,0:T(8,128)(2,1)S(1)}, u32[]{:S(2)}, u32[]{:S(2)}) collective-permute-start(bf16[64,896]{1,0:T(8,128)(2,1)} %get-tuple-element.39), channel_id=1, source_target_pairs={{0,192},{8,200},{16,208},{24,216},{32,224},{40,232},{48,240},{56,2... | collective-permute-start | bytes 344072 | tf_op jit(solution)/shard_map/ppermute | solution.py:51
  78.2 3.2 %collective-permute-start.6 = (bf16[64,896]{1,0:T(8,128)(2,1)}, bf16[64,896]{1,0:T(8,128)(2,1)S(1)}, u32[]{:S(2)}, u32[]{:S(2)}) collective-permute-start(bf16[64,896]{1,0:T(8,128)(2,1)} %get-tuple-element.40), channel_id=1, source_target_pairs={{0,128},{8,136},{16,144},{24,152},{32,160},{40,168},{48,176},{56,1... | collective-permute-start | bytes 344072 | tf_op jit(solution)/shard_map/ppermute | solution.py:51
  81.4 2.7 collective-permute-start.12
  85.6 3.5 %collective-permute-done.13.refs_7_ = bf16[64,384]{1,0:T(8,128)(2,1)S(1)} collective-permute-done((bf16[64,384]{1,0:T(8,128)(2,1)}, bf16[64,384]{1,0:T(8,128)(2,1)S(1)}, u32[]{:S(2)}, u32[]{:S(2)}) %collective-permute-start.13) | collective-permute-done | bytes 49184 | tf_op jit(solution)/shard_map/ppermute | solution.py:51
  91.1 1.7 update.1
  92.8 4.1 %collective-permute-start.22 = (bf16[64,384]{1,0:T(8,128)(2,1)S(1)}, bf16[64,384]{1,0:T(8,128)(2,1)S(1)}, u32[]{:S(2)}, u32[]{:S(2)}) collective-permute-start(bf16[64,384]{1,0:T(8,128)(2,1)S(1)} %get-tuple-element.56), channel_id=1, source_target_pairs={{0,48},{8,56},{16,0},{24,8},{32,16},{40,24},{48,32},{56,40},{64,11... | collective-permute-start | bytes 147464 | tf_op jit(solution)/shard_map/ppermute | solution.py:51
  97.5 2.2 collective-permute-start.15
  99.7 2.4 collective-permute-start.14
  102.1 3.4 %collective-permute-start.30 = (bf16[4,64,384]{2,1,0:T(8,128)(2,1)S(1)}, bf16[4,64,384]{2,1,0:T(8,128)(2,1)S(1)}, u32[]{:S(2)}, u32[]{:S(2)}) collective-permute-start(bf16[4,64,384]{2,1,0:T(8,128)(2,1)S(1)} %pad_maximum_fusion.1.refs_4_), channel_id=1, source_target_pairs={{0,8},{8,0},{16,24},{24,16},{32,40},{40,32},{48,56},{56,48},{64,72... | collective-permute-start | bytes 589832 | tf_op jit(solution)/shard_map/ppermute | solution.py:51
  105.5 4.3 %collective-permute-done.14 = bf16[64,896]{1,0:T(8,128)(2,1)S(1)} collective-permute-done((bf16[64,896]{1,0:T(8,128)(2,1)S(1)}, bf16[64,896]{1,0:T(8,128)(2,1)S(1)}, u32[]{:S(2)}, u32[]{:S(2)}) %collective-permute-start.14) | collective-permute-done | bytes 114720 | tf_op jit(solution)/shard_map/ppermute | solution.py:51
  109.9 1.6 collective-permute-start.19
  111.5 6.3 %collective-permute-start.18 = (bf16[4,64,896]{2,1,0:T(8,128)(2,1)S(1)}, bf16[4,64,896]{2,1,0:T(8,128)(2,1)S(1)}, u32[]{:S(2)}, u32[]{:S(2)}) collective-permute-start(bf16[4,64,896]{2,1,0:T(8,128)(2,1)S(1)} %pad_maximum_fusion.refs_0_), channel_id=1, source_target_pairs={{0,32},{8,40},{16,48},{24,56},{32,0},{40,8},{48,16},{56,24},{64,96... | collective-permute-start | bytes 1376264 | tf_op jit(solution)/shard_map/ppermute | solution.py:51
  119.0 18.2 %collective-permute-done.25.refs_7_ = bf16[4,64,384]{2,1,0:T(8,128)(2,1)S(1)} collective-permute-done((bf16[4,64,384]{2,1,0:T(8,128)(2,1)S(1)}, bf16[4,64,384]{2,1,0:T(8,128)(2,1)S(1)}, u32[]{:S(2)}, u32[]{:S(2)}) %collective-permute-start.25) | collective-permute-done | bytes 196640 | tf_op jit(solution)/shard_map/ppermute | solution.py:51
  137.2 1.6 collective-permute-start.33
  138.7 5.4 %collective-permute-done.23.refs_5_ = bf16[4,64,384]{2,1,0:T(8,128)(2,1)S(1)} collective-permute-done((bf16[4,64,384]{2,1,0:T(8,128)(2,1)S(1)}, bf16[4,64,384]{2,1,0:T(8,128)(2,1)S(1)}, u32[]{:S(2)}, u32[]{:S(2)}) %collective-permute-start.23) | collective-permute-done | bytes 196640 | tf_op jit(solution)/shard_map/ppermute | solution.py:51
  144.2 2.4 collective-permute-start.26
  147.6 2.6 collective-permute-done.32.refs_14_
  153.2 161.2 %place.1 = bf16[2048,1280]{1,0:T(8,128)(2,1)} custom-call(s32[3]{0:T(128)} %copy-done.11, bf16[4,64,896]{2,1,0:T(8,128)(2,1)} %copy-done.13, bf16[4,64,896]{2,1,0:T(8,128)(2,1)} %copy-done.18, bf16[4,64,896]{2,1,0:T(8,128)(2,1)} %copy-done.17, bf16[4,64,896]{2,1,0:T(8,128)(2,1)} %copy-done.16, bf16[4,64,384]{2,1,0:T(8,128)(2,1)} %copy-done.15, ...), custom_call_target="tpu_custom_call" | custom-call | tf_op jit(solution)/shard_map/place/pallas_call | solution.py:237
  (114 shorter events, 18.7 us)
Async XLA Ops:
  17.8 11.7 %collective-permute-start = (bf16[4,4,64,896]{3,2,1,0:T(8,128)(2,1)S(1)}, bf16[4,4,64,896]{3,2,1,0:T(8,128)(2,1)S(1)}, u32[]{:S(2)}, u32[]{:S(2)}) collective-permute-start(bf16[4,4,64,896]{3,2,1,0:T(8,128)(2,1)S(1)} %get-tuple-element.32), channel_id=1, source_target_pairs={{0,8},{8,0},{16,24},{24,16},{32,40},{40,32},{48,56},{56,48},{64,72... | collective-permute-start | bytes 5505032 | tf_op jit(solution)/shard_map/ppermute | solution.py:51
  29.4 8.0 %collective-permute-start.7 = (bf16[4,4,64,384]{3,2,1,0:T(8,128)(2,1)S(1)}, bf16[4,4,64,384]{3,2,1,0:T(8,128)(2,1)S(1)}, u32[]{:S(2)}, u32[]{:S(2)}) collective-permute-start(bf16[4,4,64,384]{3,2,1,0:T(8,128)(2,1)S(1)} %get-tuple-element.42), channel_id=1, source_target_pairs={{0,8},{8,0},{16,24},{24,16},{32,40},{40,32},{48,56},{56,48},{64,72... | collective-permute-start | bytes 2359304 | tf_op jit(solution)/shard_map/ppermute | solution.py:51
  34.8 37.5 %collective-permute-start.1 = (bf16[4,64,896]{2,1,0:T(8,128)(2,1)}, bf16[4,64,896]{2,1,0:T(8,128)(2,1)}, u32[]{:S(2)}, u32[]{:S(2)}) collective-permute-start(bf16[4,64,896]{2,1,0:T(8,128)(2,1)} %get-tuple-element.34), channel_id=1, source_target_pairs={{0,16},{8,24},{16,32},{24,40},{32,48},{40,56},{48,0},{56,8},{64,80... | collective-permute-start | bytes 1376264 | tf_op jit(solution)/shard_map/ppermute | solution.py:51
  34.8 37.5 %collective-permute-start.2 = (bf16[4,64,896]{2,1,0:T(8,128)(2,1)}, bf16[4,64,896]{2,1,0:T(8,128)(2,1)}, u32[]{:S(2)}, u32[]{:S(2)}) collective-permute-start(bf16[4,64,896]{2,1,0:T(8,128)(2,1)} %get-tuple-element.35), channel_id=1, source_target_pairs={{0,48},{8,56},{16,0},{24,8},{32,16},{40,24},{48,32},{56,40},{64,11... | collective-permute-start | bytes 1376264 | tf_op jit(solution)/shard_map/ppermute | solution.py:51
  37.5 34.9 %collective-permute-start.3 = (bf16[4,64,896]{2,1,0:T(8,128)(2,1)}, bf16[4,64,896]{2,1,0:T(8,128)(2,1)}, u32[]{:S(2)}, u32[]{:S(2)}) collective-permute-start(bf16[4,64,896]{2,1,0:T(8,128)(2,1)} %get-tuple-element.36), channel_id=1, source_target_pairs={{0,32},{8,40},{16,48},{24,56},{32,0},{40,8},{48,16},{56,24},{64,96... | collective-permute-start | bytes 1376264 | tf_op jit(solution)/shard_map/ppermute | solution.py:51
  41.9 10.7 %collective-permute-start.8 = (bf16[4,64,384]{2,1,0:T(8,128)(2,1)}, bf16[4,64,384]{2,1,0:T(8,128)(2,1)S(1)}, u32[]{:S(2)}, u32[]{:S(2)}) collective-permute-start(bf16[4,64,384]{2,1,0:T(8,128)(2,1)} %get-tuple-element.44), channel_id=1, source_target_pairs={{0,64},{8,72},{16,80},{24,88},{32,96},{40,104},{48,112},{56,120},{... | collective-permute-start | bytes 589832 | tf_op jit(solution)/shard_map/ppermute | solution.py:51
  44.8 16.1 %collective-permute-start.9 = (bf16[4,64,384]{2,1,0:T(8,128)(2,1)}, bf16[4,64,384]{2,1,0:T(8,128)(2,1)S(1)}, u32[]{:S(2)}, u32[]{:S(2)}) collective-permute-start(bf16[4,64,384]{2,1,0:T(8,128)(2,1)} %get-tuple-element.45), channel_id=1, source_target_pairs={{0,192},{8,200},{16,208},{24,216},{32,224},{40,232},{48,240},{56,2... | collective-permute-start | bytes 589832 | tf_op jit(solution)/shard_map/ppermute | solution.py:51
  52.7 17.0 %collective-permute-start.10 = (bf16[4,64,384]{2,1,0:T(8,128)(2,1)}, bf16[4,64,384]{2,1,0:T(8,128)(2,1)S(1)}, u32[]{:S(2)}, u32[]{:S(2)}) collective-permute-start(bf16[4,64,384]{2,1,0:T(8,128)(2,1)} %get-tuple-element.46), channel_id=1, source_target_pairs={{0,128},{8,136},{16,144},{24,152},{32,160},{40,168},{48,176},{56,1... | collective-permute-start | bytes 589832 | tf_op jit(solution)/shard_map/ppermute | solution.py:51
  72.3 11.8 %collective-permute-start.11 = (bf16[64,384]{1,0:T(8,128)(2,1)}, bf16[64,384]{1,0:T(8,128)(2,1)S(1)}, u32[]{:S(2)}, u32[]{:S(2)}) collective-permute-start(bf16[64,384]{1,0:T(8,128)(2,1)} %get-tuple-element.48), channel_id=1, source_target_pairs={{0,16},{8,24},{16,32},{24,40},{32,48},{40,56},{48,0},{56,8},{64,80... | collective-permute-start | bytes 147464 | tf_op jit(solution)/shard_map/ppermute | solution.py:51
  74.7 14.4 %collective-permute-start.4 = (bf16[64,896]{1,0:T(8,128)(2,1)}, bf16[64,896]{1,0:T(8,128)(2,1)S(1)}, u32[]{:S(2)}, u32[]{:S(2)}) collective-permute-start(bf16[64,896]{1,0:T(8,128)(2,1)} %get-tuple-element.38), channel_id=1, source_target_pairs={{0,64},{8,72},{16,80},{24,88},{32,96},{40,104},{48,112},{56,120},{... | collective-permute-start | bytes 344072 | tf_op jit(solution)/shard_map/ppermute | solution.py:51
  74.7 14.4 %collective-permute-start.5 = (bf16[64,896]{1,0:T(8,128)(2,1)}, bf16[64,896]{1,0:T(8,128)(2,1)S(1)}, u32[]{:S(2)}, u32[]{:S(2)}) collective-permute-start(bf16[64,896]{1,0:T(8,128)(2,1)} %get-tuple-element.39), channel_id=1, source_target_pairs={{0,192},{8,200},{16,208},{24,216},{32,224},{40,232},{48,240},{56,2... | collective-permute-start | bytes 344072 | tf_op jit(solution)/shard_map/ppermute | solution.py:51
  78.2 11.2 %collective-permute-start.6 = (bf16[64,896]{1,0:T(8,128)(2,1)}, bf16[64,896]{1,0:T(8,128)(2,1)S(1)}, u32[]{:S(2)}, u32[]{:S(2)}) collective-permute-start(bf16[64,896]{1,0:T(8,128)(2,1)} %get-tuple-element.40), channel_id=1, source_target_pairs={{0,128},{8,136},{16,144},{24,152},{32,160},{40,168},{48,176},{56,1... | collective-permute-start | bytes 344072 | tf_op jit(solution)/shard_map/ppermute | solution.py:51
  81.4 4.2 %collective-permute-start.12 = (bf16[64,384]{1,0:T(8,128)(2,1)}, bf16[64,384]{1,0:T(8,128)(2,1)S(1)}, u32[]{:S(2)}, u32[]{:S(2)}) collective-permute-start(bf16[64,384]{1,0:T(8,128)(2,1)} %get-tuple-element.49), channel_id=1, source_target_pairs={{0,48},{8,56},{16,0},{24,8},{32,16},{40,24},{48,32},{56,40},{64,11... | collective-permute-start | bytes 147464 | tf_op jit(solution)/shard_map/ppermute | solution.py:51
  84.1 5.0 %collective-permute-start.13 = (bf16[64,384]{1,0:T(8,128)(2,1)}, bf16[64,384]{1,0:T(8,128)(2,1)S(1)}, u32[]{:S(2)}, u32[]{:S(2)}) collective-permute-start(bf16[64,384]{1,0:T(8,128)(2,1)} %get-tuple-element.50), channel_id=1, source_target_pairs={{0,32},{8,40},{16,48},{24,56},{32,0},{40,8},{48,16},{56,24},{64,96... | collective-permute-start | bytes 147464 | tf_op jit(solution)/shard_map/ppermute | solution.py:51
  92.8 6.9 %collective-permute-start.22 = (bf16[64,384]{1,0:T(8,128)(2,1)S(1)}, bf16[64,384]{1,0:T(8,128)(2,1)S(1)}, u32[]{:S(2)}, u32[]{:S(2)}) collective-permute-start(bf16[64,384]{1,0:T(8,128)(2,1)S(1)} %get-tuple-element.56), channel_id=1, source_target_pairs={{0,48},{8,56},{16,0},{24,8},{32,16},{40,24},{48,32},{56,40},{64,11... | collective-permute-start | bytes 147464 | tf_op jit(solution)/shard_map/ppermute | solution.py:51
  96.9 5.2 %collective-permute-start.21 = (bf16[64,384]{1,0:T(8,128)(2,1)S(1)}, bf16[64,384]{1,0:T(8,128)(2,1)S(1)}, u32[]{:S(2)}, u32[]{:S(2)}) collective-permute-start(bf16[64,384]{1,0:T(8,128)(2,1)S(1)} %get-tuple-element.56), channel_id=1, source_target_pairs={{0,32},{8,40},{16,48},{24,56},{32,0},{40,8},{48,16},{56,24},{64,96... | collective-permute-start | bytes 147464 | tf_op jit(solution)/shard_map/ppermute | solution.py:51
  96.9 5.2 %collective-permute-start.20 = (bf16[64,384]{1,0:T(8,128)(2,1)S(1)}, bf16[64,384]{1,0:T(8,128)(2,1)S(1)}, u32[]{:S(2)}, u32[]{:S(2)}) collective-permute-start(bf16[64,384]{1,0:T(8,128)(2,1)S(1)} %get-tuple-element.56), channel_id=1, source_target_pairs={{0,16},{8,24},{16,32},{24,40},{32,48},{40,56},{48,0},{56,8},{64,80... | collective-permute-start | bytes 147464 | tf_op jit(solution)/shard_map/ppermute | solution.py:51
  97.5 8.0 %collective-permute-start.16 = (bf16[64,896]{1,0:T(8,128)(2,1)S(1)}, bf16[64,896]{1,0:T(8,128)(2,1)S(1)}, u32[]{:S(2)}, u32[]{:S(2)}) collective-permute-start(bf16[64,896]{1,0:T(8,128)(2,1)S(1)} %get-tuple-element.55), channel_id=1, source_target_pairs={{0,192},{8,200},{16,208},{24,216},{32,224},{40,232},{48,240},{56,2... | collective-permute-start | bytes 344072 | tf_op jit(solution)/shard_map/ppermute | solution.py:51
  97.5 8.0 %collective-permute-start.15 = (bf16[64,896]{1,0:T(8,128)(2,1)S(1)}, bf16[64,896]{1,0:T(8,128)(2,1)S(1)}, u32[]{:S(2)}, u32[]{:S(2)}) collective-permute-start(bf16[64,896]{1,0:T(8,128)(2,1)S(1)} %get-tuple-element.55), channel_id=1, source_target_pairs={{0,128},{8,136},{16,144},{24,152},{32,160},{40,168},{48,176},{56,1... | collective-permute-start | bytes 344072 | tf_op jit(solution)/shard_map/ppermute | solution.py:51
  99.7 10.1 %collective-permute-start.14 = (bf16[64,896]{1,0:T(8,128)(2,1)S(1)}, bf16[64,896]{1,0:T(8,128)(2,1)S(1)}, u32[]{:S(2)}, u32[]{:S(2)}) collective-permute-start(bf16[64,896]{1,0:T(8,128)(2,1)S(1)} %get-tuple-element.55), channel_id=1, source_target_pairs={{0,64},{8,72},{16,80},{24,88},{32,96},{40,104},{48,112},{56,120},{... | collective-permute-start | bytes 344072 | tf_op jit(solution)/shard_map/ppermute | solution.py:51
  102.1 15.6 %collective-permute-start.30 = (bf16[4,64,384]{2,1,0:T(8,128)(2,1)S(1)}, bf16[4,64,384]{2,1,0:T(8,128)(2,1)S(1)}, u32[]{:S(2)}, u32[]{:S(2)}) collective-permute-start(bf16[4,64,384]{2,1,0:T(8,128)(2,1)S(1)} %pad_maximum_fusion.1.refs_4_), channel_id=1, source_target_pairs={{0,8},{8,0},{16,24},{24,16},{32,40},{40,32},{48,56},{56,48},{64,72... | collective-permute-start | bytes 589832 | tf_op jit(solution)/shard_map/ppermute | solution.py:51
  109.9 36.6 %collective-permute-start.19 = (bf16[4,64,896]{2,1,0:T(8,128)(2,1)S(1)}, bf16[4,64,896]{2,1,0:T(8,128)(2,1)S(1)}, u32[]{:S(2)}, u32[]{:S(2)}) collective-permute-start(bf16[4,64,896]{2,1,0:T(8,128)(2,1)S(1)} %pad_maximum_fusion.refs_0_), channel_id=1, source_target_pairs={{0,48},{8,56},{16,0},{24,8},{32,16},{40,24},{48,32},{56,40},{64,11... | collective-permute-start | bytes 1376264 | tf_op jit(solution)/shard_map/ppermute | solution.py:51
  111.5 35.2 %collective-permute-start.18 = (bf16[4,64,896]{2,1,0:T(8,128)(2,1)S(1)}, bf16[4,64,896]{2,1,0:T(8,128)(2,1)S(1)}, u32[]{:S(2)}, u32[]{:S(2)}) collective-permute-start(bf16[4,64,896]{2,1,0:T(8,128)(2,1)S(1)} %pad_maximum_fusion.refs_0_), channel_id=1, source_target_pairs={{0,32},{8,40},{16,48},{24,56},{32,0},{40,8},{48,16},{56,24},{64,96... | collective-permute-start | bytes 1376264 | tf_op jit(solution)/shard_map/ppermute | solution.py:51
  117.8 29.3 %collective-permute-start.17 = (bf16[4,64,896]{2,1,0:T(8,128)(2,1)S(1)}, bf16[4,64,896]{2,1,0:T(8,128)(2,1)S(1)}, u32[]{:S(2)}, u32[]{:S(2)}) collective-permute-start(bf16[4,64,896]{2,1,0:T(8,128)(2,1)S(1)} %pad_maximum_fusion.refs_0_), channel_id=1, source_target_pairs={{0,16},{8,24},{16,32},{24,40},{32,48},{40,56},{48,0},{56,8},{64,80... | collective-permute-start | bytes 1376264 | tf_op jit(solution)/shard_map/ppermute | solution.py:51
  117.8 19.4 %collective-permute-start.25 = (bf16[4,64,384]{2,1,0:T(8,128)(2,1)S(1)}, bf16[4,64,384]{2,1,0:T(8,128)(2,1)S(1)}, u32[]{:S(2)}, u32[]{:S(2)}) collective-permute-start(bf16[4,64,384]{2,1,0:T(8,128)(2,1)S(1)} %pad_maximum_fusion.1.refs_4_), channel_id=1, source_target_pairs={{0,192},{8,200},{16,208},{24,216},{32,224},{40,232},{48,240},{56,2... | collective-permute-start | bytes 589832 | tf_op jit(solution)/shard_map/ppermute | solution.py:51
  117.8 19.3 %collective-permute-start.24 = (bf16[4,64,384]{2,1,0:T(8,128)(2,1)S(1)}, bf16[4,64,384]{2,1,0:T(8,128)(2,1)S(1)}, u32[]{:S(2)}, u32[]{:S(2)}) collective-permute-start(bf16[4,64,384]{2,1,0:T(8,128)(2,1)S(1)} %pad_maximum_fusion.1.refs_4_), channel_id=1, source_target_pairs={{0,128},{8,136},{16,144},{24,152},{32,160},{40,168},{48,176},{56,1... | collective-permute-start | bytes 589832 | tf_op jit(solution)/shard_map/ppermute | solution.py:51
  137.1 7.0 %collective-permute-start.23 = (bf16[4,64,384]{2,1,0:T(8,128)(2,1)S(1)}, bf16[4,64,384]{2,1,0:T(8,128)(2,1)S(1)}, u32[]{:S(2)}, u32[]{:S(2)}) collective-permute-start(bf16[4,64,384]{2,1,0:T(8,128)(2,1)S(1)} %pad_maximum_fusion.1.refs_4_), channel_id=1, source_target_pairs={{0,64},{8,72},{16,80},{24,88},{32,96},{40,104},{48,112},{56,120},{... | collective-permute-start | bytes 589832 | tf_op jit(solution)/shard_map/ppermute | solution.py:51
  137.2 10.0 %collective-permute-start.33 = (bf16[4,64,384]{2,1,0:T(8,128)(2,1)S(1)}, bf16[4,64,384]{2,1,0:T(8,128)(2,1)S(1)}, u32[]{:S(2)}, u32[]{:S(2)}) collective-permute-start(bf16[4,64,384]{2,1,0:T(8,128)(2,1)S(1)} %collective-permute-done.25.refs_7_), channel_id=1, source_target_pairs={{0,8},{8,0},{16,24},{24,16},{32,40},{40,32},{48,56},{56,48},{64,72... | collective-permute-start | bytes 589832 | tf_op jit(solution)/shard_map/ppermute | solution.py:51
  144.2 7.6 %collective-permute-start.26 = (bf16[4,64,896]{2,1,0:T(8,128)(2,1)S(1)}, bf16[4,64,896]{2,1,0:T(8,128)(2,1)S(1)}, u32[]{:S(2)}, u32[]{:S(2)}) collective-permute-start(bf16[4,64,896]{2,1,0:T(8,128)(2,1)S(1)} %pad_maximum_fusion.refs_0_), channel_id=1, source_target_pairs={{0,8},{8,0},{16,24},{24,16},{32,40},{40,32},{48,56},{56,48},{64,72... | collective-permute-start | bytes 1376264 | tf_op jit(solution)/shard_map/ppermute | solution.py:51
  146.6 5.1 %collective-permute-start.29 = (bf16[4,64,896]{2,1,0:T(8,128)(2,1)S(1)}, bf16[4,64,896]{2,1,0:T(8,128)(2,1)S(1)}, u32[]{:S(2)}, u32[]{:S(2)}) collective-permute-start(bf16[4,64,896]{2,1,0:T(8,128)(2,1)S(1)} %collective-permute-done.19.refs_3_), channel_id=1, source_target_pairs={{0,8},{8,0},{16,24},{24,16},{32,40},{40,32},{48,56},{56,48},{64,72... | collective-permute-start | bytes 1376264 | tf_op jit(solution)/shard_map/ppermute | solution.py:51
  146.7 5.1 %collective-permute-start.28 = (bf16[4,64,896]{2,1,0:T(8,128)(2,1)S(1)}, bf16[4,64,896]{2,1,0:T(8,128)(2,1)S(1)}, u32[]{:S(2)}, u32[]{:S(2)}) collective-permute-start(bf16[4,64,896]{2,1,0:T(8,128)(2,1)S(1)} %collective-permute-done.18.refs_2_), channel_id=1, source_target_pairs={{0,8},{8,0},{16,24},{24,16},{32,40},{40,32},{48,56},{56,48},{64,72... | collective-permute-start | bytes 1376264 | tf_op jit(solution)/shard_map/ppermute | solution.py:51
  147.1 5.3 %collective-permute-start.27 = (bf16[4,64,896]{2,1,0:T(8,128)(2,1)S(1)}, bf16[4,64,896]{2,1,0:T(8,128)(2,1)}, u32[]{:S(2)}, u32[]{:S(2)}) collective-permute-start(bf16[4,64,896]{2,1,0:T(8,128)(2,1)S(1)} %collective-permute-done.17.refs_1_), channel_id=1, source_target_pairs={{0,8},{8,0},{16,24},{24,16},{32,40},{40,32},{48,56},{56,48},{64,72... | collective-permute-start | bytes 1376264 | tf_op jit(solution)/shard_map/ppermute | solution.py:51
  (34 other events, 449.5 us)

commit v2 on v0

v2 whole, which is shorter than its diff:
```python
import functools
import math

import jax
import jax.numpy as jnp
import numpy as np
from jax import lax
from jax.experimental import pallas as pl
from jax.experimental.pallas import tpu as pltpu
from jax.sharding import PartitionSpec as P

TILE = 256
NZ, NX, NC = 4, 4, 2
REPLICAS = NZ * NX * NC
ROW = 64
GROUP = NC * ROW
ROWS = NZ * NX * GROUP
COLS = 1280
TILES = COLS // TILE
TOK = 768

beta_one = 0.9
beta_two = 0.95
epsilon = 1e-08
decay_rate = 0.1
learn_rate = 0.001
step_number = 100.0

F32 = jnp.float32
BF = jnp.bfloat16
MIB = 1024 * 1024
HBM = pl.BlockSpec(memory_space=pltpu.HBM)
FULL = pl.BlockSpec(memory_space=pltpu.VMEM)

SIDES = ((1, 1), (3, 1), (1, 2), (3, 2), (1, 3), (3, 3))
CORNERS = ((2, 1), (2, 3), (2, 2))
REST = ((0, 1), (0, 2), (0, 3), (1, 0), (2, 0), (3, 0), (0, 0))


def hadamard_table(order):
    positions = np.arange(order)
    intersection = positions[:, None] & positions[None, :]
    parity = np.zeros((order, order))
    for level in range(order.bit_length()):
        parity = parity + intersection // 2**level % 2
    return np.where(parity % 2 == 0, 1.0, -1.0) / math.sqrt(order)


def replica_perm(dx, dz, dc):
    pairs = []
    for z in range(NZ):
        for x in range(NX):
            for c in range(NC):
                to = (((z + dz) % NZ) * NX + (x + dx) % NX) * NC + (c + dc) % NC
                pairs.append(((z * NX + x) * NC + c, to))
    return pairs


def send(value, dx=0, dz=0, dc=0):
    return lax.ppermute(value, "replica", replica_perm(dx, dz, dc))


def place_of():
    replica = lax.axis_index("replica")
    return replica // (NX * NC), lax.rem(replica // NC, NX), lax.rem(replica, NC)


def vmem(*shape, dtype=BF):
    return pltpu.VMEM(shape, dtype)


def held(*arrays):
    return [pltpu.with_memory_space_constraint(a, pltpu.VMEM) for a in arrays]


def far(*arrays):
    return [pltpu.with_memory_space_constraint(a, pltpu.HBM) for a in arrays]


TINY = pl.CostEstimate(flops=1, bytes_accessed=1, transcendentals=0)


def params(mib):
    return pltpu.CompilerParams(vmem_limit_bytes=mib * MIB)


def quant_group(dx, dz, act, rotated, exps, mine, theirs, k):
    zh, x, core = place_of()
    group = lax.rem(zh + dz, NZ) * NX + lax.rem(x + dx, NX)
    lanes = pl.ds(pl.multiple_of(group * GROUP, GROUP), GROUP)
    total = lax.dot_general(
        act[:, lanes], rotated[...], (((0,), (0,)), ((), ())), preferred_element_type=F32
    )
    shrink = jnp.exp2(-exps[:, lanes].astype(F32)).T
    for tile in range(TILES):
        cut = slice(tile * TILE, (tile + 1) * TILE)
        part = jnp.clip(total[:, cut] * shrink[:, tile : tile + 1], -127.0, 127.0).astype(BF)
        top, bottom = part[:ROW], part[ROW:]
        mine[k, :, cut] = jnp.where(core == 0, top, bottom)
        theirs[k, :, cut] = jnp.where(core == 0, bottom, top)


def first_kernel(
    act_far, grads_far, exps_far, signs_far, table_far,
    mine, theirs, act, rotated, exps, signs, table,
    grads, line, sems,
):
    zh, _, _ = place_of()
    small = [
        pltpu.make_async_copy(signs_far, line, sems.at[0]),
        pltpu.make_async_copy(table_far, table, sems.at[1]),
        pltpu.make_async_copy(exps_far, exps, sems.at[2]),
    ]
    tiles = []
    for tile in range(TILES):
        cut = pl.ds(tile * TILE, TILE)
        tiles.append(
            pltpu.make_async_copy(grads_far.at[:, cut], grads.at[:, cut], sems.at[3 + tile])
        )
    quarters = []
    for dz in (1, 2, 3, 0):
        lanes = pl.ds(pl.multiple_of(lax.rem(zh + dz, NZ) * (ROWS // NZ), ROWS // NZ), ROWS // NZ)
        quarters.append(
            pltpu.make_async_copy(
                act_far.at[:, lanes], act.at[:, lanes], sems.at[3 + TILES + len(quarters)]
            )
        )
    for copy in small + tiles:
        copy.start()
    for copy in small:
        copy.wait()
    signs[...] = line[...].reshape(1, COLS)
    for tile in range(TILES):
        cut = slice(tile * TILE, (tile + 1) * TILE)
        tiles[tile].wait()
        if tile < len(quarters):
            quarters[tile].start()
        flipped = grads[:, cut] * signs[:, cut].astype(BF)
        rotated[:, cut] = jnp.dot(flipped, table[...], preferred_element_type=F32).astype(BF)
    for k, (dx, dz) in enumerate(SIDES):
        if k % 2 == 0:
            quarters[k // 2].wait()
        quant_group(dx, dz, act, rotated, exps, mine, theirs, k)
    quarters[3].wait()


def quantized_first(act, grads, exps, signs, table):
    n = len(SIDES)
    return pl.pallas_call(
        first_kernel,
        in_specs=[HBM] * 5,
        out_specs=[FULL] * 7,
        out_shape=[
            vmem(n, ROW, COLS),
            vmem(n, ROW, COLS),
            vmem(TOK, ROWS),
            vmem(TOK, COLS),
            vmem(TILES, ROWS, dtype=jnp.int32),
            vmem(1, COLS, dtype=jnp.int32),
            vmem(TILE, TILE),
        ],
        scratch_shapes=[
            pltpu.VMEM((TOK, COLS), BF),
            pltpu.VMEM((COLS,), jnp.int32),
            pltpu.SemaphoreType.DMA((7 + TILES,)),
        ],
        compiler_params=params(12),
        cost_estimate=TINY,
        name="quantize_sides",
    )(*far(act, grads, exps, signs, table))


def next_kernel(blocks, act, rotated, exps, _, mine, theirs):
    for k, (dx, dz) in enumerate(blocks):
        quant_group(dx, dz, act, rotated, exps, mine, theirs, k)


def quantized_next(blocks, act, rotated, exps, after):
    n = len(blocks)
    return pl.pallas_call(
        functools.partial(next_kernel, blocks),
        in_specs=[FULL] * 4,
        out_specs=[FULL] * 2,
        out_shape=[vmem(n, ROW, COLS)] * 2,
        compiler_params=params(8),
        cost_estimate=TINY,
        name="quantize_more",
    )(*held(act, rotated, exps, after))


def add(*parts):
    total = parts[0].astype(F32)
    for part in parts[1:]:
        total = total + part.astype(F32)
    return total.astype(BF)


def sides_kernel(mine, other, _b, _c, right, left):
    for k, (dx, dz) in enumerate(SIDES):
        out = right if dx == 1 else left
        out[dz - 1] = add(mine[k], other[k])


def sides_sum(mine, other, *after):
    return pl.pallas_call(
        sides_kernel,
        in_specs=[FULL] * 4,
        out_specs=[FULL] * 2,
        out_shape=[vmem(NZ - 1, ROW, COLS)] * 2,
        compiler_params=params(4),
        cost_estimate=TINY,
        name="sides_sum",
    )(*held(mine, other, *after))


def corners_kernel(mine, other, mine_rest, other_rest, *outs):
    for k, out in enumerate(outs[:3]):
        out[...] = add(mine[k], other[k])
    for k in range(len(REST)):
        outs[3][k] = add(mine_rest[k], other_rest[k])


def corners_sum(*parts):
    return pl.pallas_call(
        corners_kernel,
        in_specs=[FULL] * 4,
        out_specs=[FULL] * 4,
        out_shape=[vmem(ROW, COLS)] * 3 + [vmem(len(REST), ROW, COLS)],
        compiler_params=params(4),
        cost_estimate=TINY,
        name="corners_sum",
    )(*held(*parts))


def middle_kernel(pairs, left, right, below, above, across, *outs):
    z1, z2, z3, x1, x2, x3, own = outs
    for k, out in enumerate((z1, z2, z3)):
        more = (across[...],) if k == 1 else ()
        out[...] = add(pairs[k], left[k], right[k], *more)
    x1[...] = pairs[3]
    x2[...] = add(pairs[4], below[...], above[...])
    x3[...] = pairs[5]
    own[...] = pairs[6]


def middle_sum(*parts):
    return pl.pallas_call(
        middle_kernel,
        in_specs=[FULL] * 6,
        out_specs=[FULL] * 7,
        out_shape=[vmem(ROW, COLS)] * 7,
        compiler_params=params(4),
        cost_estimate=TINY,
        name="middle_sum",
    )(*held(*parts))


def update_kernel(*refs):
    parts = refs[0:7]
    exps, signs, table, master, moment, second = refs[7:13]
    grad_out, moment_out, second_out, master_out, weights_out = refs[13:18]
    zh, x, core = place_of()
    lanes = pl.ds(pl.multiple_of((zh * NX + x) * GROUP, GROUP), GROUP)
    growth = jnp.exp2(exps[:, lanes].astype(F32)).T
    growth = jnp.where(core == 0, growth[:ROW], growth[ROW:])
    first_fix = 1.0 - beta_one**step_number
    second_fix = 1.0 - beta_two**step_number
    for tile in range(TILES):
        cut = slice(tile * TILE, (tile + 1) * TILE)
        total = parts[0][:, cut].astype(F32)
        for part in parts[1:]:
            total = total + part[:, cut].astype(F32)
        decoded = total * growth[:, tile : tile + 1]
        high = decoded.astype(BF)
        rest = decoded - high.astype(F32)
        middle = rest.astype(BF)
        low = (rest - middle.astype(F32)).astype(BF)
        restored = jnp.dot(high, table[...], preferred_element_type=F32) + (
            jnp.dot(middle, table[...], preferred_element_type=F32)
            + jnp.dot(low, table[...], preferred_element_type=F32)
        )
        grad = restored * (signs[:, cut].astype(F32) * (1.0 / REPLICAS))
        moment_new = beta_one * moment[:, cut] + (1.0 - beta_one) * grad
        second_new = beta_two * second[:, cut] + (1.0 - beta_two) * grad * grad
        update = (
            moment_new / first_fix / (jnp.sqrt(second_new / second_fix) + epsilon)
            + decay_rate * master[:, cut]
        )
        master_new = master[:, cut] - learn_rate * update
        weights_out[:, cut] = master_new.astype(BF)
        grad_out[:, cut] = grad
        moment_out[:, cut] = moment_new
        second_out[:, cut] = second_new
        master_out[:, cut] = master_new


def updated(parts, exps, signs, table, state):
    return pl.pallas_call(
        update_kernel,
        in_specs=[FULL] * 13,
        out_specs=[FULL] * 5,
        out_shape=[vmem(ROW, COLS, dtype=F32)] * 4 + [vmem(ROW, COLS)],
        compiler_params=params(4),
        cost_estimate=TINY,
        name="update",
    )(*held(*parts, exps, signs, table, *state))


def join_kernel(count, *refs):
    out = refs[-1]
    row = 0
    for part in refs[:count]:
        if len(part.shape) == 3:
            out[row : row + part.shape[0]] = part[...]
            row += part.shape[0]
        else:
            out[row] = part[...]
            row += 1


def joined(*parts, after=()):
    blocks = sum(part.shape[0] if part.ndim == 3 else 1 for part in parts)
    return pl.pallas_call(
        functools.partial(join_kernel, len(parts)),
        in_specs=[FULL] * (len(parts) + len(after)),
        out_specs=FULL,
        out_shape=vmem(blocks, ROW, COLS),
        compiler_params=params(2),
        cost_estimate=TINY,
        name="join",
    )(*held(*parts, *after))


def fan_kernel(w, x3, x1, x2, z2, z3, z1, column, row, corner, first):
    for k, part in enumerate((z1, z3, z2)):
        column[k] = part[...]
    row[...] = x2[...]
    corner[...] = z2[...]
    for k, part in enumerate((w, z1, z3, z2, x2, x1, x3)):
        first[k] = part[...]


def fanned(*parts):
    return pl.pallas_call(
        fan_kernel,
        in_specs=[FULL] * 7,
        out_specs=[FULL] * 4,
        out_shape=[vmem(3, ROW, COLS), vmem(ROW, COLS), vmem(ROW, COLS), vmem(7, ROW, COLS)],
        compiler_params=params(2),
        cost_estimate=TINY,
        name="fan",
    )(*held(*parts))


def place_kernel(names, count, chained, *refs):
    pieces = refs[:2]
    state = refs[2 : 2 + count]
    out = refs[2 + count + chained]
    state_out = refs[3 + count + chained : 3 + 2 * count + chained]
    token, sems = refs[-2:]
    token[...] = jnp.zeros_like(token)
    zh, x, core = place_of()
    copies = []
    for flip, piece in enumerate(pieces):
        row_core = 1 - core if flip else core
        for k, (dx, dz) in enumerate(names):
            z_from = lax.rem(zh + NZ - dz, NZ)
            x_from = lax.rem(x + NX - dx, NX)
            row = pl.multiple_of(((z_from * NX + x_from) * NC + row_core) * ROW, ROW)
            copies.append(
                pltpu.make_async_copy(
                    piece.at[k], out.at[pl.ds(row, ROW), :], sems.at[len(copies)]
                )
            )
    for near, away in zip(state, state_out):
        copies.append(pltpu.make_async_copy(near, away, sems.at[len(copies)]))
    for copy in copies:
        copy.start()
    for copy in copies:
        copy.wait()


def placed(names, mine, other, state, previous):
    count = len(state)
    chained = previous is not None
    full = jax.ShapeDtypeStruct((ROW, COLS), F32)
    return pl.pallas_call(
        functools.partial(place_kernel, names, count, chained),
        in_specs=[FULL] * (2 + count) + [HBM] * chained,
        out_specs=[HBM] * (1 + count) + [FULL],
        out_shape=[jax.ShapeDtypeStruct((ROWS, COLS), BF)] + [full] * count + [vmem(16, 128)],
        input_output_aliases={2 + count: 0} if chained else {},
        scratch_shapes=[pltpu.SemaphoreType.DMA((2 * len(names) + count,))],
        compiler_params=params(2),
        cost_estimate=TINY,
        name="place",
    )(*held(mine, other, *state), *((previous,) if chained else ()))


def on_device(activations, out_grads, exponents, signs, master, moment, second):
    table = jnp.asarray(hadamard_table(TILE), BF)
    mine_a, theirs_a, act, rotated, exps, sign_row, table = quantized_first(
        activations, out_grads, exponents.T, signs, table
    )
    other_a = send(theirs_a, dc=1)
    mine_b, theirs_b = quantized_next(CORNERS, act, rotated, exps, theirs_a)
    other_b = send(theirs_b, dc=1)
    mine_c, theirs_c = quantized_next(REST, act, rotated, exps, theirs_b)
    other_c = send(theirs_c, dc=1)
    right, left = sides_sum(mine_a, other_a, mine_b, mine_c)
    from_left, from_right = send(right, dx=1), send(left, dx=3)
    up, down, across, pairs = corners_sum(mine_b, other_b, mine_c, other_c)
    from_below, from_above = send(up, dz=1), send(down, dz=3)
    from_across = send(across, dx=2)
    z1, z2, z3, x1, x2, x3, own = middle_sum(
        pairs, from_left, from_right, from_below, from_above, from_across
    )
    parts = [
        own,
        send(z1, dz=1),
        send(z3, dz=3),
        send(z2, dz=2),
        send(x2, dx=2),
        send(x1, dx=1),
        send(x3, dx=3),
    ]
    *state_new, w = updated(parts, exps, sign_row, table, (master, moment, second))

    x3, x1, x2 = send(w, dx=3), send(w, dx=1), send(w, dx=2)
    z2, z3, z1 = send(w, dz=2), send(w, dz=3), send(w, dz=1)
    column, row, corner, first = fanned(w, x3, x1, x2, z2, z3, z1)
    other_first = send(first, dc=1)
    x2f = send(corner, dx=2)
    z3f, z1f = send(row, dz=3), send(row, dz=1)
    x3c, x1c = send(column, dx=3), send(column, dx=1)
    names = ((0, 0), (0, 1), (0, 3), (0, 2), (2, 0), (1, 0), (3, 0))
    weights, *state_new, token = placed(names, first, other_first, state_new, None)
    last = joined(x2f, z3f, z1f, x3c, x1c, after=(token,))
    names = ((2, 2), (2, 3), (2, 1), (3, 1), (3, 3), (3, 2), (1, 1), (1, 3), (1, 2))
    weights, _ = placed(names, last, send(last, dc=1), (), weights)
    return (*state_new, weights)


def solution(mesh):
    in_specs = (
        P("replica", None),
        P("replica", "tensor"),
        P(None, "tensor"),
        P("tensor"),
        P("replica", "tensor"),
        P("replica", "tensor"),
        P("replica", "tensor"),
    )
    out_specs = (
        P("replica", "tensor"),
        P("replica", "tensor"),
        P("replica", "tensor"),
        P("replica", "tensor"),
        P(None, "tensor"),
    )
    return jax.shard_map(
        on_device, mesh=mesh, in_specs=in_specs, out_specs=out_specs, check_vma=False
    )
```

time: 215 us -> 102 us (0.47)
  the two profiles are of different devices: /device:TPU:1 before, /device:TPU:41 now
where the time goes in v2:
time: 102 us
  starting transfers between devices  48.1 us (47%)
  waiting for transfers between devices  37.8 us (37%)
  Pallas kernels  15 us (15%)
    ppermute x27, starting transfers between devices, send(): return lax.ppermute(value, 'replica', replica_perm(dx, dz, dc))  48.1 us
    ppermute x27, waiting for transfers between devices, send(): return lax.ppermute(value, 'replica', replica_perm(dx, dz, dc))  37.8 us
    pallas_call x1, Pallas kernels, quantized_first(): pl.pallas_call(first_kernel, in_specs=[HBM] * 5, out_specs=[FULL] * 7, ou...  5.52 us
    pallas_call x2, Pallas kernels, placed(): pl.pallas_call(functools.partial(place_kernel, names, count, chained), in...  4.27 us
    pallas_call x2, Pallas kernels, quantized_next(): pl.pallas_call(functools.partial(next_kernel, blocks), in_specs=[FULL] *...  3.35 us
  transfers between devices with their start and end apart: 27, of which 8 were waited for; matrix products, arithmetic and copies ran while one was open for 0% of the time, Pallas kernels for 6%

profile of v2, /device:TPU:41, one launch (start us, length us, event | category | flops | bytes accessed | tf_op | source)
XLA Modules:
  0.0 101.9 jit_solution(13487810899782021443)
XLA Ops:
  0.6 5.5 %quantize_sides.1 = (bf16[6,64,1280]{2,1,0:T(8,128)(2,1)S(1)}, bf16[6,64,1280]{2,1,0:T(8,128)(2,1)S(1)}, bf16[768,2048]{1,0:T(8,128)(2,1)S(1)}, bf16[768,1280]{1...) custom-call(bf16[768,2048]{1,0:T(8,128)(2,1)} %act_far.1, ...), custom_call_target="tpu_custom_call" | custom-call | flops 1 | bytes 1 | tf_op jit(solution)/shard_map/quantize_sides/pallas_call | solution.py:149
  6.9 1.1 %quantize_more.2 = (bf16[3,64,1280]{2,1,0:T(8,128)(2,1)S(1)}, bf16[3,64,1280]{2,1,0:T(8,128)(2,1)S(1)}) custom-call(bf16[768,2048]{1,0:T(8,128)(2,1)S(1)} %get-tuple-element.45.act, bf16[768,1280]{1,0:T(8,128)(2,1)S(1)} %get-tuple-element.46.rotated, s32[5,2048]{1,0:T(8,128)S(1)} %get-tuple-element.47.exps.refs_7_, bf16[6,64,1280]{2,1,0:T(8,128)(2,1)S(1)} %get-tuple-element.48._), custom_call_target="tpu_custom_call" | custom-call | flops 1 | bytes 1 | tf_op jit(solution)/shard_map/quantize_more/pallas_call | solution.py:180
  8.0 2.3 %quantize_more.3 = (bf16[7,64,1280]{2,1,0:T(8,128)(2,1)S(1)}, bf16[7,64,1280]{2,1,0:T(8,128)(2,1)S(1)}) custom-call(bf16[768,2048]{1,0:T(8,128)(2,1)S(1)} %get-tuple-element.45.act, bf16[768,1280]{1,0:T(8,128)(2,1)S(1)} %get-tuple-element.46.rotated, s32[5,2048]{1,0:T(8,128)S(1)} %get-tuple-element.47.exps.refs_7_, bf16[3,64,1280]{2,1,0:T(8,128)(2,1)S(1)} %get-tuple-element.50._), custom_call_target="tpu_custom_call" | custom-call | flops 1 | bytes 1 | tf_op jit(solution)/shard_map/quantize_more/pallas_call | solution.py:180
  11.1 1.3 %collective-permute-start.3 = (bf16[3,64,1280]{2,1,0:T(8,128)(2,1)S(1)}, bf16[3,64,1280]{2,1,0:T(8,128)(2,1)S(1)}, u32[]{:S(2)}, u32[]{:S(2)}) collective-permute-start(bf16[3,64,1280]{2,1,0:T(8,128)(2,1)S(1)} %get-tuple-element.55), channel_id=1, source_target_pairs={{0,16},{8,24},{16,32},{24,40},{32,48},{40,56},{48,0},{56,8},{64,80... | collective-permute-start | bytes 1474568 | tf_op jit(solution)/shard_map/ppermute | solution.py:60
  12.4 1.5 %collective-permute-start.4 = (bf16[3,64,1280]{2,1,0:T(8,128)(2,1)S(1)}, bf16[3,64,1280]{2,1,0:T(8,128)(2,1)S(1)}, u32[]{:S(2)}, u32[]{:S(2)}) collective-permute-start(bf16[3,64,1280]{2,1,0:T(8,128)(2,1)S(1)} %get-tuple-element.56), channel_id=1, source_target_pairs={{0,48},{8,56},{16,0},{24,8},{32,16},{40,24},{48,32},{56,40},{64,11... | collective-permute-start | bytes 1474568 | tf_op jit(solution)/shard_map/ppermute | solution.py:60
  14.3 3.1 %collective-permute-start.5 = (bf16[64,1280]{1,0:T(8,128)(2,1)S(1)}, bf16[64,1280]{1,0:T(8,128)(2,1)S(1)}, u32[]{:S(2)}, u32[]{:S(2)}) collective-permute-start(bf16[64,1280]{1,0:T(8,128)(2,1)S(1)} %get-tuple-element.57), channel_id=1, source_target_pairs={{0,64},{8,72},{16,80},{24,88},{32,96},{40,104},{48,112},{56,120},{... | collective-permute-start | bytes 491528 | tf_op jit(solution)/shard_map/ppermute | solution.py:60
  17.4 2.2 %collective-permute-start.6 = (bf16[64,1280]{1,0:T(8,128)(2,1)S(1)}, bf16[64,1280]{1,0:T(8,128)(2,1)S(1)}, u32[]{:S(2)}, u32[]{:S(2)}) collective-permute-start(bf16[64,1280]{1,0:T(8,128)(2,1)S(1)} %get-tuple-element.58), channel_id=1, source_target_pairs={{0,192},{8,200},{16,208},{24,216},{32,224},{40,232},{48,240},{56,2... | collective-permute-start | bytes 491528 | tf_op jit(solution)/shard_map/ppermute | solution.py:60
  19.6 2.7 %collective-permute-start.7 = (bf16[64,1280]{1,0:T(8,128)(2,1)S(1)}, bf16[64,1280]{1,0:T(8,128)(2,1)S(1)}, u32[]{:S(2)}, u32[]{:S(2)}) collective-permute-start(bf16[64,1280]{1,0:T(8,128)(2,1)S(1)} %get-tuple-element.59), channel_id=1, source_target_pairs={{0,32},{8,40},{16,48},{24,56},{32,0},{40,8},{48,16},{56,24},{64,96... | collective-permute-start | bytes 491528 | tf_op jit(solution)/shard_map/ppermute | solution.py:60
  22.3 4.9 %collective-permute-done.5.below = bf16[64,1280]{1,0:T(8,128)(2,1)S(1)} collective-permute-done((bf16[64,1280]{1,0:T(8,128)(2,1)S(1)}, bf16[64,1280]{1,0:T(8,128)(2,1)S(1)}, u32[]{:S(2)}, u32[]{:S(2)}) %collective-permute-start.5) | collective-permute-done | bytes 163872 | tf_op jit(solution)/shard_map/ppermute | solution.py:60
  27.2 2.4 %collective-permute-done.7.across = bf16[64,1280]{1,0:T(8,128)(2,1)S(1)} collective-permute-done((bf16[64,1280]{1,0:T(8,128)(2,1)S(1)}, bf16[64,1280]{1,0:T(8,128)(2,1)S(1)}, u32[]{:S(2)}, u32[]{:S(2)}) %collective-permute-start.7) | collective-permute-done | bytes 163872 | tf_op jit(solution)/shard_map/ppermute | solution.py:60
  29.9 3.0 %collective-permute-start.8 = (bf16[64,1280]{1,0:T(8,128)(2,1)S(1)}, bf16[64,1280]{1,0:T(8,128)(2,1)S(1)}, u32[]{:S(2)}, u32[]{:S(2)}) collective-permute-start(bf16[64,1280]{1,0:T(8,128)(2,1)S(1)} %get-tuple-element.61), channel_id=1, source_target_pairs={{0,64},{8,72},{16,80},{24,88},{32,96},{40,104},{48,112},{56,120},{... | collective-permute-start | bytes 491528 | tf_op jit(solution)/shard_map/ppermute | solution.py:60
  33.0 2.2 %collective-permute-start.9 = (bf16[64,1280]{1,0:T(8,128)(2,1)S(1)}, bf16[64,1280]{1,0:T(8,128)(2,1)S(1)}, u32[]{:S(2)}, u32[]{:S(2)}) collective-permute-start(bf16[64,1280]{1,0:T(8,128)(2,1)S(1)} %get-tuple-element.62), channel_id=1, source_target_pairs={{0,192},{8,200},{16,208},{24,216},{32,224},{40,232},{48,240},{56,2... | collective-permute-start | bytes 491528 | tf_op jit(solution)/shard_map/ppermute | solution.py:60
  35.2 4.4 %collective-permute-start.10 = (bf16[64,1280]{1,0:T(8,128)(2,1)S(1)}, bf16[64,1280]{1,0:T(8,128)(2,1)S(1)}, u32[]{:S(2)}, u32[]{:S(2)}) collective-permute-start(bf16[64,1280]{1,0:T(8,128)(2,1)S(1)} %get-tuple-element.63), channel_id=1, source_target_pairs={{0,128},{8,136},{16,144},{24,152},{32,160},{40,168},{48,176},{56,1... | collective-permute-start | bytes 491528 | tf_op jit(solution)/shard_map/ppermute | solution.py:60
  40.1 1.2 %collective-permute-start.12 = (bf16[64,1280]{1,0:T(8,128)(2,1)S(1)}, bf16[64,1280]{1,0:T(8,128)(2,1)S(1)}, u32[]{:S(2)}, u32[]{:S(2)}) collective-permute-start(bf16[64,1280]{1,0:T(8,128)(2,1)S(1)} %get-tuple-element.65), channel_id=1, source_target_pairs={{0,16},{8,24},{16,32},{24,40},{32,48},{40,56},{48,0},{56,8},{64,80... | collective-permute-start | bytes 491528 | tf_op jit(solution)/shard_map/ppermute | solution.py:60
  41.3 2.8 %collective-permute-done.8.refs_1_ = bf16[64,1280]{1,0:T(8,128)(2,1)S(1)} collective-permute-done((bf16[64,1280]{1,0:T(8,128)(2,1)S(1)}, bf16[64,1280]{1,0:T(8,128)(2,1)S(1)}, u32[]{:S(2)}, u32[]{:S(2)}) %collective-permute-start.8) | collective-permute-done | bytes 163872 | tf_op jit(solution)/shard_map/ppermute | solution.py:60
  44.2 2.5 %collective-permute-start.13 = (bf16[64,1280]{1,0:T(8,128)(2,1)S(1)}, bf16[64,1280]{1,0:T(8,128)(2,1)S(1)}, u32[]{:S(2)}, u32[]{:S(2)}) collective-permute-start(bf16[64,1280]{1,0:T(8,128)(2,1)S(1)} %get-tuple-element.66), channel_id=1, source_target_pairs={{0,48},{8,56},{16,0},{24,8},{32,16},{40,24},{48,32},{56,40},{64,11... | collective-permute-start | bytes 491528 | tf_op jit(solution)/shard_map/ppermute | solution.py:60
  46.6 6.8 %collective-permute-done.10.refs_3_ = bf16[64,1280]{1,0:T(8,128)(2,1)S(1)} collective-permute-done((bf16[64,1280]{1,0:T(8,128)(2,1)S(1)}, bf16[64,1280]{1,0:T(8,128)(2,1)S(1)}, u32[]{:S(2)}, u32[]{:S(2)}) %collective-permute-start.10) | collective-permute-done | bytes 163872 | tf_op jit(solution)/shard_map/ppermute | solution.py:60
  54.4 3.6 %collective-permute-start.18 = (bf16[64,1280]{1,0:T(8,128)(2,1)S(1)}, bf16[64,1280]{1,0:T(8,128)(2,1)S(1)}, u32[]{:S(2)}, u32[]{:S(2)}) collective-permute-start(bf16[64,1280]{1,0:T(8,128)(2,1)S(1)} %get-tuple-element.69.w), channel_id=1, source_target_pairs={{0,192},{8,200},{16,208},{24,216},{32,224},{40,232},{48,240},{56,2... | collective-permute-start | bytes 491528 | tf_op jit(solution)/shard_map/ppermute | solution.py:60
  57.9 2.1 %collective-permute-start.17 = (bf16[64,1280]{1,0:T(8,128)(2,1)S(1)}, bf16[64,1280]{1,0:T(8,128)(2,1)S(1)}, u32[]{:S(2)}, u32[]{:S(2)}) collective-permute-start(bf16[64,1280]{1,0:T(8,128)(2,1)S(1)} %get-tuple-element.69.w), channel_id=1, source_target_pairs={{0,128},{8,136},{16,144},{24,152},{32,160},{40,168},{48,176},{56,1... | collective-permute-start | bytes 491528 | tf_op jit(solution)/shard_map/ppermute | solution.py:60
  60.0 1.3 %collective-permute-start.16 = (bf16[64,1280]{1,0:T(8,128)(2,1)S(1)}, bf16[64,1280]{1,0:T(8,128)(2,1)S(1)}, u32[]{:S(2)}, u32[]{:S(2)}) collective-permute-start(bf16[64,1280]{1,0:T(8,128)(2,1)S(1)} %get-tuple-element.69.w), channel_id=1, source_target_pairs={{0,32},{8,40},{16,48},{24,56},{32,0},{40,8},{48,16},{56,24},{64,96... | collective-permute-start | bytes 491528 | tf_op jit(solution)/shard_map/ppermute | solution.py:60
  61.7 6.0 %collective-permute-done.19.z1 = bf16[64,1280]{1,0:T(8,128)(2,1)S(1)} collective-permute-done((bf16[64,1280]{1,0:T(8,128)(2,1)S(1)}, bf16[64,1280]{1,0:T(8,128)(2,1)S(1)}, u32[]{:S(2)}, u32[]{:S(2)}) %collective-permute-start.19) | collective-permute-done | bytes 163872 | tf_op jit(solution)/shard_map/ppermute | solution.py:60
  67.7 3.0 %collective-permute-start.14 = (bf16[64,1280]{1,0:T(8,128)(2,1)S(1)}, bf16[64,1280]{1,0:T(8,128)(2,1)S(1)}, u32[]{:S(2)}, u32[]{:S(2)}) collective-permute-start(bf16[64,1280]{1,0:T(8,128)(2,1)S(1)} %get-tuple-element.69.w), channel_id=1, source_target_pairs={{0,48},{8,56},{16,0},{24,8},{32,16},{40,24},{48,32},{56,40},{64,11... | collective-permute-start | bytes 491528 | tf_op jit(solution)/shard_map/ppermute | solution.py:60
  70.7 2.5 %collective-permute-done.14.x3 = bf16[64,1280]{1,0:T(8,128)(2,1)S(1)} collective-permute-done((bf16[64,1280]{1,0:T(8,128)(2,1)S(1)}, bf16[64,1280]{1,0:T(8,128)(2,1)S(1)}, u32[]{:S(2)}, u32[]{:S(2)}) %collective-permute-start.14) | collective-permute-done | bytes 163872 | tf_op jit(solution)/shard_map/ppermute | solution.py:60
  73.4 2.6 %collective-permute-start.20 = (bf16[7,64,1280]{2,1,0:T(8,128)(2,1)S(1)}, bf16[7,64,1280]{2,1,0:T(8,128)(2,1)S(1)}, u32[]{:S(2)}, u32[]{:S(2)}) collective-permute-start(bf16[7,64,1280]{2,1,0:T(8,128)(2,1)S(1)} %get-tuple-element.70.refs_0_), channel_id=1, source_target_pairs={{0,8},{8,0},{16,24},{24,16},{32,40},{40,32},{48,56},{56,48},{64,72... | collective-permute-start | bytes 3440648 | tf_op jit(solution)/shard_map/ppermute | solution.py:60
  76.0 1.7 %collective-permute-start.25 = (bf16[3,64,1280]{2,1,0:T(8,128)(2,1)S(1)}, bf16[3,64,1280]{2,1,0:T(8,128)(2,1)S(1)}, u32[]{:S(2)}, u32[]{:S(2)}) collective-permute-start(bf16[3,64,1280]{2,1,0:T(8,128)(2,1)S(1)} %get-tuple-element.81), channel_id=1, source_target_pairs={{0,16},{8,24},{16,32},{24,40},{32,48},{40,56},{48,0},{56,8},{64,80... | collective-permute-start | bytes 1474568 | tf_op jit(solution)/shard_map/ppermute | solution.py:60
  77.7 1.7 %collective-permute-start.24 = (bf16[3,64,1280]{2,1,0:T(8,128)(2,1)S(1)}, bf16[3,64,1280]{2,1,0:T(8,128)(2,1)S(1)}, u32[]{:S(2)}, u32[]{:S(2)}) collective-permute-start(bf16[3,64,1280]{2,1,0:T(8,128)(2,1)S(1)} %get-tuple-element.81), channel_id=1, source_target_pairs={{0,48},{8,56},{16,0},{24,8},{32,16},{40,24},{48,32},{56,40},{64,11... | collective-permute-start | bytes 1474568 | tf_op jit(solution)/shard_map/ppermute | solution.py:60
  79.4 1.2 %collective-permute-start.21 = (bf16[64,1280]{1,0:T(8,128)(2,1)S(1)}, bf16[64,1280]{1,0:T(8,128)(2,1)S(1)}, u32[]{:S(2)}, u32[]{:S(2)}) collective-permute-start(bf16[64,1280]{1,0:T(8,128)(2,1)S(1)} %get-tuple-element.79), channel_id=1, source_target_pairs={{0,32},{8,40},{16,48},{24,56},{32,0},{40,8},{48,16},{56,24},{64,96... | collective-permute-start | bytes 491528 | tf_op jit(solution)/shard_map/ppermute | solution.py:60
  80.6 3.6 %collective-permute-start.22 = (bf16[64,1280]{1,0:T(8,128)(2,1)S(1)}, bf16[64,1280]{1,0:T(8,128)(2,1)S(1)}, u32[]{:S(2)}, u32[]{:S(2)}) collective-permute-start(bf16[64,1280]{1,0:T(8,128)(2,1)S(1)} %get-tuple-element.80), channel_id=1, source_target_pairs={{0,192},{8,200},{16,208},{24,216},{32,224},{40,232},{48,240},{56,2... | collective-permute-start | bytes 491528 | tf_op jit(solution)/shard_map/ppermute | solution.py:60
  84.2 2.0 %place.2 = (bf16[2048,1280]{1,0:T(8,128)(2,1)}, f32[64,1280]{1,0:T(8,128)}, f32[64,1280]{1,0:T(8,128)}, f32[64,1280]{1,0:T(8,128)}, f32[64,1280]{1,0:T(8,128)}, /*index=5*/bf16[16,128]{1,0:T(8,128)(2,1)S(1)}) custom-call(bf16[7,64,1280]{2,1,0:T(8,128)(2,1)S(1)} %get-tuple-element.70.refs_0_, bf16[7,64,1280]{2,1,0:T(8,128)(2,1)S(1)} %collective-permute-done.20.refs_1_, ...), custom_call_target="tpu_custom_call" | custom-call | flops 1 | bytes 1 | tf_op jit(solution)/shard_map/place/pallas_call | solution.py:387
  86.2 9.3 %collective-permute-done.21.refs_0_ = bf16[64,1280]{1,0:T(8,128)(2,1)S(1)} collective-permute-done((bf16[64,1280]{1,0:T(8,128)(2,1)S(1)}, bf16[64,1280]{1,0:T(8,128)(2,1)S(1)}, u32[]{:S(2)}, u32[]{:S(2)}) %collective-permute-start.21) | collective-permute-done | bytes 163872 | tf_op jit(solution)/shard_map/ppermute | solution.py:60
  96.5 2.9 %collective-permute-done.26.refs_1_ = bf16[9,64,1280]{2,1,0:T(8,128)(2,1)S(1)} collective-permute-done((bf16[9,64,1280]{2,1,0:T(8,128)(2,1)S(1)}, bf16[9,64,1280]{2,1,0:T(8,128)(2,1)S(1)}, u32[]{:S(2)}, u32[]{:S(2)}) %collective-permute-start.26) | collective-permute-done | bytes 1474592 | tf_op jit(solution)/shard_map/ppermute | solution.py:60
  99.4 2.3 %place.3 = (bf16[2048,1280]{1,0:T(8,128)(2,1)}, bf16[16,128]{1,0:T(8,128)(2,1)}) custom-call(bf16[9,64,1280]{2,1,0:T(8,128)(2,1)S(1)} %join.1.refs_0_, bf16[9,64,1280]{2,1,0:T(8,128)(2,1)S(1)} %collective-permute-done.26.refs_1_, bf16[2048,1280]{1,0:T(8,128)(2,1)} %get-tuple-element.83.refs_2_), custom_call_target="tpu_custom_call", output_to_operand_aliasing={{0}: (2, {})} | custom-call | flops 1 | bytes 1 | tf_op jit(solution)/shard_map/place/pallas_call | solution.py:387
  (39 shorter events, 5.2 us)
Async XLA Ops:
  6.2 4.7 %collective-permute-start.2 = (bf16[6,64,1280]{2,1,0:T(8,128)(2,1)S(1)}, bf16[6,64,1280]{2,1,0:T(8,128)(2,1)S(1)}, u32[]{:S(2)}, u32[]{:S(2)}) collective-permute-start(bf16[6,64,1280]{2,1,0:T(8,128)(2,1)S(1)} %get-tuple-element.48._), channel_id=1, source_target_pairs={{0,8},{8,0},{16,24},{24,16},{32,40},{40,32},{48,56},{56,48},{64,72... | collective-permute-start | bytes 2949128 | tf_op jit(solution)/shard_map/ppermute | solution.py:60
  10.3 3.6 %collective-permute-start.1 = (bf16[7,64,1280]{2,1,0:T(8,128)(2,1)S(1)}, bf16[7,64,1280]{2,1,0:T(8,128)(2,1)S(1)}, u32[]{:S(2)}, u32[]{:S(2)}) collective-permute-start(bf16[7,64,1280]{2,1,0:T(8,128)(2,1)S(1)} %get-tuple-element.52), channel_id=1, source_target_pairs={{0,8},{8,0},{16,24},{24,16},{32,40},{40,32},{48,56},{56,48},{64,72... | collective-permute-start | bytes 3440648 | tf_op jit(solution)/shard_map/ppermute | solution.py:60
  10.4 3.5 %collective-permute-start = (bf16[3,64,1280]{2,1,0:T(8,128)(2,1)S(1)}, bf16[3,64,1280]{2,1,0:T(8,128)(2,1)S(1)}, u32[]{:S(2)}, u32[]{:S(2)}) collective-permute-start(bf16[3,64,1280]{2,1,0:T(8,128)(2,1)S(1)} %get-tuple-element.50._), channel_id=1, source_target_pairs={{0,8},{8,0},{16,24},{24,16},{32,40},{40,32},{48,56},{56,48},{64,72... | collective-permute-start | bytes 1474568 | tf_op jit(solution)/shard_map/ppermute | solution.py:60
  11.1 18.6 %collective-permute-start.3 = (bf16[3,64,1280]{2,1,0:T(8,128)(2,1)S(1)}, bf16[3,64,1280]{2,1,0:T(8,128)(2,1)S(1)}, u32[]{:S(2)}, u32[]{:S(2)}) collective-permute-start(bf16[3,64,1280]{2,1,0:T(8,128)(2,1)S(1)} %get-tuple-element.55), channel_id=1, source_target_pairs={{0,16},{8,24},{16,32},{24,40},{32,48},{40,56},{48,0},{56,8},{64,80... | collective-permute-start | bytes 1474568 | tf_op jit(solution)/shard_map/ppermute | solution.py:60
  12.4 17.3 %collective-permute-start.4 = (bf16[3,64,1280]{2,1,0:T(8,128)(2,1)S(1)}, bf16[3,64,1280]{2,1,0:T(8,128)(2,1)S(1)}, u32[]{:S(2)}, u32[]{:S(2)}) collective-permute-start(bf16[3,64,1280]{2,1,0:T(8,128)(2,1)S(1)} %get-tuple-element.56), channel_id=1, source_target_pairs={{0,48},{8,56},{16,0},{24,8},{32,16},{40,24},{48,32},{56,40},{64,11... | collective-permute-start | bytes 1474568 | tf_op jit(solution)/shard_map/ppermute | solution.py:60
  14.3 39.2 %copy-start = (f32[64,1280]{1,0:T(8,128)S(1)}, f32[64,1280]{1,0:T(8,128)}, u32[]{:S(2)}) copy-start(f32[64,1280]{1,0:T(8,128)} %refs_10_.1) | copy-start | bytes 983044
  14.3 39.2 %copy-start.1 = (f32[64,1280]{1,0:T(8,128)S(1)}, f32[64,1280]{1,0:T(8,128)}, u32[]{:S(2)}) copy-start(f32[64,1280]{1,0:T(8,128)} %refs_11_.1) | copy-start | bytes 983044
  14.3 39.2 %copy-start.2 = (f32[64,1280]{1,0:T(8,128)S(1)}, f32[64,1280]{1,0:T(8,128)}, u32[]{:S(2)}) copy-start(f32[64,1280]{1,0:T(8,128)} %refs_12_.1) | copy-start | bytes 983044
  14.3 12.9 %collective-permute-start.5 = (bf16[64,1280]{1,0:T(8,128)(2,1)S(1)}, bf16[64,1280]{1,0:T(8,128)(2,1)S(1)}, u32[]{:S(2)}, u32[]{:S(2)}) collective-permute-start(bf16[64,1280]{1,0:T(8,128)(2,1)S(1)} %get-tuple-element.57), channel_id=1, source_target_pairs={{0,64},{8,72},{16,80},{24,88},{32,96},{40,104},{48,112},{56,120},{... | collective-permute-start | bytes 491528 | tf_op jit(solution)/shard_map/ppermute | solution.py:60
  17.4 9.9 %collective-permute-start.6 = (bf16[64,1280]{1,0:T(8,128)(2,1)S(1)}, bf16[64,1280]{1,0:T(8,128)(2,1)S(1)}, u32[]{:S(2)}, u32[]{:S(2)}) collective-permute-start(bf16[64,1280]{1,0:T(8,128)(2,1)S(1)} %get-tuple-element.58), channel_id=1, source_target_pairs={{0,192},{8,200},{16,208},{24,216},{32,224},{40,232},{48,240},{56,2... | collective-permute-start | bytes 491528 | tf_op jit(solution)/shard_map/ppermute | solution.py:60
  19.6 10.1 %collective-permute-start.7 = (bf16[64,1280]{1,0:T(8,128)(2,1)S(1)}, bf16[64,1280]{1,0:T(8,128)(2,1)S(1)}, u32[]{:S(2)}, u32[]{:S(2)}) collective-permute-start(bf16[64,1280]{1,0:T(8,128)(2,1)S(1)} %get-tuple-element.59), channel_id=1, source_target_pairs={{0,32},{8,40},{16,48},{24,56},{32,0},{40,8},{48,16},{56,24},{64,96... | collective-permute-start | bytes 491528 | tf_op jit(solution)/shard_map/ppermute | solution.py:60
  29.9 14.2 %collective-permute-start.8 = (bf16[64,1280]{1,0:T(8,128)(2,1)S(1)}, bf16[64,1280]{1,0:T(8,128)(2,1)S(1)}, u32[]{:S(2)}, u32[]{:S(2)}) collective-permute-start(bf16[64,1280]{1,0:T(8,128)(2,1)S(1)} %get-tuple-element.61), channel_id=1, source_target_pairs={{0,64},{8,72},{16,80},{24,88},{32,96},{40,104},{48,112},{56,120},{... | collective-permute-start | bytes 491528 | tf_op jit(solution)/shard_map/ppermute | solution.py:60
  33.0 13.6 %collective-permute-start.9 = (bf16[64,1280]{1,0:T(8,128)(2,1)S(1)}, bf16[64,1280]{1,0:T(8,128)(2,1)S(1)}, u32[]{:S(2)}, u32[]{:S(2)}) collective-permute-start(bf16[64,1280]{1,0:T(8,128)(2,1)S(1)} %get-tuple-element.62), channel_id=1, source_target_pairs={{0,192},{8,200},{16,208},{24,216},{32,224},{40,232},{48,240},{56,2... | collective-permute-start | bytes 491528 | tf_op jit(solution)/shard_map/ppermute | solution.py:60
  35.2 18.2 %collective-permute-start.10 = (bf16[64,1280]{1,0:T(8,128)(2,1)S(1)}, bf16[64,1280]{1,0:T(8,128)(2,1)S(1)}, u32[]{:S(2)}, u32[]{:S(2)}) collective-permute-start(bf16[64,1280]{1,0:T(8,128)(2,1)S(1)} %get-tuple-element.63), channel_id=1, source_target_pairs={{0,128},{8,136},{16,144},{24,152},{32,160},{40,168},{48,176},{56,1... | collective-permute-start | bytes 491528 | tf_op jit(solution)/shard_map/ppermute | solution.py:60
  39.6 13.9 %collective-permute-start.11 = (bf16[64,1280]{1,0:T(8,128)(2,1)S(1)}, bf16[64,1280]{1,0:T(8,128)(2,1)S(1)}, u32[]{:S(2)}, u32[]{:S(2)}) collective-permute-start(bf16[64,1280]{1,0:T(8,128)(2,1)S(1)} %get-tuple-element.64), channel_id=1, source_target_pairs={{0,32},{8,40},{16,48},{24,56},{32,0},{40,8},{48,16},{56,24},{64,96... | collective-permute-start | bytes 491528 | tf_op jit(solution)/shard_map/ppermute | solution.py:60
  40.1 13.3 %collective-permute-start.12 = (bf16[64,1280]{1,0:T(8,128)(2,1)S(1)}, bf16[64,1280]{1,0:T(8,128)(2,1)S(1)}, u32[]{:S(2)}, u32[]{:S(2)}) collective-permute-start(bf16[64,1280]{1,0:T(8,128)(2,1)S(1)} %get-tuple-element.65), channel_id=1, source_target_pairs={{0,16},{8,24},{16,32},{24,40},{32,48},{40,56},{48,0},{56,8},{64,80... | collective-permute-start | bytes 491528 | tf_op jit(solution)/shard_map/ppermute | solution.py:60
  44.2 9.3 %collective-permute-start.13 = (bf16[64,1280]{1,0:T(8,128)(2,1)S(1)}, bf16[64,1280]{1,0:T(8,128)(2,1)S(1)}, u32[]{:S(2)}, u32[]{:S(2)}) collective-permute-start(bf16[64,1280]{1,0:T(8,128)(2,1)S(1)} %get-tuple-element.66), channel_id=1, source_target_pairs={{0,48},{8,56},{16,0},{24,8},{32,16},{40,24},{48,32},{56,40},{64,11... | collective-permute-start | bytes 491528 | tf_op jit(solution)/shard_map/ppermute | solution.py:60
  54.3 13.4 %collective-permute-start.19 = (bf16[64,1280]{1,0:T(8,128)(2,1)S(1)}, bf16[64,1280]{1,0:T(8,128)(2,1)S(1)}, u32[]{:S(2)}, u32[]{:S(2)}) collective-permute-start(bf16[64,1280]{1,0:T(8,128)(2,1)S(1)} %get-tuple-element.69.w), channel_id=1, source_target_pairs={{0,64},{8,72},{16,80},{24,88},{32,96},{40,104},{48,112},{56,120},{... | collective-permute-start | bytes 491528 | tf_op jit(solution)/shard_map/ppermute | solution.py:60
  54.4 16.3 %collective-permute-start.18 = (bf16[64,1280]{1,0:T(8,128)(2,1)S(1)}, bf16[64,1280]{1,0:T(8,128)(2,1)S(1)}, u32[]{:S(2)}, u32[]{:S(2)}) collective-permute-start(bf16[64,1280]{1,0:T(8,128)(2,1)S(1)} %get-tuple-element.69.w), channel_id=1, source_target_pairs={{0,192},{8,200},{16,208},{24,216},{32,224},{40,232},{48,240},{56,2... | collective-permute-start | bytes 491528 | tf_op jit(solution)/shard_map/ppermute | solution.py:60
  57.9 12.8 %collective-permute-start.17 = (bf16[64,1280]{1,0:T(8,128)(2,1)S(1)}, bf16[64,1280]{1,0:T(8,128)(2,1)S(1)}, u32[]{:S(2)}, u32[]{:S(2)}) collective-permute-start(bf16[64,1280]{1,0:T(8,128)(2,1)S(1)} %get-tuple-element.69.w), channel_id=1, source_target_pairs={{0,128},{8,136},{16,144},{24,152},{32,160},{40,168},{48,176},{56,1... | collective-permute-start | bytes 491528 | tf_op jit(solution)/shard_map/ppermute | solution.py:60
  60.0 10.7 %collective-permute-start.16 = (bf16[64,1280]{1,0:T(8,128)(2,1)S(1)}, bf16[64,1280]{1,0:T(8,128)(2,1)S(1)}, u32[]{:S(2)}, u32[]{:S(2)}) collective-permute-start(bf16[64,1280]{1,0:T(8,128)(2,1)S(1)} %get-tuple-element.69.w), channel_id=1, source_target_pairs={{0,32},{8,40},{16,48},{24,56},{32,0},{40,8},{48,16},{56,24},{64,96... | collective-permute-start | bytes 491528 | tf_op jit(solution)/shard_map/ppermute | solution.py:60
  61.3 9.4 %collective-permute-start.15 = (bf16[64,1280]{1,0:T(8,128)(2,1)S(1)}, bf16[64,1280]{1,0:T(8,128)(2,1)S(1)}, u32[]{:S(2)}, u32[]{:S(2)}) collective-permute-start(bf16[64,1280]{1,0:T(8,128)(2,1)S(1)} %get-tuple-element.69.w), channel_id=1, source_target_pairs={{0,16},{8,24},{16,32},{24,40},{32,48},{40,56},{48,0},{56,8},{64,80... | collective-permute-start | bytes 491528 | tf_op jit(solution)/shard_map/ppermute | solution.py:60
  67.7 5.6 %collective-permute-start.14 = (bf16[64,1280]{1,0:T(8,128)(2,1)S(1)}, bf16[64,1280]{1,0:T(8,128)(2,1)S(1)}, u32[]{:S(2)}, u32[]{:S(2)}) collective-permute-start(bf16[64,1280]{1,0:T(8,128)(2,1)S(1)} %get-tuple-element.69.w), channel_id=1, source_target_pairs={{0,48},{8,56},{16,0},{24,8},{32,16},{40,24},{48,32},{56,40},{64,11... | collective-permute-start | bytes 491528 | tf_op jit(solution)/shard_map/ppermute | solution.py:60
  73.4 7.2 %collective-permute-start.20 = (bf16[7,64,1280]{2,1,0:T(8,128)(2,1)S(1)}, bf16[7,64,1280]{2,1,0:T(8,128)(2,1)S(1)}, u32[]{:S(2)}, u32[]{:S(2)}) collective-permute-start(bf16[7,64,1280]{2,1,0:T(8,128)(2,1)S(1)} %get-tuple-element.70.refs_0_), channel_id=1, source_target_pairs={{0,8},{8,0},{16,24},{24,16},{32,40},{40,32},{48,56},{56,48},{64,72... | collective-permute-start | bytes 3440648 | tf_op jit(solution)/shard_map/ppermute | solution.py:60
  76.0 19.4 %collective-permute-start.25 = (bf16[3,64,1280]{2,1,0:T(8,128)(2,1)S(1)}, bf16[3,64,1280]{2,1,0:T(8,128)(2,1)S(1)}, u32[]{:S(2)}, u32[]{:S(2)}) collective-permute-start(bf16[3,64,1280]{2,1,0:T(8,128)(2,1)S(1)} %get-tuple-element.81), channel_id=1, source_target_pairs={{0,16},{8,24},{16,32},{24,40},{32,48},{40,56},{48,0},{56,8},{64,80... | collective-permute-start | bytes 1474568 | tf_op jit(solution)/shard_map/ppermute | solution.py:60
  77.7 17.7 %collective-permute-start.24 = (bf16[3,64,1280]{2,1,0:T(8,128)(2,1)S(1)}, bf16[3,64,1280]{2,1,0:T(8,128)(2,1)S(1)}, u32[]{:S(2)}, u32[]{:S(2)}) collective-permute-start(bf16[3,64,1280]{2,1,0:T(8,128)(2,1)S(1)} %get-tuple-element.81), channel_id=1, source_target_pairs={{0,48},{8,56},{16,0},{24,8},{32,16},{40,24},{48,32},{56,40},{64,11... | collective-permute-start | bytes 1474568 | tf_op jit(solution)/shard_map/ppermute | solution.py:60
  79.4 16.0 %collective-permute-start.21 = (bf16[64,1280]{1,0:T(8,128)(2,1)S(1)}, bf16[64,1280]{1,0:T(8,128)(2,1)S(1)}, u32[]{:S(2)}, u32[]{:S(2)}) collective-permute-start(bf16[64,1280]{1,0:T(8,128)(2,1)S(1)} %get-tuple-element.79), channel_id=1, source_target_pairs={{0,32},{8,40},{16,48},{24,56},{32,0},{40,8},{48,16},{56,24},{64,96... | collective-permute-start | bytes 491528 | tf_op jit(solution)/shard_map/ppermute | solution.py:60
  80.6 14.8 %collective-permute-start.23 = (bf16[64,1280]{1,0:T(8,128)(2,1)S(1)}, bf16[64,1280]{1,0:T(8,128)(2,1)S(1)}, u32[]{:S(2)}, u32[]{:S(2)}) collective-permute-start(bf16[64,1280]{1,0:T(8,128)(2,1)S(1)} %get-tuple-element.80), channel_id=1, source_target_pairs={{0,64},{8,72},{16,80},{24,88},{32,96},{40,104},{48,112},{56,120},{... | collective-permute-start | bytes 491528 | tf_op jit(solution)/shard_map/ppermute | solution.py:60
  80.6 14.8 %collective-permute-start.22 = (bf16[64,1280]{1,0:T(8,128)(2,1)S(1)}, bf16[64,1280]{1,0:T(8,128)(2,1)S(1)}, u32[]{:S(2)}, u32[]{:S(2)}) collective-permute-start(bf16[64,1280]{1,0:T(8,128)(2,1)S(1)} %get-tuple-element.80), channel_id=1, source_target_pairs={{0,192},{8,200},{16,208},{24,216},{32,224},{40,232},{48,240},{56,2... | collective-permute-start | bytes 491528 | tf_op jit(solution)/shard_map/ppermute | solution.py:60
  95.6 3.9 %collective-permute-start.26 = (bf16[9,64,1280]{2,1,0:T(8,128)(2,1)S(1)}, bf16[9,64,1280]{2,1,0:T(8,128)(2,1)S(1)}, u32[]{:S(2)}, u32[]{:S(2)}) collective-permute-start(bf16[9,64,1280]{2,1,0:T(8,128)(2,1)S(1)} %join.1.refs_0_), channel_id=1, source_target_pairs={{0,8},{8,0},{16,24},{24,16},{32,40},{40,32},{48,56},{56,48},{64,72... | collective-permute-start | bytes 4423688 | tf_op jit(solution)/shard_map/ppermute | solution.py:60

commit v3 on v2

--- a/solution.py
+++ b/solution.py
@@ -105,43 +105,35 @@
     mine, theirs, act, rotated, exps, signs, table,
     grads, line, sems,
 ):
-    zh, _, _ = place_of()
     small = [
         pltpu.make_async_copy(signs_far, line, sems.at[0]),
         pltpu.make_async_copy(table_far, table, sems.at[1]),
         pltpu.make_async_copy(exps_far, exps, sems.at[2]),
     ]
-    tiles = []
-    for tile in range(TILES):
-        cut = pl.ds(tile * TILE, TILE)
-        tiles.append(
-            pltpu.make_async_copy(grads_far.at[:, cut], grads.at[:, cut], sems.at[3 + tile])
-        )
-    quarters = []
-    for dz in (1, 2, 3, 0):
-        lanes = pl.ds(pl.multiple_of(lax.rem(zh + dz, NZ) * (ROWS // NZ), ROWS // NZ), ROWS // NZ)
-        quarters.append(
-            pltpu.make_async_copy(
-                act_far.at[:, lanes], act.at[:, lanes], sems.at[3 + TILES + len(quarters)]
+    strips = []
+    for far_ref, near, count in ((grads_far, grads, 3), (act_far, act, 4)):
+        for k in range(count):
+            rows = pl.ds(k * TOK // count, TOK // count)
+            strips.append(
+                pltpu.make_async_copy(far_ref.at[rows], near.at[rows], sems.at[3 + len(strips)])
             )
-        )
-    for copy in small + tiles:
+    for copy in small + strips:
         copy.start()
     for copy in small:
         copy.wait()
     signs[...] = line[...].reshape(1, COLS)
-    for tile in range(TILES):
-        cut = slice(tile * TILE, (tile + 1) * TILE)
-        tiles[tile].wait()
-        if tile < len(quarters):
-            quarters[tile].start()
-        flipped = grads[:, cut] * signs[:, cut].astype(BF)
-        rotated[:, cut] = jnp.dot(flipped, table[...], preferred_element_type=F32).astype(BF)
+    for k in range(3):
+        rows = slice(k * TOK // 3, (k + 1) * TOK // 3)
+        strips[k].wait()
+        for tile in range(TILES):
+            cut = slice(tile * TILE, (tile + 1) * TILE)
+            flipped = grads[rows, cut] * signs[:, cut].astype(BF)
+            turned = jnp.dot(flipped, table[...], preferred_element_type=F32)
+            rotated[rows, cut] = turned.astype(BF)
+    for copy in strips[3:]:
+        copy.wait()
     for k, (dx, dz) in enumerate(SIDES):
-        if k % 2 == 0:
-            quarters[k // 2].wait()
         quant_group(dx, dz, act, rotated, exps, mine, theirs, k)
-    quarters[3].wait()
 
 
 def quantized_first(act, grads, exps, signs, table):
@@ -162,7 +154,7 @@
         scratch_shapes=[
             pltpu.VMEM((TOK, COLS), BF),
             pltpu.VMEM((COLS,), jnp.int32),
-            pltpu.SemaphoreType.DMA((7 + TILES,)),
+            pltpu.SemaphoreType.DMA((10,)),
         ],
         compiler_params=params(12),
         cost_estimate=TINY,
@@ -255,10 +247,26 @@
     )(*held(*parts))
 
 
+def seen_kernel(*refs):
+    refs[-1][...] = jnp.zeros_like(refs[-1])
+
+
+def seen(*parts):
+    return pl.pallas_call(
+        seen_kernel,
+        in_specs=[FULL] * len(parts),
+        out_specs=FULL,
+        out_shape=vmem(16, 128),
+        compiler_params=params(1),
+        cost_estimate=TINY,
+        name="seen",
+    )(*held(*parts))
+
+
 def update_kernel(*refs):
     parts = refs[0:7]
     exps, signs, table, master, moment, second = refs[7:13]
-    grad_out, moment_out, second_out, master_out, weights_out = refs[13:18]
+    grad_out, moment_out, second_out, master_out, weights_out = refs[14:19]
     zh, x, core = place_of()
     lanes = pl.ds(pl.multiple_of((zh * NX + x) * GROUP, GROUP), GROUP)
     growth = jnp.exp2(exps[:, lanes].astype(F32)).T
@@ -294,16 +302,16 @@
         master_out[:, cut] = master_new
 
 
-def updated(parts, exps, signs, table, state):
+def updated(parts, exps, signs, table, state, after):
     return pl.pallas_call(
         update_kernel,
-        in_specs=[FULL] * 13,
+        in_specs=[FULL] * 14,
         out_specs=[FULL] * 5,
         out_shape=[vmem(ROW, COLS, dtype=F32)] * 4 + [vmem(ROW, COLS)],
         compiler_params=params(4),
         cost_estimate=TINY,
         name="update",
-    )(*held(*parts, exps, signs, table, *state))
+    )(*held(*parts, exps, signs, table, *state, after))
 
 
 def join_kernel(count, *refs):
@@ -331,7 +339,7 @@
     )(*held(*parts, *after))
 
 
-def fan_kernel(w, x3, x1, x2, z2, z3, z1, column, row, corner, first):
+def fan_kernel(w, x3, x1, x2, z2, z3, z1, _, column, row, corner, first):
     for k, part in enumerate((z1, z3, z2)):
         column[k] = part[...]
     row[...] = x2[...]
@@ -343,7 +351,7 @@
 def fanned(*parts):
     return pl.pallas_call(
         fan_kernel,
-        in_specs=[FULL] * 7,
+        in_specs=[FULL] * 8,
         out_specs=[FULL] * 4,
         out_shape=[vmem(3, ROW, COLS), vmem(ROW, COLS), vmem(ROW, COLS), vmem(7, ROW, COLS)],
         compiler_params=params(2),
@@ -352,16 +360,17 @@
     )(*held(*parts))
 
 
-def place_kernel(names, count, chained, *refs):
-    pieces = refs[:2]
-    state = refs[2 : 2 + count]
-    out = refs[2 + count + chained]
-    state_out = refs[3 + count + chained : 3 + 2 * count + chained]
+def place_kernel(names, flips, count, chained, *refs):
+    pieces = refs[: len(flips)]
+    refs = refs[len(flips) :]
+    state = refs[:count]
+    out = refs[count + chained]
+    state_out = refs[1 + count + chained : 1 + 2 * count + chained]
     token, sems = refs[-2:]
     token[...] = jnp.zeros_like(token)
     zh, x, core = place_of()
     copies = []
-    for flip, piece in enumerate(pieces):
+    for flip, piece in zip(flips, pieces):
         row_core = 1 - core if flip else core
         for k, (dx, dz) in enumerate(names):
             z_from = lax.rem(zh + NZ - dz, NZ)
@@ -380,21 +389,21 @@
         copy.wait()
 
 
-def placed(names, mine, other, state, previous):
+def placed(names, flips, pieces, state, previous):
     count = len(state)
     chained = previous is not None
     full = jax.ShapeDtypeStruct((ROW, COLS), F32)
     return pl.pallas_call(
-        functools.partial(place_kernel, names, count, chained),
-        in_specs=[FULL] * (2 + count) + [HBM] * chained,
+        functools.partial(place_kernel, names, flips, count, chained),
+        in_specs=[FULL] * (len(flips) + count) + [HBM] * chained,
         out_specs=[HBM] * (1 + count) + [FULL],
         out_shape=[jax.ShapeDtypeStruct((ROWS, COLS), BF)] + [full] * count + [vmem(16, 128)],
-        input_output_aliases={2 + count: 0} if chained else {},
-        scratch_shapes=[pltpu.SemaphoreType.DMA((2 * len(names) + count,))],
+        input_output_aliases={len(flips) + count: 0} if chained else {},
+        scratch_shapes=[pltpu.SemaphoreType.DMA((len(flips) * len(names) + count,))],
         compiler_params=params(2),
         cost_estimate=TINY,
         name="place",
-    )(*held(mine, other, *state), *((previous,) if chained else ()))
+    )(*held(*pieces, *state), *((previous,) if chained else ()))
 
 
 def on_device(activations, out_grads, exponents, signs, master, moment, second):
@@ -424,20 +433,27 @@
         send(x1, dx=1),
         send(x3, dx=3),
     ]
-    *state_new, w = updated(parts, exps, sign_row, table, (master, moment, second))
+    token = seen(parts[3], parts[4], seen(parts[1], parts[2]))
+    state = (master, moment, second)
+    *state_new, w = updated(parts, exps, sign_row, table, state, token)
 
     x3, x1, x2 = send(w, dx=3), send(w, dx=1), send(w, dx=2)
     z2, z3, z1 = send(w, dz=2), send(w, dz=3), send(w, dz=1)
-    column, row, corner, first = fanned(w, x3, x1, x2, z2, z3, z1)
+    token = seen(z2, x2, seen(z1, z3))
+    column, row, corner, first = fanned(w, x3, x1, x2, z2, z3, z1, token)
     other_first = send(first, dc=1)
     x2f = send(corner, dx=2)
     z3f, z1f = send(row, dz=3), send(row, dz=1)
     x3c, x1c = send(column, dx=3), send(column, dx=1)
     names = ((0, 0), (0, 1), (0, 3), (0, 2), (2, 0), (1, 0), (3, 0))
-    weights, *state_new, token = placed(names, first, other_first, state_new, None)
+    weights, *state_new, token = placed(
+        names, (False, True), (first, other_first), state_new, None
+    )
     last = joined(x2f, z3f, z1f, x3c, x1c, after=(token,))
     names = ((2, 2), (2, 3), (2, 1), (3, 1), (3, 3), (3, 2), (1, 1), (1, 3), (1, 2))
-    weights, _ = placed(names, last, send(last, dc=1), (), weights)
+    other_last = send(last, dc=1)
+    weights, _ = placed(names, (False,), (last,), (), weights)
+    weights, _ = placed(names, (True,), (other_last,), (), weights)
     return (*state_new, weights)
 
 

time: 102 us -> 101 us (level)
  the two profiles are of different devices: /device:TPU:41 before, /device:TPU:89 now
where the time goes in v3:
time: 101 us
  starting transfers between devices  43.5 us (43%)
  waiting for transfers between devices  41 us (41%)
  Pallas kernels  15.3 us (15%)
    ppermute x27, starting transfers between devices, send(): return lax.ppermute(value, 'replica', replica_perm(dx, dz, dc))  43.5 us
    ppermute x27, waiting for transfers between devices, send(): return lax.ppermute(value, 'replica', replica_perm(dx, dz, dc))  41 us
    pallas_call x3, Pallas kernels, placed(): pl.pallas_call(functools.partial(place_kernel, names, flips, count, chain...  5.49 us
    pallas_call x1, Pallas kernels, quantized_first(): pl.pallas_call(first_kernel, in_specs=[HBM] * 5, out_specs=[FULL] * 7, ou...  4.63 us
    pallas_call x2, Pallas kernels, quantized_next(): pl.pallas_call(functools.partial(next_kernel, blocks), in_specs=[FULL] *...  3.36 us
  transfers between devices with their start and end apart: 27, of which 12 were waited for; matrix products, arithmetic and copies ran while one was open for 0% of the time, Pallas kernels for 8%

profile of v3, /device:TPU:89, one launch (start us, length us, event | category | flops | bytes accessed | tf_op | source)
XLA Modules:
  0.0 100.8 jit_solution(12418668423239562510)
XLA Ops:
  0.6 4.6 %quantize_sides.1 = (bf16[6,64,1280]{2,1,0:T(8,128)(2,1)S(1)}, bf16[6,64,1280]{2,1,0:T(8,128)(2,1)S(1)}, bf16[768,2048]{1,0:T(8,128)(2,1)S(1)}, bf16[768,1280]{1...) custom-call(bf16[768,2048]{1,0:T(8,128)(2,1)} %act_far.1, ...), custom_call_target="tpu_custom_call" | custom-call | flops 1 | bytes 1 | tf_op jit(solution)/shard_map/quantize_sides/pallas_call | solution.py:141
  5.3 0.8 collective-permute-start.2
  6.0 1.1 %quantize_more.2 = (bf16[3,64,1280]{2,1,0:T(8,128)(2,1)S(1)}, bf16[3,64,1280]{2,1,0:T(8,128)(2,1)S(1)}) custom-call(bf16[768,2048]{1,0:T(8,128)(2,1)S(1)} %get-tuple-element.46.act, bf16[768,1280]{1,0:T(8,128)(2,1)S(1)} %get-tuple-element.47.rotated, s32[5,2048]{1,0:T(8,128)S(1)} %get-tuple-element.48.exps.refs_7_, bf16[6,64,1280]{2,1,0:T(8,128)(2,1)S(1)} %get-tuple-element.49._), custom_call_target="tpu_custom_call" | custom-call | flops 1 | bytes 1 | tf_op jit(solution)/shard_map/quantize_more/pallas_call | solution.py:172
  7.1 2.3 %quantize_more.3 = (bf16[7,64,1280]{2,1,0:T(8,128)(2,1)S(1)}, bf16[7,64,1280]{2,1,0:T(8,128)(2,1)S(1)}) custom-call(bf16[768,2048]{1,0:T(8,128)(2,1)S(1)} %get-tuple-element.46.act, bf16[768,1280]{1,0:T(8,128)(2,1)S(1)} %get-tuple-element.47.rotated, s32[5,2048]{1,0:T(8,128)S(1)} %get-tuple-element.48.exps.refs_7_, bf16[3,64,1280]{2,1,0:T(8,128)(2,1)S(1)} %get-tuple-element.51._), custom_call_target="tpu_custom_call" | custom-call | flops 1 | bytes 1 | tf_op jit(solution)/shard_map/quantize_more/pallas_call | solution.py:172
  10.2 1.3 %collective-permute-start.3 = (bf16[3,64,1280]{2,1,0:T(8,128)(2,1)S(1)}, bf16[3,64,1280]{2,1,0:T(8,128)(2,1)S(1)}, u32[]{:S(2)}, u32[]{:S(2)}) collective-permute-start(bf16[3,64,1280]{2,1,0:T(8,128)(2,1)S(1)} %get-tuple-element.56), channel_id=1, source_target_pairs={{0,16},{8,24},{16,32},{24,40},{32,48},{40,56},{48,0},{56,8},{64,80... | collective-permute-start | bytes 1474568 | tf_op jit(solution)/shard_map/ppermute | solution.py:60
  11.5 1.5 %collective-permute-start.4 = (bf16[3,64,1280]{2,1,0:T(8,128)(2,1)S(1)}, bf16[3,64,1280]{2,1,0:T(8,128)(2,1)S(1)}, u32[]{:S(2)}, u32[]{:S(2)}) collective-permute-start(bf16[3,64,1280]{2,1,0:T(8,128)(2,1)S(1)} %get-tuple-element.57), channel_id=1, source_target_pairs={{0,48},{8,56},{16,0},{24,8},{32,16},{40,24},{48,32},{56,40},{64,11... | collective-permute-start | bytes 1474568 | tf_op jit(solution)/shard_map/ppermute | solution.py:60
  13.4 4.3 %collective-permute-start.5 = (bf16[64,1280]{1,0:T(8,128)(2,1)S(1)}, bf16[64,1280]{1,0:T(8,128)(2,1)S(1)}, u32[]{:S(2)}, u32[]{:S(2)}) collective-permute-start(bf16[64,1280]{1,0:T(8,128)(2,1)S(1)} %get-tuple-element.58), channel_id=1, source_target_pairs={{0,64},{8,72},{16,80},{24,88},{32,96},{40,104},{48,112},{56,120},{... | collective-permute-start | bytes 491528 | tf_op jit(solution)/shard_map/ppermute | solution.py:60
  17.7 2.7 %collective-permute-start.7 = (bf16[64,1280]{1,0:T(8,128)(2,1)S(1)}, bf16[64,1280]{1,0:T(8,128)(2,1)S(1)}, u32[]{:S(2)}, u32[]{:S(2)}) collective-permute-start(bf16[64,1280]{1,0:T(8,128)(2,1)S(1)} %get-tuple-element.60), channel_id=1, source_target_pairs={{0,32},{8,40},{16,48},{24,56},{32,0},{40,8},{48,16},{56,24},{64,96... | collective-permute-start | bytes 491528 | tf_op jit(solution)/shard_map/ppermute | solution.py:60
  20.4 4.2 %collective-permute-done.5.below = bf16[64,1280]{1,0:T(8,128)(2,1)S(1)} collective-permute-done((bf16[64,1280]{1,0:T(8,128)(2,1)S(1)}, bf16[64,1280]{1,0:T(8,128)(2,1)S(1)}, u32[]{:S(2)}, u32[]{:S(2)}) %collective-permute-start.5) | collective-permute-done | bytes 163872 | tf_op jit(solution)/shard_map/ppermute | solution.py:60
  24.6 4.0 %collective-permute-done.6.above = bf16[64,1280]{1,0:T(8,128)(2,1)S(1)} collective-permute-done((bf16[64,1280]{1,0:T(8,128)(2,1)S(1)}, bf16[64,1280]{1,0:T(8,128)(2,1)S(1)}, u32[]{:S(2)}, u32[]{:S(2)}) %collective-permute-start.6) | collective-permute-done | bytes 163872 | tf_op jit(solution)/shard_map/ppermute | solution.py:60
  29.1 4.3 %collective-permute-start.8 = (bf16[64,1280]{1,0:T(8,128)(2,1)S(1)}, bf16[64,1280]{1,0:T(8,128)(2,1)S(1)}, u32[]{:S(2)}, u32[]{:S(2)}) collective-permute-start(bf16[64,1280]{1,0:T(8,128)(2,1)S(1)} %get-tuple-element.62), channel_id=1, source_target_pairs={{0,64},{8,72},{16,80},{24,88},{32,96},{40,104},{48,112},{56,120},{... | collective-permute-start | bytes 491528 | tf_op jit(solution)/shard_map/ppermute | solution.py:60
  33.4 3.3 %collective-permute-start.10 = (bf16[64,1280]{1,0:T(8,128)(2,1)S(1)}, bf16[64,1280]{1,0:T(8,128)(2,1)S(1)}, u32[]{:S(2)}, u32[]{:S(2)}) collective-permute-start(bf16[64,1280]{1,0:T(8,128)(2,1)S(1)} %get-tuple-element.64), channel_id=1, source_target_pairs={{0,128},{8,136},{16,144},{24,152},{32,160},{40,168},{48,176},{56,1... | collective-permute-start | bytes 491528 | tf_op jit(solution)/shard_map/ppermute | solution.py:60
  37.2 1.2 %collective-permute-start.12 = (bf16[64,1280]{1,0:T(8,128)(2,1)S(1)}, bf16[64,1280]{1,0:T(8,128)(2,1)S(1)}, u32[]{:S(2)}, u32[]{:S(2)}) collective-permute-start(bf16[64,1280]{1,0:T(8,128)(2,1)S(1)} %get-tuple-element.66), channel_id=1, source_target_pairs={{0,16},{8,24},{16,32},{24,40},{32,48},{40,56},{48,0},{56,8},{64,80... | collective-permute-start | bytes 491528 | tf_op jit(solution)/shard_map/ppermute | solution.py:60
  38.4 1.6 %collective-permute-done.8.refs_0_.refs_1_ = bf16[64,1280]{1,0:T(8,128)(2,1)S(1)} collective-permute-done((bf16[64,1280]{1,0:T(8,128)(2,1)S(1)}, bf16[64,1280]{1,0:T(8,128)(2,1)S(1)}, u32[]{:S(2)}, u32[]{:S(2)}) %collective-permute-start.8) | collective-permute-done | bytes 163872 | tf_op jit(solution)/shard_map/ppermute | solution.py:60
  39.9 5.0 %collective-permute-done.9.refs_1_.refs_2_ = bf16[64,1280]{1,0:T(8,128)(2,1)S(1)} collective-permute-done((bf16[64,1280]{1,0:T(8,128)(2,1)S(1)}, bf16[64,1280]{1,0:T(8,128)(2,1)S(1)}, u32[]{:S(2)}, u32[]{:S(2)}) %collective-permute-start.9) | collective-permute-done | bytes 163872 | tf_op jit(solution)/shard_map/ppermute | solution.py:60
  45.0 2.5 %collective-permute-done.10.refs_0_.refs_3_ = bf16[64,1280]{1,0:T(8,128)(2,1)S(1)} collective-permute-done((bf16[64,1280]{1,0:T(8,128)(2,1)S(1)}, bf16[64,1280]{1,0:T(8,128)(2,1)S(1)}, u32[]{:S(2)}, u32[]{:S(2)}) %collective-permute-start.10) | collective-permute-done | bytes 163872 | tf_op jit(solution)/shard_map/ppermute | solution.py:60
  48.3 2.0 %collective-permute-start.18 = (bf16[64,1280]{1,0:T(8,128)(2,1)S(1)}, bf16[64,1280]{1,0:T(8,128)(2,1)S(1)}, u32[]{:S(2)}, u32[]{:S(2)}) collective-permute-start(bf16[64,1280]{1,0:T(8,128)(2,1)S(1)} %get-tuple-element.70.w), channel_id=1, source_target_pairs={{0,192},{8,200},{16,208},{24,216},{32,224},{40,232},{48,240},{56,2... | collective-permute-start | bytes 491528 | tf_op jit(solution)/shard_map/ppermute | solution.py:60
  50.3 2.4 %collective-permute-start.19 = (bf16[64,1280]{1,0:T(8,128)(2,1)S(1)}, bf16[64,1280]{1,0:T(8,128)(2,1)S(1)}, u32[]{:S(2)}, u32[]{:S(2)}) collective-permute-start(bf16[64,1280]{1,0:T(8,128)(2,1)S(1)} %get-tuple-element.70.w), channel_id=1, source_target_pairs={{0,64},{8,72},{16,80},{24,88},{32,96},{40,104},{48,112},{56,120},{... | collective-permute-start | bytes 491528 | tf_op jit(solution)/shard_map/ppermute | solution.py:60
  53.4 3.1 %collective-permute-start.17 = (bf16[64,1280]{1,0:T(8,128)(2,1)S(1)}, bf16[64,1280]{1,0:T(8,128)(2,1)S(1)}, u32[]{:S(2)}, u32[]{:S(2)}) collective-permute-start(bf16[64,1280]{1,0:T(8,128)(2,1)S(1)} %get-tuple-element.70.w), channel_id=1, source_target_pairs={{0,128},{8,136},{16,144},{24,152},{32,160},{40,168},{48,176},{56,1... | collective-permute-start | bytes 491528 | tf_op jit(solution)/shard_map/ppermute | solution.py:60
  56.5 1.2 %collective-permute-start.14 = (bf16[64,1280]{1,0:T(8,128)(2,1)S(1)}, bf16[64,1280]{1,0:T(8,128)(2,1)S(1)}, u32[]{:S(2)}, u32[]{:S(2)}) collective-permute-start(bf16[64,1280]{1,0:T(8,128)(2,1)S(1)} %get-tuple-element.70.w), channel_id=1, source_target_pairs={{0,48},{8,56},{16,0},{24,8},{32,16},{40,24},{48,32},{56,40},{64,11... | collective-permute-start | bytes 491528 | tf_op jit(solution)/shard_map/ppermute | solution.py:60
  58.4 10.7 %collective-permute-done.17.refs_0_.z2 = bf16[64,1280]{1,0:T(8,128)(2,1)S(1)} collective-permute-done((bf16[64,1280]{1,0:T(8,128)(2,1)S(1)}, bf16[64,1280]{1,0:T(8,128)(2,1)S(1)}, u32[]{:S(2)}, u32[]{:S(2)}) %collective-permute-start.17) | collective-permute-done | bytes 163872 | tf_op jit(solution)/shard_map/ppermute | solution.py:60
  69.2 8.2 %collective-permute-start.20 = (bf16[7,64,1280]{2,1,0:T(8,128)(2,1)S(1)}, bf16[7,64,1280]{2,1,0:T(8,128)(2,1)S(1)}, u32[]{:S(2)}, u32[]{:S(2)}) collective-permute-start(bf16[7,64,1280]{2,1,0:T(8,128)(2,1)S(1)} %get-tuple-element.71.refs_0_), channel_id=1, source_target_pairs={{0,8},{8,0},{16,24},{24,16},{32,40},{40,32},{48,56},{56,48},{64,72... | collective-permute-start | bytes 3440648 | tf_op jit(solution)/shard_map/ppermute | solution.py:60
  77.4 1.5 %collective-permute-start.25 = (bf16[3,64,1280]{2,1,0:T(8,128)(2,1)S(1)}, bf16[3,64,1280]{2,1,0:T(8,128)(2,1)S(1)}, u32[]{:S(2)}, u32[]{:S(2)}) collective-permute-start(bf16[3,64,1280]{2,1,0:T(8,128)(2,1)S(1)} %get-tuple-element.82), channel_id=1, source_target_pairs={{0,16},{8,24},{16,32},{24,40},{32,48},{40,56},{48,0},{56,8},{64,80... | collective-permute-start | bytes 1474568 | tf_op jit(solution)/shard_map/ppermute | solution.py:60
  78.9 0.9 collective-permute-done.20.refs_1_
  79.9 2.6 %collective-permute-start.23 = (bf16[64,1280]{1,0:T(8,128)(2,1)S(1)}, bf16[64,1280]{1,0:T(8,128)(2,1)S(1)}, u32[]{:S(2)}, u32[]{:S(2)}) collective-permute-start(bf16[64,1280]{1,0:T(8,128)(2,1)S(1)} %get-tuple-element.81), channel_id=1, source_target_pairs={{0,64},{8,72},{16,80},{24,88},{32,96},{40,104},{48,112},{56,120},{... | collective-permute-start | bytes 491528 | tf_op jit(solution)/shard_map/ppermute | solution.py:60
  82.5 2.0 %place.3 = (bf16[2048,1280]{1,0:T(8,128)(2,1)}, f32[64,1280]{1,0:T(8,128)}, f32[64,1280]{1,0:T(8,128)}, f32[64,1280]{1,0:T(8,128)}, f32[64,1280]{1,0:T(8,128)}, /*index=5*/bf16[16,128]{1,0:T(8,128)(2,1)S(1)}) custom-call(bf16[7,64,1280]{2,1,0:T(8,128)(2,1)S(1)} %get-tuple-element.71.refs_0_, bf16[7,64,1280]{2,1,0:T(8,128)(2,1)S(1)} %collective-permute-done.20.refs_1_, ...), custom_call_target="tpu_custom_call" | custom-call | flops 1 | bytes 1 | tf_op jit(solution)/shard_map/place/pallas_call | solution.py:396
  84.5 8.4 %collective-permute-done.21.refs_0_ = bf16[64,1280]{1,0:T(8,128)(2,1)S(1)} collective-permute-done((bf16[64,1280]{1,0:T(8,128)(2,1)S(1)}, bf16[64,1280]{1,0:T(8,128)(2,1)S(1)}, u32[]{:S(2)}, u32[]{:S(2)}) %collective-permute-start.21) | collective-permute-done | bytes 163872 | tf_op jit(solution)/shard_map/ppermute | solution.py:60
  92.9 1.9 %collective-permute-done.25.refs_4_ = bf16[3,64,1280]{2,1,0:T(8,128)(2,1)S(1)} collective-permute-done((bf16[3,64,1280]{2,1,0:T(8,128)(2,1)S(1)}, bf16[3,64,1280]{2,1,0:T(8,128)(2,1)S(1)}, u32[]{:S(2)}, u32[]{:S(2)}) %collective-permute-start.25) | collective-permute-done | bytes 491552 | tf_op jit(solution)/shard_map/ppermute | solution.py:60
  94.9 1.1 %collective-permute-start.26 = (bf16[9,64,1280]{2,1,0:T(8,128)(2,1)S(1)}, bf16[9,64,1280]{2,1,0:T(8,128)(2,1)S(1)}, u32[]{:S(2)}, u32[]{:S(2)}) collective-permute-start(bf16[9,64,1280]{2,1,0:T(8,128)(2,1)S(1)} %join.1.refs_0_), channel_id=1, source_target_pairs={{0,8},{8,0},{16,24},{24,16},{32,40},{40,32},{48,56},{56,48},{64,72... | collective-permute-start | bytes 4423688 | tf_op jit(solution)/shard_map/ppermute | solution.py:60
  96.0 1.8 %place.4 = (bf16[2048,1280]{1,0:T(8,128)(2,1)}, bf16[16,128]{1,0:T(8,128)(2,1)}) custom-call(bf16[9,64,1280]{2,1,0:T(8,128)(2,1)S(1)} %join.1.refs_0_, bf16[2048,1280]{1,0:T(8,128)(2,1)} %get-tuple-element.84.refs_1_), custom_call_target="tpu_custom_call", output_to_operand_aliasing={{0}: (1, {})} | custom-call | flops 1 | bytes 1 | tf_op jit(solution)/shard_map/place/pallas_call | solution.py:396
  97.8 1.1 %collective-permute-done.26.refs_0_ = bf16[9,64,1280]{2,1,0:T(8,128)(2,1)S(1)} collective-permute-done((bf16[9,64,1280]{2,1,0:T(8,128)(2,1)S(1)}, bf16[9,64,1280]{2,1,0:T(8,128)(2,1)S(1)}, u32[]{:S(2)}, u32[]{:S(2)}) %collective-permute-start.26) | collective-permute-done | bytes 1474592 | tf_op jit(solution)/shard_map/ppermute | solution.py:60
  98.9 1.8 %place.5 = (bf16[2048,1280]{1,0:T(8,128)(2,1)}, bf16[16,128]{1,0:T(8,128)(2,1)}) custom-call(bf16[9,64,1280]{2,1,0:T(8,128)(2,1)S(1)} %collective-permute-done.26.refs_0_, bf16[2048,1280]{1,0:T(8,128)(2,1)} %get-tuple-element.85.refs_1_), custom_call_target="tpu_custom_call", output_to_operand_aliasing={{0}: (1, {})} | custom-call | flops 1 | bytes 1 | tf_op jit(solution)/shard_map/place/pallas_call | solution.py:396
  (44 shorter events, 4.6 us)
Async XLA Ops:
  5.3 4.7 %collective-permute-start.2 = (bf16[6,64,1280]{2,1,0:T(8,128)(2,1)S(1)}, bf16[6,64,1280]{2,1,0:T(8,128)(2,1)S(1)}, u32[]{:S(2)}, u32[]{:S(2)}) collective-permute-start(bf16[6,64,1280]{2,1,0:T(8,128)(2,1)S(1)} %get-tuple-element.49._), channel_id=1, source_target_pairs={{0,8},{8,0},{16,24},{24,16},{32,40},{40,32},{48,56},{56,48},{64,72... | collective-permute-start | bytes 2949128 | tf_op jit(solution)/shard_map/ppermute | solution.py:60
  9.4 3.6 %collective-permute-start.1 = (bf16[7,64,1280]{2,1,0:T(8,128)(2,1)S(1)}, bf16[7,64,1280]{2,1,0:T(8,128)(2,1)S(1)}, u32[]{:S(2)}, u32[]{:S(2)}) collective-permute-start(bf16[7,64,1280]{2,1,0:T(8,128)(2,1)S(1)} %get-tuple-element.53), channel_id=1, source_target_pairs={{0,8},{8,0},{16,24},{24,16},{32,40},{40,32},{48,56},{56,48},{64,72... | collective-permute-start | bytes 3440648 | tf_op jit(solution)/shard_map/ppermute | solution.py:60
  9.5 3.5 %collective-permute-start = (bf16[3,64,1280]{2,1,0:T(8,128)(2,1)S(1)}, bf16[3,64,1280]{2,1,0:T(8,128)(2,1)S(1)}, u32[]{:S(2)}, u32[]{:S(2)}) collective-permute-start(bf16[3,64,1280]{2,1,0:T(8,128)(2,1)S(1)} %get-tuple-element.51._), channel_id=1, source_target_pairs={{0,8},{8,0},{16,24},{24,16},{32,40},{40,32},{48,56},{56,48},{64,72... | collective-permute-start | bytes 1474568 | tf_op jit(solution)/shard_map/ppermute | solution.py:60
  10.2 18.5 %collective-permute-start.3 = (bf16[3,64,1280]{2,1,0:T(8,128)(2,1)S(1)}, bf16[3,64,1280]{2,1,0:T(8,128)(2,1)S(1)}, u32[]{:S(2)}, u32[]{:S(2)}) collective-permute-start(bf16[3,64,1280]{2,1,0:T(8,128)(2,1)S(1)} %get-tuple-element.56), channel_id=1, source_target_pairs={{0,16},{8,24},{16,32},{24,40},{32,48},{40,56},{48,0},{56,8},{64,80... | collective-permute-start | bytes 1474568 | tf_op jit(solution)/shard_map/ppermute | solution.py:60
  11.5 17.3 %collective-permute-start.4 = (bf16[3,64,1280]{2,1,0:T(8,128)(2,1)S(1)}, bf16[3,64,1280]{2,1,0:T(8,128)(2,1)S(1)}, u32[]{:S(2)}, u32[]{:S(2)}) collective-permute-start(bf16[3,64,1280]{2,1,0:T(8,128)(2,1)S(1)} %get-tuple-element.57), channel_id=1, source_target_pairs={{0,48},{8,56},{16,0},{24,8},{32,16},{40,24},{48,32},{56,40},{64,11... | collective-permute-start | bytes 1474568 | tf_op jit(solution)/shard_map/ppermute | solution.py:60
  13.4 11.2 %collective-permute-start.5 = (bf16[64,1280]{1,0:T(8,128)(2,1)S(1)}, bf16[64,1280]{1,0:T(8,128)(2,1)S(1)}, u32[]{:S(2)}, u32[]{:S(2)}) collective-permute-start(bf16[64,1280]{1,0:T(8,128)(2,1)S(1)} %get-tuple-element.58), channel_id=1, source_target_pairs={{0,64},{8,72},{16,80},{24,88},{32,96},{40,104},{48,112},{56,120},{... | collective-permute-start | bytes 491528 | tf_op jit(solution)/shard_map/ppermute | solution.py:60
  17.7 10.9 %collective-permute-start.6 = (bf16[64,1280]{1,0:T(8,128)(2,1)S(1)}, bf16[64,1280]{1,0:T(8,128)(2,1)S(1)}, u32[]{:S(2)}, u32[]{:S(2)}) collective-permute-start(bf16[64,1280]{1,0:T(8,128)(2,1)S(1)} %get-tuple-element.59), channel_id=1, source_target_pairs={{0,192},{8,200},{16,208},{24,216},{32,224},{40,232},{48,240},{56,2... | collective-permute-start | bytes 491528 | tf_op jit(solution)/shard_map/ppermute | solution.py:60
  17.7 11.1 %collective-permute-start.7 = (bf16[64,1280]{1,0:T(8,128)(2,1)S(1)}, bf16[64,1280]{1,0:T(8,128)(2,1)S(1)}, u32[]{:S(2)}, u32[]{:S(2)}) collective-permute-start(bf16[64,1280]{1,0:T(8,128)(2,1)S(1)} %get-tuple-element.60), channel_id=1, source_target_pairs={{0,32},{8,40},{16,48},{24,56},{32,0},{40,8},{48,16},{56,24},{64,96... | collective-permute-start | bytes 491528 | tf_op jit(solution)/shard_map/ppermute | solution.py:60
  28.8 18.8 %copy-start = (f32[64,1280]{1,0:T(8,128)S(1)}, f32[64,1280]{1,0:T(8,128)}, u32[]{:S(2)}) copy-start(f32[64,1280]{1,0:T(8,128)} %refs_10_.1) | copy-start | bytes 983044
  28.8 18.8 %copy-start.1 = (f32[64,1280]{1,0:T(8,128)S(1)}, f32[64,1280]{1,0:T(8,128)}, u32[]{:S(2)}) copy-start(f32[64,1280]{1,0:T(8,128)} %refs_11_.1) | copy-start | bytes 983044
  28.8 18.8 %copy-start.2 = (f32[64,1280]{1,0:T(8,128)S(1)}, f32[64,1280]{1,0:T(8,128)}, u32[]{:S(2)}) copy-start(f32[64,1280]{1,0:T(8,128)} %refs_12_.1) | copy-start | bytes 983044
  29.1 10.8 %collective-permute-start.8 = (bf16[64,1280]{1,0:T(8,128)(2,1)S(1)}, bf16[64,1280]{1,0:T(8,128)(2,1)S(1)}, u32[]{:S(2)}, u32[]{:S(2)}) collective-permute-start(bf16[64,1280]{1,0:T(8,128)(2,1)S(1)} %get-tuple-element.62), channel_id=1, source_target_pairs={{0,64},{8,72},{16,80},{24,88},{32,96},{40,104},{48,112},{56,120},{... | collective-permute-start | bytes 491528 | tf_op jit(solution)/shard_map/ppermute | solution.py:60
  33.4 11.6 %collective-permute-start.9 = (bf16[64,1280]{1,0:T(8,128)(2,1)S(1)}, bf16[64,1280]{1,0:T(8,128)(2,1)S(1)}, u32[]{:S(2)}, u32[]{:S(2)}) collective-permute-start(bf16[64,1280]{1,0:T(8,128)(2,1)S(1)} %get-tuple-element.63), channel_id=1, source_target_pairs={{0,192},{8,200},{16,208},{24,216},{32,224},{40,232},{48,240},{56,2... | collective-permute-start | bytes 491528 | tf_op jit(solution)/shard_map/ppermute | solution.py:60
  33.4 14.1 %collective-permute-start.10 = (bf16[64,1280]{1,0:T(8,128)(2,1)S(1)}, bf16[64,1280]{1,0:T(8,128)(2,1)S(1)}, u32[]{:S(2)}, u32[]{:S(2)}) collective-permute-start(bf16[64,1280]{1,0:T(8,128)(2,1)S(1)} %get-tuple-element.64), channel_id=1, source_target_pairs={{0,128},{8,136},{16,144},{24,152},{32,160},{40,168},{48,176},{56,1... | collective-permute-start | bytes 491528 | tf_op jit(solution)/shard_map/ppermute | solution.py:60
  36.6 10.9 %collective-permute-start.11 = (bf16[64,1280]{1,0:T(8,128)(2,1)S(1)}, bf16[64,1280]{1,0:T(8,128)(2,1)S(1)}, u32[]{:S(2)}, u32[]{:S(2)}) collective-permute-start(bf16[64,1280]{1,0:T(8,128)(2,1)S(1)} %get-tuple-element.65), channel_id=1, source_target_pairs={{0,32},{8,40},{16,48},{24,56},{32,0},{40,8},{48,16},{56,24},{64,96... | collective-permute-start | bytes 491528 | tf_op jit(solution)/shard_map/ppermute | solution.py:60
  37.2 10.3 %collective-permute-start.12 = (bf16[64,1280]{1,0:T(8,128)(2,1)S(1)}, bf16[64,1280]{1,0:T(8,128)(2,1)S(1)}, u32[]{:S(2)}, u32[]{:S(2)}) collective-permute-start(bf16[64,1280]{1,0:T(8,128)(2,1)S(1)} %get-tuple-element.66), channel_id=1, source_target_pairs={{0,16},{8,24},{16,32},{24,40},{32,48},{40,56},{48,0},{56,8},{64,80... | collective-permute-start | bytes 491528 | tf_op jit(solution)/shard_map/ppermute | solution.py:60
  39.9 7.6 %collective-permute-start.13 = (bf16[64,1280]{1,0:T(8,128)(2,1)S(1)}, bf16[64,1280]{1,0:T(8,128)(2,1)S(1)}, u32[]{:S(2)}, u32[]{:S(2)}) collective-permute-start(bf16[64,1280]{1,0:T(8,128)(2,1)S(1)} %get-tuple-element.67), channel_id=1, source_target_pairs={{0,48},{8,56},{16,0},{24,8},{32,16},{40,24},{48,32},{56,40},{64,11... | collective-permute-start | bytes 491528 | tf_op jit(solution)/shard_map/ppermute | solution.py:60
  48.3 9.5 %collective-permute-start.18 = (bf16[64,1280]{1,0:T(8,128)(2,1)S(1)}, bf16[64,1280]{1,0:T(8,128)(2,1)S(1)}, u32[]{:S(2)}, u32[]{:S(2)}) collective-permute-start(bf16[64,1280]{1,0:T(8,128)(2,1)S(1)} %get-tuple-element.70.w), channel_id=1, source_target_pairs={{0,192},{8,200},{16,208},{24,216},{32,224},{40,232},{48,240},{56,2... | collective-permute-start | bytes 491528 | tf_op jit(solution)/shard_map/ppermute | solution.py:60
  50.3 7.7 %collective-permute-start.19 = (bf16[64,1280]{1,0:T(8,128)(2,1)S(1)}, bf16[64,1280]{1,0:T(8,128)(2,1)S(1)}, u32[]{:S(2)}, u32[]{:S(2)}) collective-permute-start(bf16[64,1280]{1,0:T(8,128)(2,1)S(1)} %get-tuple-element.70.w), channel_id=1, source_target_pairs={{0,64},{8,72},{16,80},{24,88},{32,96},{40,104},{48,112},{56,120},{... | collective-permute-start | bytes 491528 | tf_op jit(solution)/shard_map/ppermute | solution.py:60
  52.7 5.7 %collective-permute-start.16 = (bf16[64,1280]{1,0:T(8,128)(2,1)S(1)}, bf16[64,1280]{1,0:T(8,128)(2,1)S(1)}, u32[]{:S(2)}, u32[]{:S(2)}) collective-permute-start(bf16[64,1280]{1,0:T(8,128)(2,1)S(1)} %get-tuple-element.70.w), channel_id=1, source_target_pairs={{0,32},{8,40},{16,48},{24,56},{32,0},{40,8},{48,16},{56,24},{64,96... | collective-permute-start | bytes 491528 | tf_op jit(solution)/shard_map/ppermute | solution.py:60
  53.4 15.6 %collective-permute-start.17 = (bf16[64,1280]{1,0:T(8,128)(2,1)S(1)}, bf16[64,1280]{1,0:T(8,128)(2,1)S(1)}, u32[]{:S(2)}, u32[]{:S(2)}) collective-permute-start(bf16[64,1280]{1,0:T(8,128)(2,1)S(1)} %get-tuple-element.70.w), channel_id=1, source_target_pairs={{0,128},{8,136},{16,144},{24,152},{32,160},{40,168},{48,176},{56,1... | collective-permute-start | bytes 491528 | tf_op jit(solution)/shard_map/ppermute | solution.py:60
  56.5 12.5 %collective-permute-start.14 = (bf16[64,1280]{1,0:T(8,128)(2,1)S(1)}, bf16[64,1280]{1,0:T(8,128)(2,1)S(1)}, u32[]{:S(2)}, u32[]{:S(2)}) collective-permute-start(bf16[64,1280]{1,0:T(8,128)(2,1)S(1)} %get-tuple-element.70.w), channel_id=1, source_target_pairs={{0,48},{8,56},{16,0},{24,8},{32,16},{40,24},{48,32},{56,40},{64,11... | collective-permute-start | bytes 491528 | tf_op jit(solution)/shard_map/ppermute | solution.py:60
  57.8 11.3 %collective-permute-start.15 = (bf16[64,1280]{1,0:T(8,128)(2,1)S(1)}, bf16[64,1280]{1,0:T(8,128)(2,1)S(1)}, u32[]{:S(2)}, u32[]{:S(2)}) collective-permute-start(bf16[64,1280]{1,0:T(8,128)(2,1)S(1)} %get-tuple-element.70.w), channel_id=1, source_target_pairs={{0,16},{8,24},{16,32},{24,40},{32,48},{40,56},{48,0},{56,8},{64,80... | collective-permute-start | bytes 491528 | tf_op jit(solution)/shard_map/ppermute | solution.py:60
  69.2 10.7 %collective-permute-start.20 = (bf16[7,64,1280]{2,1,0:T(8,128)(2,1)S(1)}, bf16[7,64,1280]{2,1,0:T(8,128)(2,1)S(1)}, u32[]{:S(2)}, u32[]{:S(2)}) collective-permute-start(bf16[7,64,1280]{2,1,0:T(8,128)(2,1)S(1)} %get-tuple-element.71.refs_0_), channel_id=1, source_target_pairs={{0,8},{8,0},{16,24},{24,16},{32,40},{40,32},{48,56},{56,48},{64,72... | collective-permute-start | bytes 3440648 | tf_op jit(solution)/shard_map/ppermute | solution.py:60
  77.4 15.4 %collective-permute-start.24 = (bf16[3,64,1280]{2,1,0:T(8,128)(2,1)S(1)}, bf16[3,64,1280]{2,1,0:T(8,128)(2,1)S(1)}, u32[]{:S(2)}, u32[]{:S(2)}) collective-permute-start(bf16[3,64,1280]{2,1,0:T(8,128)(2,1)S(1)} %get-tuple-element.82), channel_id=1, source_target_pairs={{0,48},{8,56},{16,0},{24,8},{32,16},{40,24},{48,32},{56,40},{64,11... | collective-permute-start | bytes 1474568 | tf_op jit(solution)/shard_map/ppermute | solution.py:60
  77.4 17.4 %collective-permute-start.25 = (bf16[3,64,1280]{2,1,0:T(8,128)(2,1)S(1)}, bf16[3,64,1280]{2,1,0:T(8,128)(2,1)S(1)}, u32[]{:S(2)}, u32[]{:S(2)}) collective-permute-start(bf16[3,64,1280]{2,1,0:T(8,128)(2,1)S(1)} %get-tuple-element.82), channel_id=1, source_target_pairs={{0,16},{8,24},{16,32},{24,40},{32,48},{40,56},{48,0},{56,8},{64,80... | collective-permute-start | bytes 1474568 | tf_op jit(solution)/shard_map/ppermute | solution.py:60
  78.9 13.9 %collective-permute-start.21 = (bf16[64,1280]{1,0:T(8,128)(2,1)S(1)}, bf16[64,1280]{1,0:T(8,128)(2,1)S(1)}, u32[]{:S(2)}, u32[]{:S(2)}) collective-permute-start(bf16[64,1280]{1,0:T(8,128)(2,1)S(1)} %get-tuple-element.80), channel_id=1, source_target_pairs={{0,32},{8,40},{16,48},{24,56},{32,0},{40,8},{48,16},{56,24},{64,96... | collective-permute-start | bytes 491528 | tf_op jit(solution)/shard_map/ppermute | solution.py:60
  78.9 13.9 %collective-permute-start.22 = (bf16[64,1280]{1,0:T(8,128)(2,1)S(1)}, bf16[64,1280]{1,0:T(8,128)(2,1)S(1)}, u32[]{:S(2)}, u32[]{:S(2)}) collective-permute-start(bf16[64,1280]{1,0:T(8,128)(2,1)S(1)} %get-tuple-element.81), channel_id=1, source_target_pairs={{0,192},{8,200},{16,208},{24,216},{32,224},{40,232},{48,240},{56,2... | collective-permute-start | bytes 491528 | tf_op jit(solution)/shard_map/ppermute | solution.py:60
  79.9 13.0 %collective-permute-start.23 = (bf16[64,1280]{1,0:T(8,128)(2,1)S(1)}, bf16[64,1280]{1,0:T(8,128)(2,1)S(1)}, u32[]{:S(2)}, u32[]{:S(2)}) collective-permute-start(bf16[64,1280]{1,0:T(8,128)(2,1)S(1)} %get-tuple-element.81), channel_id=1, source_target_pairs={{0,64},{8,72},{16,80},{24,88},{32,96},{40,104},{48,112},{56,120},{... | collective-permute-start | bytes 491528 | tf_op jit(solution)/shard_map/ppermute | solution.py:60
  94.9 4.0 %collective-permute-start.26 = (bf16[9,64,1280]{2,1,0:T(8,128)(2,1)S(1)}, bf16[9,64,1280]{2,1,0:T(8,128)(2,1)S(1)}, u32[]{:S(2)}, u32[]{:S(2)}) collective-permute-start(bf16[9,64,1280]{2,1,0:T(8,128)(2,1)S(1)} %join.1.refs_0_), channel_id=1, source_target_pairs={{0,8},{8,0},{16,24},{24,16},{32,40},{40,32},{48,56},{56,48},{64,72... | collective-permute-start | bytes 4423688 | tf_op jit(solution)/shard_map/ppermute | solution.py:60

commit v4 on v3

--- a/solution.py
+++ b/solution.py
@@ -32,9 +32,9 @@
 HBM = pl.BlockSpec(memory_space=pltpu.HBM)
 FULL = pl.BlockSpec(memory_space=pltpu.VMEM)
 
-SIDES = ((1, 1), (3, 1), (1, 2), (3, 2), (1, 3), (3, 3))
-CORNERS = ((2, 1), (2, 3), (2, 2))
-REST = ((0, 1), (0, 2), (0, 3), (1, 0), (2, 0), (3, 0), (0, 0))
+FIRST_NAMES = ((0, 0), (0, "a"), (0, 2), (2, 0), ("a", 0), ("b", 0))
+LAST_NAMES = ((0, "b"), ("a", "b"), ("b", "b"), (2, "b"))
+LAST_NAMES += ((2, "a"), (2, 2), ("b", "a"), ("b", 2), ("a", "a"), ("a", 2))
 
 
 def hadamard_table(order):
@@ -46,13 +46,21 @@
     return np.where(parity % 2 == 0, 1.0, -1.0) / math.sqrt(order)
 
 
+def step(way, core):
+    if way == "a":
+        return 1 + 2 * core
+    if way == "b":
+        return 3 - 2 * core
+    return way
+
+
 def replica_perm(dx, dz, dc):
     pairs = []
     for z in range(NZ):
         for x in range(NX):
             for c in range(NC):
-                to = (((z + dz) % NZ) * NX + (x + dx) % NX) * NC + (c + dc) % NC
-                pairs.append(((z * NX + x) * NC + c, to))
+                z_to, x_to = (z + step(dz, c)) % NZ, (x + step(dx, c)) % NX
+                pairs.append(((z * NX + x) * NC + c, (z_to * NX + x_to) * NC + (c + dc) % NC))
     return pairs
 
 
@@ -84,7 +92,7 @@
     return pltpu.CompilerParams(vmem_limit_bytes=mib * MIB)
 
 
-def quant_group(dx, dz, act, rotated, exps, mine, theirs, k):
+def quant_group(dx, dz, act, rotated, exps, mine, theirs):
     zh, x, core = place_of()
     group = lax.rem(zh + dz, NZ) * NX + lax.rem(x + dx, NX)
     lanes = pl.ds(pl.multiple_of(group * GROUP, GROUP), GROUP)
@@ -96,8 +104,8 @@
         cut = slice(tile * TILE, (tile + 1) * TILE)
         part = jnp.clip(total[:, cut] * shrink[:, tile : tile + 1], -127.0, 127.0).astype(BF)
         top, bottom = part[:ROW], part[ROW:]
-        mine[k, :, cut] = jnp.where(core == 0, top, bottom)
-        theirs[k, :, cut] = jnp.where(core == 0, bottom, top)
+        mine[:, cut] = jnp.where(core == 0, top, bottom)
+        theirs[:, cut] = jnp.where(core == 0, bottom, top)
 
 
 def first_kernel(
@@ -132,19 +140,21 @@
             rotated[rows, cut] = turned.astype(BF)
     for copy in strips[3:]:
         copy.wait()
-    for k, (dx, dz) in enumerate(SIDES):
-        quant_group(dx, dz, act, rotated, exps, mine, theirs, k)
+    _, _, core = place_of()
+    for dx in range(NX):
+        here, there = mine.at[dx], theirs.at[NX + dx]
+        quant_group(dx, step("a", core), act, rotated, exps, here, there)
+        here, there = mine.at[NX + dx], theirs.at[dx]
+        quant_group(dx, step("b", core), act, rotated, exps, here, there)
 
 
 def quantized_first(act, grads, exps, signs, table):
-    n = len(SIDES)
     return pl.pallas_call(
         first_kernel,
         in_specs=[HBM] * 5,
         out_specs=[FULL] * 7,
-        out_shape=[
-            vmem(n, ROW, COLS),
-            vmem(n, ROW, COLS),
+        out_shape=[vmem(2 * NX, ROW, COLS)] * 2
+        + [
             vmem(TOK, ROWS),
             vmem(TOK, COLS),
             vmem(TILES, ROWS, dtype=jnp.int32),
@@ -158,25 +168,24 @@
         ],
         compiler_params=params(12),
         cost_estimate=TINY,
-        name="quantize_sides",
+        name="quantize_first",
     )(*far(act, grads, exps, signs, table))
 
 
-def next_kernel(blocks, act, rotated, exps, _, mine, theirs):
-    for k, (dx, dz) in enumerate(blocks):
-        quant_group(dx, dz, act, rotated, exps, mine, theirs, k)
-
-
-def quantized_next(blocks, act, rotated, exps, after):
-    n = len(blocks)
-    return pl.pallas_call(
-        functools.partial(next_kernel, blocks),
+def next_kernel(dz, act, rotated, exps, _, mine, theirs):
+    for dx in range(NX):
+        quant_group(dx, dz, act, rotated, exps, mine.at[dx], theirs.at[dx])
+
+
+def quantized_next(dz, act, rotated, exps, after):
+    return pl.pallas_call(
+        functools.partial(next_kernel, dz),
         in_specs=[FULL] * 4,
         out_specs=[FULL] * 2,
-        out_shape=[vmem(n, ROW, COLS)] * 2,
+        out_shape=[vmem(NX, ROW, COLS)] * 2,
         compiler_params=params(8),
         cost_estimate=TINY,
-        name="quantize_more",
+        name="quantize_next",
     )(*held(act, rotated, exps, after))
 
 
@@ -187,60 +196,63 @@
     return total.astype(BF)
 
 
-def sides_kernel(mine, other, _b, _c, right, left):
-    for k, (dx, dz) in enumerate(SIDES):
-        out = right if dx == 1 else left
-        out[dz - 1] = add(mine[k], other[k])
-
-
-def sides_sum(mine, other, *after):
+def row_kernel(mine, other, _, out):
+    for k in range(NX):
+        out[k] = add(mine[k], other[k])
+
+
+def row_sum(mine, other, after):
+    return pl.pallas_call(
+        row_kernel,
+        in_specs=[FULL] * 3,
+        out_specs=FULL,
+        out_shape=vmem(NX, ROW, COLS),
+        compiler_params=params(2),
+        cost_estimate=TINY,
+        name="row_sum",
+    )(*held(mine, other, after))
+
+
+def sides_kernel(mine, other, mine_2, other_2, mine_0, other_0, xa, xb, x2, pairs):
+    _, _, core = place_of()
+    a, b = step("a", core), step("b", core)
+    for k, out in ((a, xa), (b, xb), (2, x2)):
+        out[0] = add(mine[NX + k], other[NX + k])
+        out[1] = add(mine_2[k], other_2[k])
+    pairs[0] = add(mine[NX], other[NX])
+    pairs[1] = add(mine_2[0], other_2[0])
+    for k, way in enumerate((a, b, 2, 0)):
+        pairs[2 + k] = add(mine_0[way], other_0[way])
+
+
+def sides_sum(*parts):
     return pl.pallas_call(
         sides_kernel,
-        in_specs=[FULL] * 4,
-        out_specs=[FULL] * 2,
-        out_shape=[vmem(NZ - 1, ROW, COLS)] * 2,
+        in_specs=[FULL] * 6,
+        out_specs=[FULL] * 4,
+        out_shape=[vmem(2, ROW, COLS)] * 3 + [vmem(6, ROW, COLS)],
         compiler_params=params(4),
         cost_estimate=TINY,
         name="sides_sum",
-    )(*held(mine, other, *after))
-
-
-def corners_kernel(mine, other, mine_rest, other_rest, *outs):
-    for k, out in enumerate(outs[:3]):
-        out[...] = add(mine[k], other[k])
-    for k in range(len(REST)):
-        outs[3][k] = add(mine_rest[k], other_rest[k])
-
-
-def corners_sum(*parts):
-    return pl.pallas_call(
-        corners_kernel,
-        in_specs=[FULL] * 4,
-        out_specs=[FULL] * 4,
-        out_shape=[vmem(ROW, COLS)] * 3 + [vmem(len(REST), ROW, COLS)],
-        compiler_params=params(4),
-        cost_estimate=TINY,
-        name="corners_sum",
     )(*held(*parts))
 
 
-def middle_kernel(pairs, left, right, below, above, across, *outs):
-    z1, z2, z3, x1, x2, x3, own = outs
-    for k, out in enumerate((z1, z2, z3)):
-        more = (across[...],) if k == 1 else ()
-        out[...] = add(pairs[k], left[k], right[k], *more)
-    x1[...] = pairs[3]
-    x2[...] = add(pairs[4], below[...], above[...])
-    x3[...] = pairs[5]
-    own[...] = pairs[6]
+def middle_kernel(pairs, xa, xb, x2, row, *outs):
+    zb_out, z2_out, xa_out, xb_out, x2_out, own_out = outs
+    _, _, core = place_of()
+    for k, out in enumerate((zb_out, z2_out)):
+        out[...] = add(pairs[k], xa[k], xb[k], x2[k])
+    ways = (step("a", core), step("b", core), 2, 0)
+    for k, out in enumerate((xa_out, xb_out, x2_out, own_out)):
+        out[...] = add(pairs[2 + k], row[ways[k]])
 
 
 def middle_sum(*parts):
     return pl.pallas_call(
         middle_kernel,
-        in_specs=[FULL] * 6,
-        out_specs=[FULL] * 7,
-        out_shape=[vmem(ROW, COLS)] * 7,
+        in_specs=[FULL] * 5,
+        out_specs=[FULL] * 6,
+        out_shape=[vmem(ROW, COLS)] * 6,
         compiler_params=params(4),
         cost_estimate=TINY,
         name="middle_sum",
@@ -264,9 +276,9 @@
 
 
 def update_kernel(*refs):
-    parts = refs[0:7]
-    exps, signs, table, master, moment, second = refs[7:13]
-    grad_out, moment_out, second_out, master_out, weights_out = refs[14:19]
+    parts = refs[0:6]
+    exps, signs, table, master, moment, second = refs[6:12]
+    grad_out, moment_out, second_out, master_out, weights_out = refs[13:18]
     zh, x, core = place_of()
     lanes = pl.ds(pl.multiple_of((zh * NX + x) * GROUP, GROUP), GROUP)
     growth = jnp.exp2(exps[:, lanes].astype(F32)).T
@@ -305,7 +317,7 @@
 def updated(parts, exps, signs, table, state, after):
     return pl.pallas_call(
         update_kernel,
-        in_specs=[FULL] * 14,
+        in_specs=[FULL] * 13,
         out_specs=[FULL] * 5,
         out_shape=[vmem(ROW, COLS, dtype=F32)] * 4 + [vmem(ROW, COLS)],
         compiler_params=params(4),
@@ -339,21 +351,21 @@
     )(*held(*parts, *after))
 
 
-def fan_kernel(w, x3, x1, x2, z2, z3, z1, _, column, row, corner, first):
-    for k, part in enumerate((z1, z3, z2)):
+def fan_kernel(w, xb, xa, x2, z2, za, _, column, row, first):
+    for k, part in enumerate((za, z2)):
         column[k] = part[...]
-    row[...] = x2[...]
-    corner[...] = z2[...]
-    for k, part in enumerate((w, z1, z3, z2, x2, x1, x3)):
+    for k, part in enumerate((w, xa, xb, x2)):
+        row[k] = part[...]
+    for k, part in enumerate((w, za, z2, x2, xa, xb)):
         first[k] = part[...]
 
 
 def fanned(*parts):
     return pl.pallas_call(
         fan_kernel,
-        in_specs=[FULL] * 8,
-        out_specs=[FULL] * 4,
-        out_shape=[vmem(3, ROW, COLS), vmem(ROW, COLS), vmem(ROW, COLS), vmem(7, ROW, COLS)],
+        in_specs=[FULL] * 7,
+        out_specs=[FULL] * 3,
+        out_shape=[vmem(2, ROW, COLS), vmem(4, ROW, COLS), vmem(6, ROW, COLS)],
         compiler_params=params(2),
         cost_estimate=TINY,
         name="fan",
@@ -373,8 +385,8 @@
     for flip, piece in zip(flips, pieces):
         row_core = 1 - core if flip else core
         for k, (dx, dz) in enumerate(names):
-            z_from = lax.rem(zh + NZ - dz, NZ)
-            x_from = lax.rem(x + NX - dx, NX)
+            z_from = lax.rem(zh + NZ - step(dz, row_core), NZ)
+            x_from = lax.rem(x + NX - step(dx, row_core), NX)
             row = pl.multiple_of(((z_from * NX + x_from) * NC + row_core) * ROW, ROW)
             copies.append(
                 pltpu.make_async_copy(
@@ -406,54 +418,41 @@
     )(*held(*pieces, *state), *((previous,) if chained else ()))
 
 
-def on_device(activations, out_grads, exponents, signs, master, moment, second):
+def on_device(activations, out_grads, exponents, signs, master, moment, second_moment):
     table = jnp.asarray(hadamard_table(TILE), BF)
-    mine_a, theirs_a, act, rotated, exps, sign_row, table = quantized_first(
+    mine, theirs, act, rotated, exps, sign_row, table = quantized_first(
         activations, out_grads, exponents.T, signs, table
     )
-    other_a = send(theirs_a, dc=1)
-    mine_b, theirs_b = quantized_next(CORNERS, act, rotated, exps, theirs_a)
-    other_b = send(theirs_b, dc=1)
-    mine_c, theirs_c = quantized_next(REST, act, rotated, exps, theirs_b)
-    other_c = send(theirs_c, dc=1)
-    right, left = sides_sum(mine_a, other_a, mine_b, mine_c)
-    from_left, from_right = send(right, dx=1), send(left, dx=3)
-    up, down, across, pairs = corners_sum(mine_b, other_b, mine_c, other_c)
-    from_below, from_above = send(up, dz=1), send(down, dz=3)
-    from_across = send(across, dx=2)
-    z1, z2, z3, x1, x2, x3, own = middle_sum(
-        pairs, from_left, from_right, from_below, from_above, from_across
-    )
-    parts = [
-        own,
-        send(z1, dz=1),
-        send(z3, dz=3),
-        send(z2, dz=2),
-        send(x2, dx=2),
-        send(x1, dx=1),
-        send(x3, dx=3),
-    ]
-    token = seen(parts[3], parts[4], seen(parts[1], parts[2]))
-    state = (master, moment, second)
+    other = send(theirs, dc=1)
+    mine_2, theirs_2 = quantized_next(2, act, rotated, exps, theirs)
+    other_2 = send(theirs_2, dc=1)
+    mine_0, theirs_0 = quantized_next(0, act, rotated, exps, theirs_2)
+    other_0 = send(theirs_0, dc=1)
+    row = send(row_sum(mine, other, mine_0), dz="a")
+    xa, xb, x2, pairs = sides_sum(mine, other, mine_2, other_2, mine_0, other_0)
+    xa, xb, x2 = send(xa, dx="a"), send(xb, dx="b"), send(x2, dx=2)
+    zb, z2, xa, xb, x2, own = middle_sum(pairs, xa, xb, x2, row)
+    zb, z2 = send(zb, dz="b"), send(z2, dz=2)
+    x2, xa, xb = send(x2, dx=2), send(xa, dx="a"), send(xb, dx="b")
+    parts = [own, zb, z2, x2, xa, xb]
+    token = seen(z2, zb)
+    state = (master, moment, second_moment)
     *state_new, w = updated(parts, exps, sign_row, table, state, token)
 
-    x3, x1, x2 = send(w, dx=3), send(w, dx=1), send(w, dx=2)
-    z2, z3, z1 = send(w, dz=2), send(w, dz=3), send(w, dz=1)
-    token = seen(z2, x2, seen(z1, z3))
-    column, row, corner, first = fanned(w, x3, x1, x2, z2, z3, z1, token)
+    za, z2 = send(w, dz="a"), send(w, dz=2)
+    x2, xa, xb = send(w, dx=2), send(w, dx="a"), send(w, dx="b")
+    token = seen(z2, za)
+    column, row, first = fanned(w, xb, xa, x2, z2, za, token)
     other_first = send(first, dc=1)
-    x2f = send(corner, dx=2)
-    z3f, z1f = send(row, dz=3), send(row, dz=1)
-    x3c, x1c = send(column, dx=3), send(column, dx=1)
-    names = ((0, 0), (0, 1), (0, 3), (0, 2), (2, 0), (1, 0), (3, 0))
+    zbr = send(row, dz="b")
+    xac, xbc, x2c = send(column, dx="a"), send(column, dx="b"), send(column, dx=2)
     weights, *state_new, token = placed(
-        names, (False, True), (first, other_first), state_new, None
-    )
-    last = joined(x2f, z3f, z1f, x3c, x1c, after=(token,))
-    names = ((2, 2), (2, 3), (2, 1), (3, 1), (3, 3), (3, 2), (1, 1), (1, 3), (1, 2))
+        FIRST_NAMES, (False, True), (first, other_first), state_new, None
+    )
+    last = joined(zbr, x2c, xbc, xac, after=(token,))
     other_last = send(last, dc=1)
-    weights, _ = placed(names, (False,), (last,), (), weights)
-    weights, _ = placed(names, (True,), (other_last,), (), weights)
+    weights, _ = placed(LAST_NAMES, (False,), (last,), (), weights)
+    weights, _ = placed(LAST_NAMES, (True,), (other_last,), (), weights)
     return (*state_new, weights)
 
 

time: 101 us -> 96.4 us (0.954)
  the two profiles are of different devices: /device:TPU:89 before, /device:TPU:1 now
where the time goes in v4:
time: 96.4 us; the launch traced here: 96.3 us
  waiting for transfers between devices  43.9 us (46%)
  starting transfers between devices  36 us (37%)
  Pallas kernels  15.4 us (16%)
    ppermute x23, waiting for transfers between devices, send(): return lax.ppermute(value, 'replica', replica_perm(dx, dz, dc))  43.9 us
    ppermute x23, starting transfers between devices, send(): return lax.ppermute(value, 'replica', replica_perm(dx, dz, dc))  36 us
    pallas_call x3, Pallas kernels, placed(): pl.pallas_call(functools.partial(place_kernel, names, flips, count, chain...  5.5 us
    pallas_call x1, Pallas kernels, quantized_first(): pl.pallas_call(first_kernel, in_specs=[HBM] * 5, out_specs=[FULL] * 7, ou...  5.24 us
    pallas_call x2, Pallas kernels, quantized_next(): pl.pallas_call(functools.partial(next_kernel, dz), in_specs=[FULL] * 4, o...  2.74 us
  transfers between devices with their start and end apart: 23, of which 9 were waited for; matrix products, arithmetic and copies ran while one was open for 0% of the time, Pallas kernels for 7%

profile of v4, /device:TPU:1, one launch (start us, length us, event | category | flops | bytes accessed | tf_op | source)
XLA Modules:
  0.0 96.3 jit_solution(16335210325687879734)
XLA Ops:
  0.6 5.2 %quantize_first.1 = (bf16[8,64,1280]{2,1,0:T(8,128)(2,1)S(1)}, bf16[8,64,1280]{2,1,0:T(8,128)(2,1)S(1)}, bf16[768,2048]{1,0:T(8,128)(2,1)S(1)}, bf16[768,1280]{1...) custom-call(bf16[768,2048]{1,0:T(8,128)(2,1)} %act_far.1, ...), custom_call_target="tpu_custom_call" | custom-call | flops 1 | bytes 1 | tf_op jit(solution)/shard_map/quantize_first/pallas_call | solution.py:152
  5.9 3.3 %collective-permute-start = (bf16[8,64,1280]{2,1,0:T(8,128)(2,1)S(1)}, bf16[8,64,1280]{2,1,0:T(8,128)(2,1)S(1)}, u32[]{:S(2)}, u32[]{:S(2)}) collective-permute-start(bf16[8,64,1280]{2,1,0:T(8,128)(2,1)S(1)} %get-tuple-element.43._), channel_id=1, source_target_pairs={{0,8},{8,0},{16,24},{24,16},{32,40},{40,32},{48,56},{56,48},{64,72... | collective-permute-start | bytes 3932168 | tf_op jit(solution)/shard_map/ppermute | solution.py:68
  9.2 1.4 %quantize_next.2 = (bf16[4,64,1280]{2,1,0:T(8,128)(2,1)S(1)}, bf16[4,64,1280]{2,1,0:T(8,128)(2,1)S(1)}) custom-call(bf16[768,2048]{1,0:T(8,128)(2,1)S(1)} %get-tuple-element.44.act, bf16[768,1280]{1,0:T(8,128)(2,1)S(1)} %get-tuple-element.45.rotated, s32[5,2048]{1,0:T(8,128)S(1)} %get-tuple-element.46.exps.refs_6_, bf16[8,64,1280]{2,1,0:T(8,128)(2,1)S(1)} %get-tuple-element.43._), custom_call_target="tpu_custom_call" | custom-call | flops 1 | bytes 1 | tf_op jit(solution)/shard_map/quantize_next/pallas_call | solution.py:181
  10.6 1.4 %quantize_next.3 = (bf16[4,64,1280]{2,1,0:T(8,128)(2,1)S(1)}, bf16[4,64,1280]{2,1,0:T(8,128)(2,1)S(1)}) custom-call(bf16[768,2048]{1,0:T(8,128)(2,1)S(1)} %get-tuple-element.44.act, bf16[768,1280]{1,0:T(8,128)(2,1)S(1)} %get-tuple-element.45.rotated, s32[5,2048]{1,0:T(8,128)S(1)} %get-tuple-element.46.exps.refs_6_, bf16[4,64,1280]{2,1,0:T(8,128)(2,1)S(1)} %get-tuple-element.48._), custom_call_target="tpu_custom_call" | custom-call | flops 1 | bytes 1 | tf_op jit(solution)/shard_map/quantize_next/pallas_call | solution.py:181
  12.1 0.5 collective-permute-start.1
  12.7 4.4 %collective-permute-start.6 = (bf16[4,64,1280]{2,1,0:T(8,128)(2,1)S(1)}, bf16[4,64,1280]{2,1,0:T(8,128)(2,1)S(1)}, u32[]{:S(2)}, u32[]{:S(2)}) collective-permute-start(bf16[4,64,1280]{2,1,0:T(8,128)(2,1)S(1)} %row_sum.1), channel_id=1, source_target_pairs={{0,64},{8,200},{16,80},{24,216},{32,96},{40,232},{48,112},{56,248}... | collective-permute-start | bytes 1966088 | tf_op jit(solution)/shard_map/ppermute | solution.py:68
  17.6 2.5 %collective-permute-start.3 = (bf16[2,64,1280]{2,1,0:T(8,128)(2,1)S(1)}, bf16[2,64,1280]{2,1,0:T(8,128)(2,1)S(1)}, u32[]{:S(2)}, u32[]{:S(2)}) collective-permute-start(bf16[2,64,1280]{2,1,0:T(8,128)(2,1)S(1)} %get-tuple-element.52), channel_id=1, source_target_pairs={{0,16},{8,56},{16,32},{24,8},{32,48},{40,24},{48,0},{56,40},{64,80... | collective-permute-start | bytes 983048 | tf_op jit(solution)/shard_map/ppermute | solution.py:68
  20.1 1.7 %collective-permute-start.5 = (bf16[2,64,1280]{2,1,0:T(8,128)(2,1)S(1)}, bf16[2,64,1280]{2,1,0:T(8,128)(2,1)S(1)}, u32[]{:S(2)}, u32[]{:S(2)}) collective-permute-start(bf16[2,64,1280]{2,1,0:T(8,128)(2,1)S(1)} %get-tuple-element.54), channel_id=1, source_target_pairs={{0,32},{8,40},{16,48},{24,56},{32,0},{40,8},{48,16},{56,24},{64,96... | collective-permute-start | bytes 983048 | tf_op jit(solution)/shard_map/ppermute | solution.py:68
  21.9 11.9 %collective-permute-done.3.xa = bf16[2,64,1280]{2,1,0:T(8,128)(2,1)S(1)} collective-permute-done((bf16[2,64,1280]{2,1,0:T(8,128)(2,1)S(1)}, bf16[2,64,1280]{2,1,0:T(8,128)(2,1)S(1)}, u32[]{:S(2)}, u32[]{:S(2)}) %collective-permute-start.3) | collective-permute-done | bytes 327712 | tf_op jit(solution)/shard_map/ppermute | solution.py:68
  33.8 0.5 collective-permute-done.4.xb
  34.6 3.1 %collective-permute-start.7 = (bf16[64,1280]{1,0:T(8,128)(2,1)S(1)}, bf16[64,1280]{1,0:T(8,128)(2,1)S(1)}, u32[]{:S(2)}, u32[]{:S(2)}) collective-permute-start(bf16[64,1280]{1,0:T(8,128)(2,1)S(1)} %get-tuple-element.56), channel_id=1, source_target_pairs={{0,192},{8,72},{16,208},{24,88},{32,224},{40,104},{48,240},{56,120... | collective-permute-start | bytes 491528 | tf_op jit(solution)/shard_map/ppermute | solution.py:68
  37.7 4.4 %collective-permute-start.8 = (bf16[64,1280]{1,0:T(8,128)(2,1)S(1)}, bf16[64,1280]{1,0:T(8,128)(2,1)S(1)}, u32[]{:S(2)}, u32[]{:S(2)}) collective-permute-start(bf16[64,1280]{1,0:T(8,128)(2,1)S(1)} %get-tuple-element.57), channel_id=1, source_target_pairs={{0,128},{8,136},{16,144},{24,152},{32,160},{40,168},{48,176},{56,1... | collective-permute-start | bytes 491528 | tf_op jit(solution)/shard_map/ppermute | solution.py:68
  42.0 1.5 %collective-permute-start.11 = (bf16[64,1280]{1,0:T(8,128)(2,1)S(1)}, bf16[64,1280]{1,0:T(8,128)(2,1)S(1)}, u32[]{:S(2)}, u32[]{:S(2)}) collective-permute-start(bf16[64,1280]{1,0:T(8,128)(2,1)S(1)} %get-tuple-element.60), channel_id=1, source_target_pairs={{0,48},{8,24},{16,0},{24,40},{32,16},{40,56},{48,32},{56,8},{64,11... | collective-permute-start | bytes 491528 | tf_op jit(solution)/shard_map/ppermute | solution.py:68
  43.8 7.6 %collective-permute-done.8.refs_0_.refs_2_ = bf16[64,1280]{1,0:T(8,128)(2,1)S(1)} collective-permute-done((bf16[64,1280]{1,0:T(8,128)(2,1)S(1)}, bf16[64,1280]{1,0:T(8,128)(2,1)S(1)}, u32[]{:S(2)}, u32[]{:S(2)}) %collective-permute-start.8) | collective-permute-done | bytes 163872 | tf_op jit(solution)/shard_map/ppermute | solution.py:68
  51.5 0.9 collective-permute-done.11.refs_5_
  52.4 0.8 update.1
  53.2 4.0 %collective-permute-start.15 = (bf16[64,1280]{1,0:T(8,128)(2,1)S(1)}, bf16[64,1280]{1,0:T(8,128)(2,1)S(1)}, u32[]{:S(2)}, u32[]{:S(2)}) collective-permute-start(bf16[64,1280]{1,0:T(8,128)(2,1)S(1)} %get-tuple-element.63.w), channel_id=1, source_target_pairs={{0,128},{8,136},{16,144},{24,152},{32,160},{40,168},{48,176},{56,1... | collective-permute-start | bytes 491528 | tf_op jit(solution)/shard_map/ppermute | solution.py:68
  57.2 2.6 %collective-permute-start.13 = (bf16[64,1280]{1,0:T(8,128)(2,1)S(1)}, bf16[64,1280]{1,0:T(8,128)(2,1)S(1)}, u32[]{:S(2)}, u32[]{:S(2)}) collective-permute-start(bf16[64,1280]{1,0:T(8,128)(2,1)S(1)} %get-tuple-element.63.w), channel_id=1, source_target_pairs={{0,16},{8,56},{16,32},{24,8},{32,48},{40,24},{48,0},{56,40},{64,80... | collective-permute-start | bytes 491528 | tf_op jit(solution)/shard_map/ppermute | solution.py:68
  59.8 0.5 collective-permute-start.14
  60.3 1.4 %collective-permute-done.15.refs_0_.z2 = bf16[64,1280]{1,0:T(8,128)(2,1)S(1)} collective-permute-done((bf16[64,1280]{1,0:T(8,128)(2,1)S(1)}, bf16[64,1280]{1,0:T(8,128)(2,1)S(1)}, u32[]{:S(2)}, u32[]{:S(2)}) %collective-permute-start.15) | collective-permute-done | bytes 163872 | tf_op jit(solution)/shard_map/ppermute | solution.py:68
  61.7 7.2 %collective-permute-done.16.refs_1_.za = bf16[64,1280]{1,0:T(8,128)(2,1)S(1)} collective-permute-done((bf16[64,1280]{1,0:T(8,128)(2,1)S(1)}, bf16[64,1280]{1,0:T(8,128)(2,1)S(1)}, u32[]{:S(2)}, u32[]{:S(2)}) %collective-permute-start.16) | collective-permute-done | bytes 163872 | tf_op jit(solution)/shard_map/ppermute | solution.py:68
  69.1 1.7 %collective-permute-start.17 = (bf16[6,64,1280]{2,1,0:T(8,128)(2,1)S(1)}, bf16[6,64,1280]{2,1,0:T(8,128)(2,1)S(1)}, u32[]{:S(2)}, u32[]{:S(2)}) collective-permute-start(bf16[6,64,1280]{2,1,0:T(8,128)(2,1)S(1)} %get-tuple-element.64.refs_0_), channel_id=1, source_target_pairs={{0,8},{8,0},{16,24},{24,16},{32,40},{40,32},{48,56},{56,48},{64,72... | collective-permute-start | bytes 2949128 | tf_op jit(solution)/shard_map/ppermute | solution.py:68
  70.8 1.8 %collective-permute-start.18 = (bf16[4,64,1280]{2,1,0:T(8,128)(2,1)S(1)}, bf16[4,64,1280]{2,1,0:T(8,128)(2,1)S(1)}, u32[]{:S(2)}, u32[]{:S(2)}) collective-permute-start(bf16[4,64,1280]{2,1,0:T(8,128)(2,1)S(1)} %get-tuple-element.73), channel_id=1, source_target_pairs={{0,192},{8,72},{16,208},{24,88},{32,224},{40,104},{48,240},{56,120... | collective-permute-start | bytes 1966088 | tf_op jit(solution)/shard_map/ppermute | solution.py:68
  72.6 1.8 %collective-permute-start.20 = (bf16[2,64,1280]{2,1,0:T(8,128)(2,1)S(1)}, bf16[2,64,1280]{2,1,0:T(8,128)(2,1)S(1)}, u32[]{:S(2)}, u32[]{:S(2)}) collective-permute-start(bf16[2,64,1280]{2,1,0:T(8,128)(2,1)S(1)} %get-tuple-element.74), channel_id=1, source_target_pairs={{0,48},{8,24},{16,0},{24,40},{32,16},{40,56},{48,32},{56,8},{64,11... | collective-permute-start | bytes 983048 | tf_op jit(solution)/shard_map/ppermute | solution.py:68
  74.3 0.9 collective-permute-start.21
  75.3 1.8 %place.3 = (bf16[2048,1280]{1,0:T(8,128)(2,1)}, f32[64,1280]{1,0:T(8,128)}, f32[64,1280]{1,0:T(8,128)}, f32[64,1280]{1,0:T(8,128)}, f32[64,1280]{1,0:T(8,128)}, /*index=5*/bf16[16,128]{1,0:T(8,128)(2,1)S(1)}) custom-call(bf16[6,64,1280]{2,1,0:T(8,128)(2,1)S(1)} %get-tuple-element.64.refs_0_, bf16[6,64,1280]{2,1,0:T(8,128)(2,1)S(1)} %collective-permute-done.17.refs_1_, ...), custom_call_target="tpu_custom_call" | custom-call | flops 1 | bytes 1 | tf_op jit(solution)/shard_map/place/pallas_call | solution.py:408
  77.1 6.0 %collective-permute-done.19.refs_1_ = bf16[2,64,1280]{2,1,0:T(8,128)(2,1)S(1)} collective-permute-done((bf16[2,64,1280]{2,1,0:T(8,128)(2,1)S(1)}, bf16[2,64,1280]{2,1,0:T(8,128)(2,1)S(1)}, u32[]{:S(2)}, u32[]{:S(2)}) %collective-permute-start.19) | collective-permute-done | bytes 327712 | tf_op jit(solution)/shard_map/ppermute | solution.py:68
  83.1 7.0 %collective-permute-done.20.refs_2_ = bf16[2,64,1280]{2,1,0:T(8,128)(2,1)S(1)} collective-permute-done((bf16[2,64,1280]{2,1,0:T(8,128)(2,1)S(1)}, bf16[2,64,1280]{2,1,0:T(8,128)(2,1)S(1)}, u32[]{:S(2)}, u32[]{:S(2)}) %collective-permute-start.20) | collective-permute-done | bytes 327712 | tf_op jit(solution)/shard_map/ppermute | solution.py:68
  90.2 0.9 collective-permute-start.22
  91.1 1.8 %place.4 = (bf16[2048,1280]{1,0:T(8,128)(2,1)}, bf16[16,128]{1,0:T(8,128)(2,1)}) custom-call(bf16[10,64,1280]{2,1,0:T(8,128)(2,1)S(1)} %join.1.refs_0_, bf16[2048,1280]{1,0:T(8,128)(2,1)} %get-tuple-element.76.refs_1_), custom_call_target="tpu_custom_call", output_to_operand_aliasing={{0}: (1, {})} | custom-call | flops 1 | bytes 1 | tf_op jit(solution)/shard_map/place/pallas_call | solution.py:408
  93.0 1.3 %collective-permute-done.22.refs_0_ = bf16[10,64,1280]{2,1,0:T(8,128)(2,1)S(1)} collective-permute-done((bf16[10,64,1280]{2,1,0:T(8,128)(2,1)S(1)}, bf16[10,64,1280]{2,1,0:T(8,128)(2,1)S(1)}, u32[]{:S(2)}, u32[]{:S(2)}) %collective-permute-start.22) | collective-permute-done | bytes 1638432 | tf_op jit(solution)/shard_map/ppermute | solution.py:68
  94.3 1.8 %place.5 = (bf16[2048,1280]{1,0:T(8,128)(2,1)}, bf16[16,128]{1,0:T(8,128)(2,1)}) custom-call(bf16[10,64,1280]{2,1,0:T(8,128)(2,1)S(1)} %collective-permute-done.22.refs_0_, bf16[2048,1280]{1,0:T(8,128)(2,1)} %get-tuple-element.77.refs_1_), custom_call_target="tpu_custom_call", output_to_operand_aliasing={{0}: (1, {})} | custom-call | flops 1 | bytes 1 | tf_op jit(solution)/shard_map/place/pallas_call | solution.py:408
  (34 shorter events, 1.7 us)
Async XLA Ops:
  5.9 6.7 %collective-permute-start = (bf16[8,64,1280]{2,1,0:T(8,128)(2,1)S(1)}, bf16[8,64,1280]{2,1,0:T(8,128)(2,1)S(1)}, u32[]{:S(2)}, u32[]{:S(2)}) collective-permute-start(bf16[8,64,1280]{2,1,0:T(8,128)(2,1)S(1)} %get-tuple-element.43._), channel_id=1, source_target_pairs={{0,8},{8,0},{16,24},{24,16},{32,40},{40,32},{48,56},{56,48},{64,72... | collective-permute-start | bytes 3932168 | tf_op jit(solution)/shard_map/ppermute | solution.py:68
  12.0 5.1 %collective-permute-start.2 = (bf16[4,64,1280]{2,1,0:T(8,128)(2,1)S(1)}, bf16[4,64,1280]{2,1,0:T(8,128)(2,1)S(1)}, u32[]{:S(2)}, u32[]{:S(2)}) collective-permute-start(bf16[4,64,1280]{2,1,0:T(8,128)(2,1)S(1)} %get-tuple-element.50), channel_id=1, source_target_pairs={{0,8},{8,0},{16,24},{24,16},{32,40},{40,32},{48,56},{56,48},{64,72... | collective-permute-start | bytes 1966088 | tf_op jit(solution)/shard_map/ppermute | solution.py:68
  12.1 5.0 %collective-permute-start.1 = (bf16[4,64,1280]{2,1,0:T(8,128)(2,1)S(1)}, bf16[4,64,1280]{2,1,0:T(8,128)(2,1)S(1)}, u32[]{:S(2)}, u32[]{:S(2)}) collective-permute-start(bf16[4,64,1280]{2,1,0:T(8,128)(2,1)S(1)} %get-tuple-element.48._), channel_id=1, source_target_pairs={{0,8},{8,0},{16,24},{24,16},{32,40},{40,32},{48,56},{56,48},{64,72... | collective-permute-start | bytes 1966088 | tf_op jit(solution)/shard_map/ppermute | solution.py:68
  12.7 21.6 %collective-permute-start.6 = (bf16[4,64,1280]{2,1,0:T(8,128)(2,1)S(1)}, bf16[4,64,1280]{2,1,0:T(8,128)(2,1)S(1)}, u32[]{:S(2)}, u32[]{:S(2)}) collective-permute-start(bf16[4,64,1280]{2,1,0:T(8,128)(2,1)S(1)} %row_sum.1), channel_id=1, source_target_pairs={{0,64},{8,200},{16,80},{24,216},{32,96},{40,232},{48,112},{56,248}... | collective-permute-start | bytes 1966088 | tf_op jit(solution)/shard_map/ppermute | solution.py:68
  17.6 34.9 %copy-start = (f32[64,1280]{1,0:T(8,128)S(1)}, f32[64,1280]{1,0:T(8,128)}, u32[]{:S(2)}) copy-start(f32[64,1280]{1,0:T(8,128)} %refs_9_.1) | copy-start | bytes 983044
  17.6 34.9 %copy-start.1 = (f32[64,1280]{1,0:T(8,128)S(1)}, f32[64,1280]{1,0:T(8,128)}, u32[]{:S(2)}) copy-start(f32[64,1280]{1,0:T(8,128)} %refs_10_.1) | copy-start | bytes 983044
  17.6 34.8 %copy-start.2 = (f32[64,1280]{1,0:T(8,128)S(1)}, f32[64,1280]{1,0:T(8,128)}, u32[]{:S(2)}) copy-start(f32[64,1280]{1,0:T(8,128)} %refs_11_.1) | copy-start | bytes 983044
  17.6 16.2 %collective-permute-start.3 = (bf16[2,64,1280]{2,1,0:T(8,128)(2,1)S(1)}, bf16[2,64,1280]{2,1,0:T(8,128)(2,1)S(1)}, u32[]{:S(2)}, u32[]{:S(2)}) collective-permute-start(bf16[2,64,1280]{2,1,0:T(8,128)(2,1)S(1)} %get-tuple-element.52), channel_id=1, source_target_pairs={{0,16},{8,56},{16,32},{24,8},{32,48},{40,24},{48,0},{56,40},{64,80... | collective-permute-start | bytes 983048 | tf_op jit(solution)/shard_map/ppermute | solution.py:68
  20.1 14.2 %collective-permute-start.4 = (bf16[2,64,1280]{2,1,0:T(8,128)(2,1)S(1)}, bf16[2,64,1280]{2,1,0:T(8,128)(2,1)S(1)}, u32[]{:S(2)}, u32[]{:S(2)}) collective-permute-start(bf16[2,64,1280]{2,1,0:T(8,128)(2,1)S(1)} %get-tuple-element.53), channel_id=1, source_target_pairs={{0,48},{8,24},{16,0},{24,40},{32,16},{40,56},{48,32},{56,8},{64,11... | collective-permute-start | bytes 983048 | tf_op jit(solution)/shard_map/ppermute | solution.py:68
  20.1 14.2 %collective-permute-start.5 = (bf16[2,64,1280]{2,1,0:T(8,128)(2,1)S(1)}, bf16[2,64,1280]{2,1,0:T(8,128)(2,1)S(1)}, u32[]{:S(2)}, u32[]{:S(2)}) collective-permute-start(bf16[2,64,1280]{2,1,0:T(8,128)(2,1)S(1)} %get-tuple-element.54), channel_id=1, source_target_pairs={{0,32},{8,40},{16,48},{24,56},{32,0},{40,8},{48,16},{56,24},{64,96... | collective-permute-start | bytes 983048 | tf_op jit(solution)/shard_map/ppermute | solution.py:68
  34.6 9.2 %collective-permute-start.7 = (bf16[64,1280]{1,0:T(8,128)(2,1)S(1)}, bf16[64,1280]{1,0:T(8,128)(2,1)S(1)}, u32[]{:S(2)}, u32[]{:S(2)}) collective-permute-start(bf16[64,1280]{1,0:T(8,128)(2,1)S(1)} %get-tuple-element.56), channel_id=1, source_target_pairs={{0,192},{8,72},{16,208},{24,88},{32,224},{40,104},{48,240},{56,120... | collective-permute-start | bytes 491528 | tf_op jit(solution)/shard_map/ppermute | solution.py:68
  37.7 13.8 %collective-permute-start.8 = (bf16[64,1280]{1,0:T(8,128)(2,1)S(1)}, bf16[64,1280]{1,0:T(8,128)(2,1)S(1)}, u32[]{:S(2)}, u32[]{:S(2)}) collective-permute-start(bf16[64,1280]{1,0:T(8,128)(2,1)S(1)} %get-tuple-element.57), channel_id=1, source_target_pairs={{0,128},{8,136},{16,144},{24,152},{32,160},{40,168},{48,176},{56,1... | collective-permute-start | bytes 491528 | tf_op jit(solution)/shard_map/ppermute | solution.py:68
  42.0 9.4 %collective-permute-start.10 = (bf16[64,1280]{1,0:T(8,128)(2,1)S(1)}, bf16[64,1280]{1,0:T(8,128)(2,1)S(1)}, u32[]{:S(2)}, u32[]{:S(2)}) collective-permute-start(bf16[64,1280]{1,0:T(8,128)(2,1)S(1)} %get-tuple-element.59), channel_id=1, source_target_pairs={{0,16},{8,56},{16,32},{24,8},{32,48},{40,24},{48,0},{56,40},{64,80... | collective-permute-start | bytes 491528 | tf_op jit(solution)/shard_map/ppermute | solution.py:68
  42.0 10.4 %collective-permute-start.11 = (bf16[64,1280]{1,0:T(8,128)(2,1)S(1)}, bf16[64,1280]{1,0:T(8,128)(2,1)S(1)}, u32[]{:S(2)}, u32[]{:S(2)}) collective-permute-start(bf16[64,1280]{1,0:T(8,128)(2,1)S(1)} %get-tuple-element.60), channel_id=1, source_target_pairs={{0,48},{8,24},{16,0},{24,40},{32,16},{40,56},{48,32},{56,8},{64,11... | collective-permute-start | bytes 491528 | tf_op jit(solution)/shard_map/ppermute | solution.py:68
  43.5 8.9 %collective-permute-start.9 = (bf16[64,1280]{1,0:T(8,128)(2,1)S(1)}, bf16[64,1280]{1,0:T(8,128)(2,1)S(1)}, u32[]{:S(2)}, u32[]{:S(2)}) collective-permute-start(bf16[64,1280]{1,0:T(8,128)(2,1)S(1)} %get-tuple-element.58), channel_id=1, source_target_pairs={{0,32},{8,40},{16,48},{24,56},{32,0},{40,8},{48,16},{56,24},{64,96... | collective-permute-start | bytes 491528 | tf_op jit(solution)/shard_map/ppermute | solution.py:68
  53.2 8.5 %collective-permute-start.15 = (bf16[64,1280]{1,0:T(8,128)(2,1)S(1)}, bf16[64,1280]{1,0:T(8,128)(2,1)S(1)}, u32[]{:S(2)}, u32[]{:S(2)}) collective-permute-start(bf16[64,1280]{1,0:T(8,128)(2,1)S(1)} %get-tuple-element.63.w), channel_id=1, source_target_pairs={{0,128},{8,136},{16,144},{24,152},{32,160},{40,168},{48,176},{56,1... | collective-permute-start | bytes 491528 | tf_op jit(solution)/shard_map/ppermute | solution.py:68
  57.1 11.8 %collective-permute-start.16 = (bf16[64,1280]{1,0:T(8,128)(2,1)S(1)}, bf16[64,1280]{1,0:T(8,128)(2,1)S(1)}, u32[]{:S(2)}, u32[]{:S(2)}) collective-permute-start(bf16[64,1280]{1,0:T(8,128)(2,1)S(1)} %get-tuple-element.63.w), channel_id=1, source_target_pairs={{0,64},{8,200},{16,80},{24,216},{32,96},{40,232},{48,112},{56,248}... | collective-permute-start | bytes 491528 | tf_op jit(solution)/shard_map/ppermute | solution.py:68
  57.1 11.8 %collective-permute-start.12 = (bf16[64,1280]{1,0:T(8,128)(2,1)S(1)}, bf16[64,1280]{1,0:T(8,128)(2,1)S(1)}, u32[]{:S(2)}, u32[]{:S(2)}) collective-permute-start(bf16[64,1280]{1,0:T(8,128)(2,1)S(1)} %get-tuple-element.63.w), channel_id=1, source_target_pairs={{0,48},{8,24},{16,0},{24,40},{32,16},{40,56},{48,32},{56,8},{64,11... | collective-permute-start | bytes 491528 | tf_op jit(solution)/shard_map/ppermute | solution.py:68
  57.2 11.7 %collective-permute-start.13 = (bf16[64,1280]{1,0:T(8,128)(2,1)S(1)}, bf16[64,1280]{1,0:T(8,128)(2,1)S(1)}, u32[]{:S(2)}, u32[]{:S(2)}) collective-permute-start(bf16[64,1280]{1,0:T(8,128)(2,1)S(1)} %get-tuple-element.63.w), channel_id=1, source_target_pairs={{0,16},{8,56},{16,32},{24,8},{32,48},{40,24},{48,0},{56,40},{64,80... | collective-permute-start | bytes 491528 | tf_op jit(solution)/shard_map/ppermute | solution.py:68
  59.8 9.1 %collective-permute-start.14 = (bf16[64,1280]{1,0:T(8,128)(2,1)S(1)}, bf16[64,1280]{1,0:T(8,128)(2,1)S(1)}, u32[]{:S(2)}, u32[]{:S(2)}) collective-permute-start(bf16[64,1280]{1,0:T(8,128)(2,1)S(1)} %get-tuple-element.63.w), channel_id=1, source_target_pairs={{0,32},{8,40},{16,48},{24,56},{32,0},{40,8},{48,16},{56,24},{64,96... | collective-permute-start | bytes 491528 | tf_op jit(solution)/shard_map/ppermute | solution.py:68
  69.1 6.2 %collective-permute-start.17 = (bf16[6,64,1280]{2,1,0:T(8,128)(2,1)S(1)}, bf16[6,64,1280]{2,1,0:T(8,128)(2,1)S(1)}, u32[]{:S(2)}, u32[]{:S(2)}) collective-permute-start(bf16[6,64,1280]{2,1,0:T(8,128)(2,1)S(1)} %get-tuple-element.64.refs_0_), channel_id=1, source_target_pairs={{0,8},{8,0},{16,24},{24,16},{32,40},{40,32},{48,56},{56,48},{64,72... | collective-permute-start | bytes 2949128 | tf_op jit(solution)/shard_map/ppermute | solution.py:68
  70.8 19.3 %collective-permute-start.18 = (bf16[4,64,1280]{2,1,0:T(8,128)(2,1)S(1)}, bf16[4,64,1280]{2,1,0:T(8,128)(2,1)S(1)}, u32[]{:S(2)}, u32[]{:S(2)}) collective-permute-start(bf16[4,64,1280]{2,1,0:T(8,128)(2,1)S(1)} %get-tuple-element.73), channel_id=1, source_target_pairs={{0,192},{8,72},{16,208},{24,88},{32,224},{40,104},{48,240},{56,120... | collective-permute-start | bytes 1966088 | tf_op jit(solution)/shard_map/ppermute | solution.py:68
  72.6 10.5 %collective-permute-start.19 = (bf16[2,64,1280]{2,1,0:T(8,128)(2,1)S(1)}, bf16[2,64,1280]{2,1,0:T(8,128)(2,1)S(1)}, u32[]{:S(2)}, u32[]{:S(2)}) collective-permute-start(bf16[2,64,1280]{2,1,0:T(8,128)(2,1)S(1)} %get-tuple-element.74), channel_id=1, source_target_pairs={{0,32},{8,40},{16,48},{24,56},{32,0},{40,8},{48,16},{56,24},{64,96... | collective-permute-start | bytes 983048 | tf_op jit(solution)/shard_map/ppermute | solution.py:68
  72.6 17.5 %collective-permute-start.20 = (bf16[2,64,1280]{2,1,0:T(8,128)(2,1)S(1)}, bf16[2,64,1280]{2,1,0:T(8,128)(2,1)S(1)}, u32[]{:S(2)}, u32[]{:S(2)}) collective-permute-start(bf16[2,64,1280]{2,1,0:T(8,128)(2,1)S(1)} %get-tuple-element.74), channel_id=1, source_target_pairs={{0,48},{8,24},{16,0},{24,40},{32,16},{40,56},{48,32},{56,8},{64,11... | collective-permute-start | bytes 983048 | tf_op jit(solution)/shard_map/ppermute | solution.py:68
  74.3 15.8 %collective-permute-start.21 = (bf16[2,64,1280]{2,1,0:T(8,128)(2,1)S(1)}, bf16[2,64,1280]{2,1,0:T(8,128)(2,1)S(1)}, u32[]{:S(2)}, u32[]{:S(2)}) collective-permute-start(bf16[2,64,1280]{2,1,0:T(8,128)(2,1)S(1)} %get-tuple-element.74), channel_id=1, source_target_pairs={{0,16},{8,56},{16,32},{24,8},{32,48},{40,24},{48,0},{56,40},{64,80... | collective-permute-start | bytes 983048 | tf_op jit(solution)/shard_map/ppermute | solution.py:68
  90.2 4.1 %collective-permute-start.22 = (bf16[10,64,1280]{2,1,0:T(8,128)(2,1)S(1)}, bf16[10,64,1280]{2,1,0:T(8,128)(2,1)S(1)}, u32[]{:S(2)}, u32[]{:S(2)}) collective-permute-start(bf16[10,64,1280]{2,1,0:T(8,128)(2,1)S(1)} %join.1.refs_0_), channel_id=1, source_target_pairs={{0,8},{8,0},{16,24},{24,16},{32,40},{40,32},{48,56},{56,48},{64,72... | collective-permute-start | bytes 4915208 | tf_op jit(solution)/shard_map/ppermute | solution.py:68

commit v5 on v4

--- a/solution.py
+++ b/solution.py
@@ -213,44 +213,40 @@
     )(*held(mine, other, after))
 
 
-def sides_kernel(mine, other, mine_2, other_2, mine_0, other_0, xa, xb, x2, pairs):
+def sides_kernel(mine, other, mine_2, other_2, xa, xb, x2):
     _, _, core = place_of()
     a, b = step("a", core), step("b", core)
     for k, out in ((a, xa), (b, xb), (2, x2)):
         out[0] = add(mine[NX + k], other[NX + k])
         out[1] = add(mine_2[k], other_2[k])
-    pairs[0] = add(mine[NX], other[NX])
-    pairs[1] = add(mine_2[0], other_2[0])
-    for k, way in enumerate((a, b, 2, 0)):
-        pairs[2 + k] = add(mine_0[way], other_0[way])
 
 
 def sides_sum(*parts):
     return pl.pallas_call(
         sides_kernel,
-        in_specs=[FULL] * 6,
-        out_specs=[FULL] * 4,
-        out_shape=[vmem(2, ROW, COLS)] * 3 + [vmem(6, ROW, COLS)],
+        in_specs=[FULL] * 4,
+        out_specs=[FULL] * 3,
+        out_shape=[vmem(2, ROW, COLS)] * 3,
         compiler_params=params(4),
         cost_estimate=TINY,
         name="sides_sum",
     )(*held(*parts))
 
 
-def middle_kernel(pairs, xa, xb, x2, row, *outs):
+def middle_kernel(mine, other, mine_2, other_2, mine_0, other_0, xa, xb, x2, row, *outs):
     zb_out, z2_out, xa_out, xb_out, x2_out, own_out = outs
     _, _, core = place_of()
-    for k, out in enumerate((zb_out, z2_out)):
-        out[...] = add(pairs[k], xa[k], xb[k], x2[k])
+    zb_out[...] = add(mine[NX], other[NX], xa[0], xb[0], x2[0])
+    z2_out[...] = add(mine_2[0], other_2[0], xa[1], xb[1], x2[1])
     ways = (step("a", core), step("b", core), 2, 0)
-    for k, out in enumerate((xa_out, xb_out, x2_out, own_out)):
-        out[...] = add(pairs[2 + k], row[ways[k]])
+    for way, out in zip(ways, (xa_out, xb_out, x2_out, own_out)):
+        out[...] = add(mine_0[way], other_0[way], row[way])
 
 
 def middle_sum(*parts):
     return pl.pallas_call(
         middle_kernel,
-        in_specs=[FULL] * 5,
+        in_specs=[FULL] * 10,
         out_specs=[FULL] * 6,
         out_shape=[vmem(ROW, COLS)] * 6,
         compiler_params=params(4),
@@ -429,9 +425,11 @@
     mine_0, theirs_0 = quantized_next(0, act, rotated, exps, theirs_2)
     other_0 = send(theirs_0, dc=1)
     row = send(row_sum(mine, other, mine_0), dz="a")
-    xa, xb, x2, pairs = sides_sum(mine, other, mine_2, other_2, mine_0, other_0)
+    xa, xb, x2 = sides_sum(mine, other, mine_2, other_2)
     xa, xb, x2 = send(xa, dx="a"), send(xb, dx="b"), send(x2, dx=2)
-    zb, z2, xa, xb, x2, own = middle_sum(pairs, xa, xb, x2, row)
+    zb, z2, xa, xb, x2, own = middle_sum(
+        mine, other, mine_2, other_2, mine_0, other_0, xa, xb, x2, row
+    )
     zb, z2 = send(zb, dz="b"), send(z2, dz=2)
     x2, xa, xb = send(x2, dx=2), send(xa, dx="a"), send(xb, dx="b")
     parts = [own, zb, z2, x2, xa, xb]

time: 96.4 us -> 95.4 us (0.990)
  waiting for transfers between devices: 43.9 us -> 42.8 us
    ppermute x23, waiting for transfers between devices: 43.9 us -> 42.8 us  [send(): return lax.ppermute(value, 'replica', replica_perm(dx, dz, dc))]
  transfers between devices with their start and end apart: 23 -> 23, of which waited for: 9 -> 12; matrix products, arithmetic and copies ran while one was open for 0% -> 0% of each run, Pallas kernels for 7% -> 7%
where the time goes in v5:
time: 95.4 us; the launch traced here: 95.3 us
  waiting for transfers between devices  42.8 us (45%)
  starting transfers between devices  35.6 us (37%)
  Pallas kernels  15.9 us (17%)
    ppermute x23, waiting for transfers between devices, send(): return lax.ppermute(value, 'replica', replica_perm(dx, dz, dc))  42.8 us
    ppermute x23, starting transfers between devices, send(): return lax.ppermute(value, 'replica', replica_perm(dx, dz, dc))  35.6 us
    pallas_call x1, Pallas kernels, quantized_first(): pl.pallas_call(first_kernel, in_specs=[HBM] * 5, out_specs=[FULL] * 7, ou...  5.54 us
    pallas_call x3, Pallas kernels, placed(): pl.pallas_call(functools.partial(place_kernel, names, flips, count, chain...  5.5 us
    pallas_call x2, Pallas kernels, quantized_next(): pl.pallas_call(functools.partial(next_kernel, dz), in_specs=[FULL] * 4, o...  3.08 us
  transfers between devices with their start and end apart: 23, of which 12 were waited for; matrix products, arithmetic and copies ran while one was open for 0% of the time, Pallas kernels for 7%

profile of v5, /device:TPU:1, one launch (start us, length us, event | category | flops | bytes accessed | tf_op | source)
XLA Modules:
  0.0 95.3 jit_solution(16756982460810881973)
XLA Ops:
  0.6 5.5 %quantize_first.1 = (bf16[8,64,1280]{2,1,0:T(8,128)(2,1)S(1)}, bf16[8,64,1280]{2,1,0:T(8,128)(2,1)S(1)}, bf16[768,2048]{1,0:T(8,128)(2,1)S(1)}, bf16[768,1280]{1...) custom-call(bf16[768,2048]{1,0:T(8,128)(2,1)} %act_far.1, ...), custom_call_target="tpu_custom_call" | custom-call | flops 1 | bytes 1 | tf_op jit(solution)/shard_map/quantize_first/pallas_call | solution.py:152
  6.2 3.3 %collective-permute-start = (bf16[8,64,1280]{2,1,0:T(8,128)(2,1)S(1)}, bf16[8,64,1280]{2,1,0:T(8,128)(2,1)S(1)}, u32[]{:S(2)}, u32[]{:S(2)}) collective-permute-start(bf16[8,64,1280]{2,1,0:T(8,128)(2,1)S(1)} %get-tuple-element.42._), channel_id=1, source_target_pairs={{0,8},{8,0},{16,24},{24,16},{32,40},{40,32},{48,56},{56,48},{64,72... | collective-permute-start | bytes 3932168 | tf_op jit(solution)/shard_map/ppermute | solution.py:68
  9.5 1.5 %quantize_next.2 = (bf16[4,64,1280]{2,1,0:T(8,128)(2,1)S(1)}, bf16[4,64,1280]{2,1,0:T(8,128)(2,1)S(1)}) custom-call(bf16[768,2048]{1,0:T(8,128)(2,1)S(1)} %get-tuple-element.43.act, bf16[768,1280]{1,0:T(8,128)(2,1)S(1)} %get-tuple-element.44.rotated, s32[5,2048]{1,0:T(8,128)S(1)} %get-tuple-element.45.exps.refs_6_, bf16[8,64,1280]{2,1,0:T(8,128)(2,1)S(1)} %get-tuple-element.42._), custom_call_target="tpu_custom_call" | custom-call | flops 1 | bytes 1 | tf_op jit(solution)/shard_map/quantize_next/pallas_call | solution.py:181
  11.2 1.5 %quantize_next.3 = (bf16[4,64,1280]{2,1,0:T(8,128)(2,1)S(1)}, bf16[4,64,1280]{2,1,0:T(8,128)(2,1)S(1)}) custom-call(bf16[768,2048]{1,0:T(8,128)(2,1)S(1)} %get-tuple-element.43.act, bf16[768,1280]{1,0:T(8,128)(2,1)S(1)} %get-tuple-element.44.rotated, s32[5,2048]{1,0:T(8,128)S(1)} %get-tuple-element.45.exps.refs_6_, bf16[4,64,1280]{2,1,0:T(8,128)(2,1)S(1)} %get-tuple-element.47._), custom_call_target="tpu_custom_call" | custom-call | flops 1 | bytes 1 | tf_op jit(solution)/shard_map/quantize_next/pallas_call | solution.py:181
  12.7 0.6 collective-permute-start.2
  13.4 4.3 %collective-permute-start.6 = (bf16[4,64,1280]{2,1,0:T(8,128)(2,1)S(1)}, bf16[4,64,1280]{2,1,0:T(8,128)(2,1)S(1)}, u32[]{:S(2)}, u32[]{:S(2)}) collective-permute-start(bf16[4,64,1280]{2,1,0:T(8,128)(2,1)S(1)} %row_sum.1), channel_id=1, source_target_pairs={{0,64},{8,200},{16,80},{24,216},{32,96},{40,232},{48,112},{56,248}... | collective-permute-start | bytes 1966088 | tf_op jit(solution)/shard_map/ppermute | solution.py:68
  18.0 2.5 %collective-permute-start.3 = (bf16[2,64,1280]{2,1,0:T(8,128)(2,1)S(1)}, bf16[2,64,1280]{2,1,0:T(8,128)(2,1)S(1)}, u32[]{:S(2)}, u32[]{:S(2)}) collective-permute-start(bf16[2,64,1280]{2,1,0:T(8,128)(2,1)S(1)} %get-tuple-element.50), channel_id=1, source_target_pairs={{0,16},{8,56},{16,32},{24,8},{32,48},{40,24},{48,0},{56,40},{64,80... | collective-permute-start | bytes 983048 | tf_op jit(solution)/shard_map/ppermute | solution.py:68
  20.6 1.7 %collective-permute-start.5 = (bf16[2,64,1280]{2,1,0:T(8,128)(2,1)S(1)}, bf16[2,64,1280]{2,1,0:T(8,128)(2,1)S(1)}, u32[]{:S(2)}, u32[]{:S(2)}) collective-permute-start(bf16[2,64,1280]{2,1,0:T(8,128)(2,1)S(1)} %get-tuple-element.52), channel_id=1, source_target_pairs={{0,32},{8,40},{16,48},{24,56},{32,0},{40,8},{48,16},{56,24},{64,96... | collective-permute-start | bytes 983048 | tf_op jit(solution)/shard_map/ppermute | solution.py:68
  22.3 5.5 %collective-permute-done.3.xa = bf16[2,64,1280]{2,1,0:T(8,128)(2,1)S(1)} collective-permute-done((bf16[2,64,1280]{2,1,0:T(8,128)(2,1)S(1)}, bf16[2,64,1280]{2,1,0:T(8,128)(2,1)S(1)}, u32[]{:S(2)}, u32[]{:S(2)}) %collective-permute-start.3) | collective-permute-done | bytes 327712 | tf_op jit(solution)/shard_map/ppermute | solution.py:68
  27.8 6.9 %collective-permute-done.4.xb = bf16[2,64,1280]{2,1,0:T(8,128)(2,1)S(1)} collective-permute-done((bf16[2,64,1280]{2,1,0:T(8,128)(2,1)S(1)}, bf16[2,64,1280]{2,1,0:T(8,128)(2,1)S(1)}, u32[]{:S(2)}, u32[]{:S(2)}) %collective-permute-start.4) | collective-permute-done | bytes 327712 | tf_op jit(solution)/shard_map/ppermute | solution.py:68
  35.4 4.6 %collective-permute-start.8 = (bf16[64,1280]{1,0:T(8,128)(2,1)S(1)}, bf16[64,1280]{1,0:T(8,128)(2,1)S(1)}, u32[]{:S(2)}, u32[]{:S(2)}) collective-permute-start(bf16[64,1280]{1,0:T(8,128)(2,1)S(1)} %get-tuple-element.55), channel_id=1, source_target_pairs={{0,128},{8,136},{16,144},{24,152},{32,160},{40,168},{48,176},{56,1... | collective-permute-start | bytes 491528 | tf_op jit(solution)/shard_map/ppermute | solution.py:68
  40.0 2.1 %collective-permute-start.10 = (bf16[64,1280]{1,0:T(8,128)(2,1)S(1)}, bf16[64,1280]{1,0:T(8,128)(2,1)S(1)}, u32[]{:S(2)}, u32[]{:S(2)}) collective-permute-start(bf16[64,1280]{1,0:T(8,128)(2,1)S(1)} %get-tuple-element.57), channel_id=1, source_target_pairs={{0,16},{8,56},{16,32},{24,8},{32,48},{40,24},{48,0},{56,40},{64,80... | collective-permute-start | bytes 491528 | tf_op jit(solution)/shard_map/ppermute | solution.py:68
  42.2 1.2 %collective-permute-start.9 = (bf16[64,1280]{1,0:T(8,128)(2,1)S(1)}, bf16[64,1280]{1,0:T(8,128)(2,1)S(1)}, u32[]{:S(2)}, u32[]{:S(2)}) collective-permute-start(bf16[64,1280]{1,0:T(8,128)(2,1)S(1)} %get-tuple-element.56), channel_id=1, source_target_pairs={{0,32},{8,40},{16,48},{24,56},{32,0},{40,8},{48,16},{56,24},{64,96... | collective-permute-start | bytes 491528 | tf_op jit(solution)/shard_map/ppermute | solution.py:68
  43.3 1.4 %collective-permute-done.7.refs_1_ = bf16[64,1280]{1,0:T(8,128)(2,1)S(1)} collective-permute-done((bf16[64,1280]{1,0:T(8,128)(2,1)S(1)}, bf16[64,1280]{1,0:T(8,128)(2,1)S(1)}, u32[]{:S(2)}, u32[]{:S(2)}) %collective-permute-start.7) | collective-permute-done | bytes 163872 | tf_op jit(solution)/shard_map/ppermute | solution.py:68
  44.8 3.0 %collective-permute-done.8.refs_0_.refs_2_ = bf16[64,1280]{1,0:T(8,128)(2,1)S(1)} collective-permute-done((bf16[64,1280]{1,0:T(8,128)(2,1)S(1)}, bf16[64,1280]{1,0:T(8,128)(2,1)S(1)}, u32[]{:S(2)}, u32[]{:S(2)}) %collective-permute-start.8) | collective-permute-done | bytes 163872 | tf_op jit(solution)/shard_map/ppermute | solution.py:68
  47.8 3.8 %collective-permute-done.11.refs_5_ = bf16[64,1280]{1,0:T(8,128)(2,1)S(1)} collective-permute-done((bf16[64,1280]{1,0:T(8,128)(2,1)S(1)}, bf16[64,1280]{1,0:T(8,128)(2,1)S(1)}, u32[]{:S(2)}, u32[]{:S(2)}) %collective-permute-start.11) | collective-permute-done | bytes 163872 | tf_op jit(solution)/shard_map/ppermute | solution.py:68
  51.7 0.8 update.1
  53.0 4.7 %collective-permute-start.16 = (bf16[64,1280]{1,0:T(8,128)(2,1)S(1)}, bf16[64,1280]{1,0:T(8,128)(2,1)S(1)}, u32[]{:S(2)}, u32[]{:S(2)}) collective-permute-start(bf16[64,1280]{1,0:T(8,128)(2,1)S(1)} %get-tuple-element.61.w), channel_id=1, source_target_pairs={{0,64},{8,200},{16,80},{24,216},{32,96},{40,232},{48,112},{56,248}... | collective-permute-start | bytes 491528 | tf_op jit(solution)/shard_map/ppermute | solution.py:68
  57.7 2.7 %collective-permute-start.13 = (bf16[64,1280]{1,0:T(8,128)(2,1)S(1)}, bf16[64,1280]{1,0:T(8,128)(2,1)S(1)}, u32[]{:S(2)}, u32[]{:S(2)}) collective-permute-start(bf16[64,1280]{1,0:T(8,128)(2,1)S(1)} %get-tuple-element.61.w), channel_id=1, source_target_pairs={{0,16},{8,56},{16,32},{24,8},{32,48},{40,24},{48,0},{56,40},{64,80... | collective-permute-start | bytes 491528 | tf_op jit(solution)/shard_map/ppermute | solution.py:68
  60.3 1.9 %collective-permute-done.15.refs_0_.z2 = bf16[64,1280]{1,0:T(8,128)(2,1)S(1)} collective-permute-done((bf16[64,1280]{1,0:T(8,128)(2,1)S(1)}, bf16[64,1280]{1,0:T(8,128)(2,1)S(1)}, u32[]{:S(2)}, u32[]{:S(2)}) %collective-permute-start.15) | collective-permute-done | bytes 163872 | tf_op jit(solution)/shard_map/ppermute | solution.py:68
  62.2 5.3 %collective-permute-done.16.refs_1_.za = bf16[64,1280]{1,0:T(8,128)(2,1)S(1)} collective-permute-done((bf16[64,1280]{1,0:T(8,128)(2,1)S(1)}, bf16[64,1280]{1,0:T(8,128)(2,1)S(1)}, u32[]{:S(2)}, u32[]{:S(2)}) %collective-permute-start.16) | collective-permute-done | bytes 163872 | tf_op jit(solution)/shard_map/ppermute | solution.py:68
  68.3 1.8 %collective-permute-start.17 = (bf16[6,64,1280]{2,1,0:T(8,128)(2,1)S(1)}, bf16[6,64,1280]{2,1,0:T(8,128)(2,1)S(1)}, u32[]{:S(2)}, u32[]{:S(2)}) collective-permute-start(bf16[6,64,1280]{2,1,0:T(8,128)(2,1)S(1)} %get-tuple-element.62.refs_0_), channel_id=1, source_target_pairs={{0,8},{8,0},{16,24},{24,16},{32,40},{40,32},{48,56},{56,48},{64,72... | collective-permute-start | bytes 2949128 | tf_op jit(solution)/shard_map/ppermute | solution.py:68
  70.1 1.5 %collective-permute-start.18 = (bf16[4,64,1280]{2,1,0:T(8,128)(2,1)S(1)}, bf16[4,64,1280]{2,1,0:T(8,128)(2,1)S(1)}, u32[]{:S(2)}, u32[]{:S(2)}) collective-permute-start(bf16[4,64,1280]{2,1,0:T(8,128)(2,1)S(1)} %get-tuple-element.71), channel_id=1, source_target_pairs={{0,192},{8,72},{16,208},{24,88},{32,224},{40,104},{48,240},{56,120... | collective-permute-start | bytes 1966088 | tf_op jit(solution)/shard_map/ppermute | solution.py:68
  71.6 0.7 collective-permute-start.20
  72.3 2.0 %collective-permute-start.21 = (bf16[2,64,1280]{2,1,0:T(8,128)(2,1)S(1)}, bf16[2,64,1280]{2,1,0:T(8,128)(2,1)S(1)}, u32[]{:S(2)}, u32[]{:S(2)}) collective-permute-start(bf16[2,64,1280]{2,1,0:T(8,128)(2,1)S(1)} %get-tuple-element.72), channel_id=1, source_target_pairs={{0,16},{8,56},{16,32},{24,8},{32,48},{40,24},{48,0},{56,40},{64,80... | collective-permute-start | bytes 983048 | tf_op jit(solution)/shard_map/ppermute | solution.py:68
  74.3 1.8 %place.3 = (bf16[2048,1280]{1,0:T(8,128)(2,1)}, f32[64,1280]{1,0:T(8,128)}, f32[64,1280]{1,0:T(8,128)}, f32[64,1280]{1,0:T(8,128)}, f32[64,1280]{1,0:T(8,128)}, /*index=5*/bf16[16,128]{1,0:T(8,128)(2,1)S(1)}) custom-call(bf16[6,64,1280]{2,1,0:T(8,128)(2,1)S(1)} %get-tuple-element.62.refs_0_, bf16[6,64,1280]{2,1,0:T(8,128)(2,1)S(1)} %collective-permute-done.17.refs_1_, ...), custom_call_target="tpu_custom_call" | custom-call | flops 1 | bytes 1 | tf_op jit(solution)/shard_map/place/pallas_call | solution.py:404
  76.1 5.7 %collective-permute-done.19.refs_1_ = bf16[2,64,1280]{2,1,0:T(8,128)(2,1)S(1)} collective-permute-done((bf16[2,64,1280]{2,1,0:T(8,128)(2,1)S(1)}, bf16[2,64,1280]{2,1,0:T(8,128)(2,1)S(1)}, u32[]{:S(2)}, u32[]{:S(2)}) %collective-permute-start.19) | collective-permute-done | bytes 327712 | tf_op jit(solution)/shard_map/ppermute | solution.py:68
  81.9 7.3 %collective-permute-done.20.refs_2_ = bf16[2,64,1280]{2,1,0:T(8,128)(2,1)S(1)} collective-permute-done((bf16[2,64,1280]{2,1,0:T(8,128)(2,1)S(1)}, bf16[2,64,1280]{2,1,0:T(8,128)(2,1)S(1)}, u32[]{:S(2)}, u32[]{:S(2)}) %collective-permute-start.20) | collective-permute-done | bytes 327712 | tf_op jit(solution)/shard_map/ppermute | solution.py:68
  89.3 0.9 collective-permute-start.22
  90.2 1.8 %place.4 = (bf16[2048,1280]{1,0:T(8,128)(2,1)}, bf16[16,128]{1,0:T(8,128)(2,1)}) custom-call(bf16[10,64,1280]{2,1,0:T(8,128)(2,1)S(1)} %join.1.refs_0_, bf16[2048,1280]{1,0:T(8,128)(2,1)} %get-tuple-element.74.refs_1_), custom_call_target="tpu_custom_call", output_to_operand_aliasing={{0}: (1, {})} | custom-call | flops 1 | bytes 1 | tf_op jit(solution)/shard_map/place/pallas_call | solution.py:404
  92.0 1.3 %collective-permute-done.22.refs_0_ = bf16[10,64,1280]{2,1,0:T(8,128)(2,1)S(1)} collective-permute-done((bf16[10,64,1280]{2,1,0:T(8,128)(2,1)S(1)}, bf16[10,64,1280]{2,1,0:T(8,128)(2,1)S(1)}, u32[]{:S(2)}, u32[]{:S(2)}) %collective-permute-start.22) | collective-permute-done | bytes 1638432 | tf_op jit(solution)/shard_map/ppermute | solution.py:68
  93.3 1.8 %place.5 = (bf16[2048,1280]{1,0:T(8,128)(2,1)}, bf16[16,128]{1,0:T(8,128)(2,1)}) custom-call(bf16[10,64,1280]{2,1,0:T(8,128)(2,1)S(1)} %collective-permute-done.22.refs_0_, bf16[2048,1280]{1,0:T(8,128)(2,1)} %get-tuple-element.75.refs_1_), custom_call_target="tpu_custom_call", output_to_operand_aliasing={{0}: (1, {})} | custom-call | flops 1 | bytes 1 | tf_op jit(solution)/shard_map/place/pallas_call | solution.py:404
  (34 shorter events, 2.7 us)
Async XLA Ops:
  6.2 7.1 %collective-permute-start = (bf16[8,64,1280]{2,1,0:T(8,128)(2,1)S(1)}, bf16[8,64,1280]{2,1,0:T(8,128)(2,1)S(1)}, u32[]{:S(2)}, u32[]{:S(2)}) collective-permute-start(bf16[8,64,1280]{2,1,0:T(8,128)(2,1)S(1)} %get-tuple-element.42._), channel_id=1, source_target_pairs={{0,8},{8,0},{16,24},{24,16},{32,40},{40,32},{48,56},{56,48},{64,72... | collective-permute-start | bytes 3932168 | tf_op jit(solution)/shard_map/ppermute | solution.py:68
  11.1 6.7 %collective-permute-start.1 = (bf16[4,64,1280]{2,1,0:T(8,128)(2,1)S(1)}, bf16[4,64,1280]{2,1,0:T(8,128)(2,1)S(1)}, u32[]{:S(2)}, u32[]{:S(2)}) collective-permute-start(bf16[4,64,1280]{2,1,0:T(8,128)(2,1)S(1)} %get-tuple-element.47._), channel_id=1, source_target_pairs={{0,8},{8,0},{16,24},{24,16},{32,40},{40,32},{48,56},{56,48},{64,72... | collective-permute-start | bytes 1966088 | tf_op jit(solution)/shard_map/ppermute | solution.py:68
  12.7 9.6 %collective-permute-start.2 = (bf16[4,64,1280]{2,1,0:T(8,128)(2,1)S(1)}, bf16[4,64,1280]{2,1,0:T(8,128)(2,1)S(1)}, u32[]{:S(2)}, u32[]{:S(2)}) collective-permute-start(bf16[4,64,1280]{2,1,0:T(8,128)(2,1)S(1)} %get-tuple-element.49), channel_id=1, source_target_pairs={{0,8},{8,0},{16,24},{24,16},{32,40},{40,32},{48,56},{56,48},{64,72... | collective-permute-start | bytes 1966088 | tf_op jit(solution)/shard_map/ppermute | solution.py:68
  13.4 21.3 %collective-permute-start.6 = (bf16[4,64,1280]{2,1,0:T(8,128)(2,1)S(1)}, bf16[4,64,1280]{2,1,0:T(8,128)(2,1)S(1)}, u32[]{:S(2)}, u32[]{:S(2)}) collective-permute-start(bf16[4,64,1280]{2,1,0:T(8,128)(2,1)S(1)} %row_sum.1), channel_id=1, source_target_pairs={{0,64},{8,200},{16,80},{24,216},{32,96},{40,232},{48,112},{56,248}... | collective-permute-start | bytes 1966088 | tf_op jit(solution)/shard_map/ppermute | solution.py:68
  18.0 9.8 %collective-permute-start.3 = (bf16[2,64,1280]{2,1,0:T(8,128)(2,1)S(1)}, bf16[2,64,1280]{2,1,0:T(8,128)(2,1)S(1)}, u32[]{:S(2)}, u32[]{:S(2)}) collective-permute-start(bf16[2,64,1280]{2,1,0:T(8,128)(2,1)S(1)} %get-tuple-element.50), channel_id=1, source_target_pairs={{0,16},{8,56},{16,32},{24,8},{32,48},{40,24},{48,0},{56,40},{64,80... | collective-permute-start | bytes 983048 | tf_op jit(solution)/shard_map/ppermute | solution.py:68
  20.6 14.2 %collective-permute-start.4 = (bf16[2,64,1280]{2,1,0:T(8,128)(2,1)S(1)}, bf16[2,64,1280]{2,1,0:T(8,128)(2,1)S(1)}, u32[]{:S(2)}, u32[]{:S(2)}) collective-permute-start(bf16[2,64,1280]{2,1,0:T(8,128)(2,1)S(1)} %get-tuple-element.51), channel_id=1, source_target_pairs={{0,48},{8,24},{16,0},{24,40},{32,16},{40,56},{48,32},{56,8},{64,11... | collective-permute-start | bytes 983048 | tf_op jit(solution)/shard_map/ppermute | solution.py:68
  20.6 31.1 %copy-start = (f32[64,1280]{1,0:T(8,128)S(1)}, f32[64,1280]{1,0:T(8,128)}, u32[]{:S(2)}) copy-start(f32[64,1280]{1,0:T(8,128)} %refs_9_.1) | copy-start | bytes 983044
  20.6 31.1 %copy-start.1 = (f32[64,1280]{1,0:T(8,128)S(1)}, f32[64,1280]{1,0:T(8,128)}, u32[]{:S(2)}) copy-start(f32[64,1280]{1,0:T(8,128)} %refs_10_.1) | copy-start | bytes 983044
  20.6 31.1 %copy-start.2 = (f32[64,1280]{1,0:T(8,128)S(1)}, f32[64,1280]{1,0:T(8,128)}, u32[]{:S(2)}) copy-start(f32[64,1280]{1,0:T(8,128)} %refs_11_.1) | copy-start | bytes 983044
  20.6 14.1 %collective-permute-start.5 = (bf16[2,64,1280]{2,1,0:T(8,128)(2,1)S(1)}, bf16[2,64,1280]{2,1,0:T(8,128)(2,1)S(1)}, u32[]{:S(2)}, u32[]{:S(2)}) collective-permute-start(bf16[2,64,1280]{2,1,0:T(8,128)(2,1)S(1)} %get-tuple-element.52), channel_id=1, source_target_pairs={{0,32},{8,40},{16,48},{24,56},{32,0},{40,8},{48,16},{56,24},{64,96... | collective-permute-start | bytes 983048 | tf_op jit(solution)/shard_map/ppermute | solution.py:68
  35.2 9.6 %collective-permute-start.7 = (bf16[64,1280]{1,0:T(8,128)(2,1)S(1)}, bf16[64,1280]{1,0:T(8,128)(2,1)S(1)}, u32[]{:S(2)}, u32[]{:S(2)}) collective-permute-start(bf16[64,1280]{1,0:T(8,128)(2,1)S(1)} %get-tuple-element.54), channel_id=1, source_target_pairs={{0,192},{8,72},{16,208},{24,88},{32,224},{40,104},{48,240},{56,120... | collective-permute-start | bytes 491528 | tf_op jit(solution)/shard_map/ppermute | solution.py:68
  35.4 12.4 %collective-permute-start.8 = (bf16[64,1280]{1,0:T(8,128)(2,1)S(1)}, bf16[64,1280]{1,0:T(8,128)(2,1)S(1)}, u32[]{:S(2)}, u32[]{:S(2)}) collective-permute-start(bf16[64,1280]{1,0:T(8,128)(2,1)S(1)} %get-tuple-element.55), channel_id=1, source_target_pairs={{0,128},{8,136},{16,144},{24,152},{32,160},{40,168},{48,176},{56,1... | collective-permute-start | bytes 491528 | tf_op jit(solution)/shard_map/ppermute | solution.py:68
  40.0 7.8 %collective-permute-start.10 = (bf16[64,1280]{1,0:T(8,128)(2,1)S(1)}, bf16[64,1280]{1,0:T(8,128)(2,1)S(1)}, u32[]{:S(2)}, u32[]{:S(2)}) collective-permute-start(bf16[64,1280]{1,0:T(8,128)(2,1)S(1)} %get-tuple-element.57), channel_id=1, source_target_pairs={{0,16},{8,56},{16,32},{24,8},{32,48},{40,24},{48,0},{56,40},{64,80... | collective-permute-start | bytes 491528 | tf_op jit(solution)/shard_map/ppermute | solution.py:68
  42.1 9.5 %collective-permute-start.11 = (bf16[64,1280]{1,0:T(8,128)(2,1)S(1)}, bf16[64,1280]{1,0:T(8,128)(2,1)S(1)}, u32[]{:S(2)}, u32[]{:S(2)}) collective-permute-start(bf16[64,1280]{1,0:T(8,128)(2,1)S(1)} %get-tuple-element.58), channel_id=1, source_target_pairs={{0,48},{8,24},{16,0},{24,40},{32,16},{40,56},{48,32},{56,8},{64,11... | collective-permute-start | bytes 491528 | tf_op jit(solution)/shard_map/ppermute | solution.py:68
  42.2 9.5 %collective-permute-start.9 = (bf16[64,1280]{1,0:T(8,128)(2,1)S(1)}, bf16[64,1280]{1,0:T(8,128)(2,1)S(1)}, u32[]{:S(2)}, u32[]{:S(2)}) collective-permute-start(bf16[64,1280]{1,0:T(8,128)(2,1)S(1)} %get-tuple-element.56), channel_id=1, source_target_pairs={{0,32},{8,40},{16,48},{24,56},{32,0},{40,8},{48,16},{56,24},{64,96... | collective-permute-start | bytes 491528 | tf_op jit(solution)/shard_map/ppermute | solution.py:68
  52.4 9.8 %collective-permute-start.15 = (bf16[64,1280]{1,0:T(8,128)(2,1)S(1)}, bf16[64,1280]{1,0:T(8,128)(2,1)S(1)}, u32[]{:S(2)}, u32[]{:S(2)}) collective-permute-start(bf16[64,1280]{1,0:T(8,128)(2,1)S(1)} %get-tuple-element.61.w), channel_id=1, source_target_pairs={{0,128},{8,136},{16,144},{24,152},{32,160},{40,168},{48,176},{56,1... | collective-permute-start | bytes 491528 | tf_op jit(solution)/shard_map/ppermute | solution.py:68
  53.0 14.5 %collective-permute-start.16 = (bf16[64,1280]{1,0:T(8,128)(2,1)S(1)}, bf16[64,1280]{1,0:T(8,128)(2,1)S(1)}, u32[]{:S(2)}, u32[]{:S(2)}) collective-permute-start(bf16[64,1280]{1,0:T(8,128)(2,1)S(1)} %get-tuple-element.61.w), channel_id=1, source_target_pairs={{0,64},{8,200},{16,80},{24,216},{32,96},{40,232},{48,112},{56,248}... | collective-permute-start | bytes 491528 | tf_op jit(solution)/shard_map/ppermute | solution.py:68
  57.6 9.8 %collective-permute-start.12 = (bf16[64,1280]{1,0:T(8,128)(2,1)S(1)}, bf16[64,1280]{1,0:T(8,128)(2,1)S(1)}, u32[]{:S(2)}, u32[]{:S(2)}) collective-permute-start(bf16[64,1280]{1,0:T(8,128)(2,1)S(1)} %get-tuple-element.61.w), channel_id=1, source_target_pairs={{0,48},{8,24},{16,0},{24,40},{32,16},{40,56},{48,32},{56,8},{64,11... | collective-permute-start | bytes 491528 | tf_op jit(solution)/shard_map/ppermute | solution.py:68
  57.7 9.9 %collective-permute-start.13 = (bf16[64,1280]{1,0:T(8,128)(2,1)S(1)}, bf16[64,1280]{1,0:T(8,128)(2,1)S(1)}, u32[]{:S(2)}, u32[]{:S(2)}) collective-permute-start(bf16[64,1280]{1,0:T(8,128)(2,1)S(1)} %get-tuple-element.61.w), channel_id=1, source_target_pairs={{0,16},{8,56},{16,32},{24,8},{32,48},{40,24},{48,0},{56,40},{64,80... | collective-permute-start | bytes 491528 | tf_op jit(solution)/shard_map/ppermute | solution.py:68
  60.3 7.8 %collective-permute-start.14 = (bf16[64,1280]{1,0:T(8,128)(2,1)S(1)}, bf16[64,1280]{1,0:T(8,128)(2,1)S(1)}, u32[]{:S(2)}, u32[]{:S(2)}) collective-permute-start(bf16[64,1280]{1,0:T(8,128)(2,1)S(1)} %get-tuple-element.61.w), channel_id=1, source_target_pairs={{0,32},{8,40},{16,48},{24,56},{32,0},{40,8},{48,16},{56,24},{64,96... | collective-permute-start | bytes 491528 | tf_op jit(solution)/shard_map/ppermute | solution.py:68
  68.3 6.0 %collective-permute-start.17 = (bf16[6,64,1280]{2,1,0:T(8,128)(2,1)S(1)}, bf16[6,64,1280]{2,1,0:T(8,128)(2,1)S(1)}, u32[]{:S(2)}, u32[]{:S(2)}) collective-permute-start(bf16[6,64,1280]{2,1,0:T(8,128)(2,1)S(1)} %get-tuple-element.62.refs_0_), channel_id=1, source_target_pairs={{0,8},{8,0},{16,24},{24,16},{32,40},{40,32},{48,56},{56,48},{64,72... | collective-permute-start | bytes 2949128 | tf_op jit(solution)/shard_map/ppermute | solution.py:68
  70.1 19.0 %collective-permute-start.18 = (bf16[4,64,1280]{2,1,0:T(8,128)(2,1)S(1)}, bf16[4,64,1280]{2,1,0:T(8,128)(2,1)S(1)}, u32[]{:S(2)}, u32[]{:S(2)}) collective-permute-start(bf16[4,64,1280]{2,1,0:T(8,128)(2,1)S(1)} %get-tuple-element.71), channel_id=1, source_target_pairs={{0,192},{8,72},{16,208},{24,88},{32,224},{40,104},{48,240},{56,120... | collective-permute-start | bytes 1966088 | tf_op jit(solution)/shard_map/ppermute | solution.py:68
  71.6 10.3 %collective-permute-start.19 = (bf16[2,64,1280]{2,1,0:T(8,128)(2,1)S(1)}, bf16[2,64,1280]{2,1,0:T(8,128)(2,1)S(1)}, u32[]{:S(2)}, u32[]{:S(2)}) collective-permute-start(bf16[2,64,1280]{2,1,0:T(8,128)(2,1)S(1)} %get-tuple-element.72), channel_id=1, source_target_pairs={{0,32},{8,40},{16,48},{24,56},{32,0},{40,8},{48,16},{56,24},{64,96... | collective-permute-start | bytes 983048 | tf_op jit(solution)/shard_map/ppermute | solution.py:68
  71.6 17.5 %collective-permute-start.20 = (bf16[2,64,1280]{2,1,0:T(8,128)(2,1)S(1)}, bf16[2,64,1280]{2,1,0:T(8,128)(2,1)S(1)}, u32[]{:S(2)}, u32[]{:S(2)}) collective-permute-start(bf16[2,64,1280]{2,1,0:T(8,128)(2,1)S(1)} %get-tuple-element.72), channel_id=1, source_target_pairs={{0,48},{8,24},{16,0},{24,40},{32,16},{40,56},{48,32},{56,8},{64,11... | collective-permute-start | bytes 983048 | tf_op jit(solution)/shard_map/ppermute | solution.py:68
  72.3 16.8 %collective-permute-start.21 = (bf16[2,64,1280]{2,1,0:T(8,128)(2,1)S(1)}, bf16[2,64,1280]{2,1,0:T(8,128)(2,1)S(1)}, u32[]{:S(2)}, u32[]{:S(2)}) collective-permute-start(bf16[2,64,1280]{2,1,0:T(8,128)(2,1)S(1)} %get-tuple-element.72), channel_id=1, source_target_pairs={{0,16},{8,56},{16,32},{24,8},{32,48},{40,24},{48,0},{56,40},{64,80... | collective-permute-start | bytes 983048 | tf_op jit(solution)/shard_map/ppermute | solution.py:68
  89.3 4.1 %collective-permute-start.22 = (bf16[10,64,1280]{2,1,0:T(8,128)(2,1)S(1)}, bf16[10,64,1280]{2,1,0:T(8,128)(2,1)S(1)}, u32[]{:S(2)}, u32[]{:S(2)}) collective-permute-start(bf16[10,64,1280]{2,1,0:T(8,128)(2,1)S(1)} %join.1.refs_0_), channel_id=1, source_target_pairs={{0,8},{8,0},{16,24},{24,16},{32,40},{40,32},{48,56},{56,48},{64,72... | collective-permute-start | bytes 4915208 | tf_op jit(solution)/shard_map/ppermute | solution.py:68

commit v6 on v5

--- a/solution.py
+++ b/solution.py
@@ -233,7 +233,7 @@
     )(*held(*parts))
 
 
-def middle_kernel(mine, other, mine_2, other_2, mine_0, other_0, xa, xb, x2, row, *outs):
+def middle_kernel(mine, other, mine_2, other_2, mine_0, other_0, x2, xa, xb, row, *outs):
     zb_out, z2_out, xa_out, xb_out, x2_out, own_out = outs
     _, _, core = place_of()
     zb_out[...] = add(mine[NX], other[NX], xa[0], xb[0], x2[0])
@@ -428,7 +428,7 @@
     xa, xb, x2 = sides_sum(mine, other, mine_2, other_2)
     xa, xb, x2 = send(xa, dx="a"), send(xb, dx="b"), send(x2, dx=2)
     zb, z2, xa, xb, x2, own = middle_sum(
-        mine, other, mine_2, other_2, mine_0, other_0, xa, xb, x2, row
+        mine, other, mine_2, other_2, mine_0, other_0, x2, xa, xb, row
     )
     zb, z2 = send(zb, dz="b"), send(z2, dz=2)
     x2, xa, xb = send(x2, dx=2), send(xa, dx="a"), send(xb, dx="b")

time: 95.4 us -> 94.2 us (0.987)
  waiting for transfers between devices: 42.8 us -> 40.2 us
  starting transfers between devices: 35.6 us -> 37.1 us
    ppermute x23, waiting for transfers between devices: 42.8 us -> 40.2 us  [send(): return lax.ppermute(value, 'replica', replica_perm(dx, dz, dc))]
    ppermute x23, starting transfers between devices: 35.6 us -> 37.1 us  [send(): return lax.ppermute(value, 'replica', replica_perm(dx, dz, dc))]
  transfers between devices with their start and end apart: 23 -> 23, of which waited for: 12 -> 9; matrix products, arithmetic and copies ran while one was open for 0% -> 0% of each run, Pallas kernels for 7% -> 8%
where the time goes in v6:
time: 94.2 us
  waiting for transfers between devices  40.2 us (43%)
  starting transfers between devices  37.1 us (39%)
  Pallas kernels  15.9 us (17%)
    ppermute x23, waiting for transfers between devices, send(): return lax.ppermute(value, 'replica', replica_perm(dx, dz, dc))  40.2 us
    ppermute x23, starting transfers between devices, send(): return lax.ppermute(value, 'replica', replica_perm(dx, dz, dc))  37.1 us
    pallas_call x1, Pallas kernels, quantized_first(): pl.pallas_call(first_kernel, in_specs=[HBM] * 5, out_specs=[FULL] * 7, ou...  5.54 us
    pallas_call x3, Pallas kernels, placed(): pl.pallas_call(functools.partial(place_kernel, names, flips, count, chain...  5.5 us
    pallas_call x2, Pallas kernels, quantized_next(): pl.pallas_call(functools.partial(next_kernel, dz), in_specs=[FULL] * 4, o...  3.08 us
  transfers between devices with their start and end apart: 23, of which 9 were waited for; matrix products, arithmetic and copies ran while one was open for 0% of the time, Pallas kernels for 8%

profile of v6, /device:TPU:1, one launch (start us, length us, event | category | flops | bytes accessed | tf_op | source)
XLA Modules:
  0.0 94.2 jit_solution(4706100772685684585)
XLA Ops:
  0.6 5.5 %quantize_first.1 = (bf16[8,64,1280]{2,1,0:T(8,128)(2,1)S(1)}, bf16[8,64,1280]{2,1,0:T(8,128)(2,1)S(1)}, bf16[768,2048]{1,0:T(8,128)(2,1)S(1)}, bf16[768,1280]{1...) custom-call(bf16[768,2048]{1,0:T(8,128)(2,1)} %act_far.1, ...), custom_call_target="tpu_custom_call" | custom-call | flops 1 | bytes 1 | tf_op jit(solution)/shard_map/quantize_first/pallas_call | solution.py:152
  6.2 3.3 %collective-permute-start = (bf16[8,64,1280]{2,1,0:T(8,128)(2,1)S(1)}, bf16[8,64,1280]{2,1,0:T(8,128)(2,1)S(1)}, u32[]{:S(2)}, u32[]{:S(2)}) collective-permute-start(bf16[8,64,1280]{2,1,0:T(8,128)(2,1)S(1)} %get-tuple-element.42._), channel_id=1, source_target_pairs={{0,8},{8,0},{16,24},{24,16},{32,40},{40,32},{48,56},{56,48},{64,72... | collective-permute-start | bytes 3932168 | tf_op jit(solution)/shard_map/ppermute | solution.py:68
  9.5 1.5 %quantize_next.2 = (bf16[4,64,1280]{2,1,0:T(8,128)(2,1)S(1)}, bf16[4,64,1280]{2,1,0:T(8,128)(2,1)S(1)}) custom-call(bf16[768,2048]{1,0:T(8,128)(2,1)S(1)} %get-tuple-element.43.act, bf16[768,1280]{1,0:T(8,128)(2,1)S(1)} %get-tuple-element.44.rotated, s32[5,2048]{1,0:T(8,128)S(1)} %get-tuple-element.45.exps.refs_6_, bf16[8,64,1280]{2,1,0:T(8,128)(2,1)S(1)} %get-tuple-element.42._), custom_call_target="tpu_custom_call" | custom-call | flops 1 | bytes 1 | tf_op jit(solution)/shard_map/quantize_next/pallas_call | solution.py:181
  11.2 1.5 %quantize_next.3 = (bf16[4,64,1280]{2,1,0:T(8,128)(2,1)S(1)}, bf16[4,64,1280]{2,1,0:T(8,128)(2,1)S(1)}) custom-call(bf16[768,2048]{1,0:T(8,128)(2,1)S(1)} %get-tuple-element.43.act, bf16[768,1280]{1,0:T(8,128)(2,1)S(1)} %get-tuple-element.44.rotated, s32[5,2048]{1,0:T(8,128)S(1)} %get-tuple-element.45.exps.refs_6_, bf16[4,64,1280]{2,1,0:T(8,128)(2,1)S(1)} %get-tuple-element.47._), custom_call_target="tpu_custom_call" | custom-call | flops 1 | bytes 1 | tf_op jit(solution)/shard_map/quantize_next/pallas_call | solution.py:181
  13.4 4.3 %collective-permute-start.6 = (bf16[4,64,1280]{2,1,0:T(8,128)(2,1)S(1)}, bf16[4,64,1280]{2,1,0:T(8,128)(2,1)S(1)}, u32[]{:S(2)}, u32[]{:S(2)}) collective-permute-start(bf16[4,64,1280]{2,1,0:T(8,128)(2,1)S(1)} %row_sum.1), channel_id=1, source_target_pairs={{0,64},{8,200},{16,80},{24,216},{32,96},{40,232},{48,112},{56,248}... | collective-permute-start | bytes 1966088 | tf_op jit(solution)/shard_map/ppermute | solution.py:68
  18.0 2.8 %collective-permute-start.3 = (bf16[2,64,1280]{2,1,0:T(8,128)(2,1)S(1)}, bf16[2,64,1280]{2,1,0:T(8,128)(2,1)S(1)}, u32[]{:S(2)}, u32[]{:S(2)}) collective-permute-start(bf16[2,64,1280]{2,1,0:T(8,128)(2,1)S(1)} %get-tuple-element.50), channel_id=1, source_target_pairs={{0,32},{8,40},{16,48},{24,56},{32,0},{40,8},{48,16},{56,24},{64,96... | collective-permute-start | bytes 983048 | tf_op jit(solution)/shard_map/ppermute | solution.py:68
  20.8 0.9 collective-permute-start.4
  21.7 0.6 collective-permute-start.5
  22.3 6.8 %collective-permute-done.3.x2 = bf16[2,64,1280]{2,1,0:T(8,128)(2,1)S(1)} collective-permute-done((bf16[2,64,1280]{2,1,0:T(8,128)(2,1)S(1)}, bf16[2,64,1280]{2,1,0:T(8,128)(2,1)S(1)}, u32[]{:S(2)}, u32[]{:S(2)}) %collective-permute-start.3) | collective-permute-done | bytes 327712 | tf_op jit(solution)/shard_map/ppermute | solution.py:68
  29.1 4.7 %collective-permute-done.4.xa = bf16[2,64,1280]{2,1,0:T(8,128)(2,1)S(1)} collective-permute-done((bf16[2,64,1280]{2,1,0:T(8,128)(2,1)S(1)}, bf16[2,64,1280]{2,1,0:T(8,128)(2,1)S(1)}, u32[]{:S(2)}, u32[]{:S(2)}) %collective-permute-start.4) | collective-permute-done | bytes 327712 | tf_op jit(solution)/shard_map/ppermute | solution.py:68
  34.7 4.9 %collective-permute-start.8 = (bf16[64,1280]{1,0:T(8,128)(2,1)S(1)}, bf16[64,1280]{1,0:T(8,128)(2,1)S(1)}, u32[]{:S(2)}, u32[]{:S(2)}) collective-permute-start(bf16[64,1280]{1,0:T(8,128)(2,1)S(1)} %get-tuple-element.55), channel_id=1, source_target_pairs={{0,128},{8,136},{16,144},{24,152},{32,160},{40,168},{48,176},{56,1... | collective-permute-start | bytes 491528 | tf_op jit(solution)/shard_map/ppermute | solution.py:68
  39.6 2.5 %collective-permute-start.10 = (bf16[64,1280]{1,0:T(8,128)(2,1)S(1)}, bf16[64,1280]{1,0:T(8,128)(2,1)S(1)}, u32[]{:S(2)}, u32[]{:S(2)}) collective-permute-start(bf16[64,1280]{1,0:T(8,128)(2,1)S(1)} %get-tuple-element.57), channel_id=1, source_target_pairs={{0,16},{8,56},{16,32},{24,8},{32,48},{40,24},{48,0},{56,40},{64,80... | collective-permute-start | bytes 491528 | tf_op jit(solution)/shard_map/ppermute | solution.py:68
  42.0 1.3 %collective-permute-start.9 = (bf16[64,1280]{1,0:T(8,128)(2,1)S(1)}, bf16[64,1280]{1,0:T(8,128)(2,1)S(1)}, u32[]{:S(2)}, u32[]{:S(2)}) collective-permute-start(bf16[64,1280]{1,0:T(8,128)(2,1)S(1)} %get-tuple-element.56), channel_id=1, source_target_pairs={{0,32},{8,40},{16,48},{24,56},{32,0},{40,8},{48,16},{56,24},{64,96... | collective-permute-start | bytes 491528 | tf_op jit(solution)/shard_map/ppermute | solution.py:68
  43.3 5.2 %collective-permute-done.8.refs_0_.refs_2_ = bf16[64,1280]{1,0:T(8,128)(2,1)S(1)} collective-permute-done((bf16[64,1280]{1,0:T(8,128)(2,1)S(1)}, bf16[64,1280]{1,0:T(8,128)(2,1)S(1)}, u32[]{:S(2)}, u32[]{:S(2)}) %collective-permute-start.8) | collective-permute-done | bytes 163872 | tf_op jit(solution)/shard_map/ppermute | solution.py:68
  48.6 2.9 %collective-permute-done.9.refs_3_ = bf16[64,1280]{1,0:T(8,128)(2,1)S(1)} collective-permute-done((bf16[64,1280]{1,0:T(8,128)(2,1)S(1)}, bf16[64,1280]{1,0:T(8,128)(2,1)S(1)}, u32[]{:S(2)}, u32[]{:S(2)}) %collective-permute-start.9) | collective-permute-done | bytes 163872 | tf_op jit(solution)/shard_map/ppermute | solution.py:68
  51.4 0.8 update.1
  52.2 0.6 collective-permute-start.15
  52.8 4.4 %collective-permute-start.16 = (bf16[64,1280]{1,0:T(8,128)(2,1)S(1)}, bf16[64,1280]{1,0:T(8,128)(2,1)S(1)}, u32[]{:S(2)}, u32[]{:S(2)}) collective-permute-start(bf16[64,1280]{1,0:T(8,128)(2,1)S(1)} %get-tuple-element.61.w), channel_id=1, source_target_pairs={{0,64},{8,200},{16,80},{24,216},{32,96},{40,232},{48,112},{56,248}... | collective-permute-start | bytes 491528 | tf_op jit(solution)/shard_map/ppermute | solution.py:68
  57.2 0.9 collective-permute-start.12
  58.1 1.8 %collective-permute-start.13 = (bf16[64,1280]{1,0:T(8,128)(2,1)S(1)}, bf16[64,1280]{1,0:T(8,128)(2,1)S(1)}, u32[]{:S(2)}, u32[]{:S(2)}) collective-permute-start(bf16[64,1280]{1,0:T(8,128)(2,1)S(1)} %get-tuple-element.61.w), channel_id=1, source_target_pairs={{0,16},{8,56},{16,32},{24,8},{32,48},{40,24},{48,0},{56,40},{64,80... | collective-permute-start | bytes 491528 | tf_op jit(solution)/shard_map/ppermute | solution.py:68
  59.9 0.6 collective-permute-start.14
  60.5 1.8 %collective-permute-done.15.refs_0_.z2 = bf16[64,1280]{1,0:T(8,128)(2,1)S(1)} collective-permute-done((bf16[64,1280]{1,0:T(8,128)(2,1)S(1)}, bf16[64,1280]{1,0:T(8,128)(2,1)S(1)}, u32[]{:S(2)}, u32[]{:S(2)}) %collective-permute-start.15) | collective-permute-done | bytes 163872 | tf_op jit(solution)/shard_map/ppermute | solution.py:68
  62.3 6.0 %collective-permute-done.16.refs_1_.za = bf16[64,1280]{1,0:T(8,128)(2,1)S(1)} collective-permute-done((bf16[64,1280]{1,0:T(8,128)(2,1)S(1)}, bf16[64,1280]{1,0:T(8,128)(2,1)S(1)}, u32[]{:S(2)}, u32[]{:S(2)}) %collective-permute-start.16) | collective-permute-done | bytes 163872 | tf_op jit(solution)/shard_map/ppermute | solution.py:68
  68.5 1.6 %collective-permute-start.17 = (bf16[6,64,1280]{2,1,0:T(8,128)(2,1)S(1)}, bf16[6,64,1280]{2,1,0:T(8,128)(2,1)S(1)}, u32[]{:S(2)}, u32[]{:S(2)}) collective-permute-start(bf16[6,64,1280]{2,1,0:T(8,128)(2,1)S(1)} %get-tuple-element.62.refs_0_), channel_id=1, source_target_pairs={{0,8},{8,0},{16,24},{24,16},{32,40},{40,32},{48,56},{56,48},{64,72... | collective-permute-start | bytes 2949128 | tf_op jit(solution)/shard_map/ppermute | solution.py:68
  70.2 2.2 %collective-permute-start.19 = (bf16[2,64,1280]{2,1,0:T(8,128)(2,1)S(1)}, bf16[2,64,1280]{2,1,0:T(8,128)(2,1)S(1)}, u32[]{:S(2)}, u32[]{:S(2)}) collective-permute-start(bf16[2,64,1280]{2,1,0:T(8,128)(2,1)S(1)} %get-tuple-element.72), channel_id=1, source_target_pairs={{0,32},{8,40},{16,48},{24,56},{32,0},{40,8},{48,16},{56,24},{64,96... | collective-permute-start | bytes 983048 | tf_op jit(solution)/shard_map/ppermute | solution.py:68
  72.4 2.7 %collective-permute-start.21 = (bf16[2,64,1280]{2,1,0:T(8,128)(2,1)S(1)}, bf16[2,64,1280]{2,1,0:T(8,128)(2,1)S(1)}, u32[]{:S(2)}, u32[]{:S(2)}) collective-permute-start(bf16[2,64,1280]{2,1,0:T(8,128)(2,1)S(1)} %get-tuple-element.72), channel_id=1, source_target_pairs={{0,16},{8,56},{16,32},{24,8},{32,48},{40,24},{48,0},{56,40},{64,80... | collective-permute-start | bytes 983048 | tf_op jit(solution)/shard_map/ppermute | solution.py:68
  75.0 1.8 %place.3 = (bf16[2048,1280]{1,0:T(8,128)(2,1)}, f32[64,1280]{1,0:T(8,128)}, f32[64,1280]{1,0:T(8,128)}, f32[64,1280]{1,0:T(8,128)}, f32[64,1280]{1,0:T(8,128)}, /*index=5*/bf16[16,128]{1,0:T(8,128)(2,1)S(1)}) custom-call(bf16[6,64,1280]{2,1,0:T(8,128)(2,1)S(1)} %get-tuple-element.62.refs_0_, bf16[6,64,1280]{2,1,0:T(8,128)(2,1)S(1)} %collective-permute-done.17.refs_1_, ...), custom_call_target="tpu_custom_call" | custom-call | flops 1 | bytes 1 | tf_op jit(solution)/shard_map/place/pallas_call | solution.py:404
  76.9 1.9 %collective-permute-done.19.refs_1_ = bf16[2,64,1280]{2,1,0:T(8,128)(2,1)S(1)} collective-permute-done((bf16[2,64,1280]{2,1,0:T(8,128)(2,1)S(1)}, bf16[2,64,1280]{2,1,0:T(8,128)(2,1)S(1)}, u32[]{:S(2)}, u32[]{:S(2)}) %collective-permute-start.19) | collective-permute-done | bytes 327712 | tf_op jit(solution)/shard_map/ppermute | solution.py:68
  78.8 9.5 %collective-permute-done.20.refs_2_ = bf16[2,64,1280]{2,1,0:T(8,128)(2,1)S(1)} collective-permute-done((bf16[2,64,1280]{2,1,0:T(8,128)(2,1)S(1)}, bf16[2,64,1280]{2,1,0:T(8,128)(2,1)S(1)}, u32[]{:S(2)}, u32[]{:S(2)}) %collective-permute-start.20) | collective-permute-done | bytes 327712 | tf_op jit(solution)/shard_map/ppermute | solution.py:68
  89.0 1.8 %place.4 = (bf16[2048,1280]{1,0:T(8,128)(2,1)}, bf16[16,128]{1,0:T(8,128)(2,1)}) custom-call(bf16[10,64,1280]{2,1,0:T(8,128)(2,1)S(1)} %join.1.refs_0_, bf16[2048,1280]{1,0:T(8,128)(2,1)} %get-tuple-element.74.refs_1_), custom_call_target="tpu_custom_call", output_to_operand_aliasing={{0}: (1, {})} | custom-call | flops 1 | bytes 1 | tf_op jit(solution)/shard_map/place/pallas_call | solution.py:404
  90.9 1.3 %collective-permute-done.22.refs_0_ = bf16[10,64,1280]{2,1,0:T(8,128)(2,1)S(1)} collective-permute-done((bf16[10,64,1280]{2,1,0:T(8,128)(2,1)S(1)}, bf16[10,64,1280]{2,1,0:T(8,128)(2,1)S(1)}, u32[]{:S(2)}, u32[]{:S(2)}) %collective-permute-start.22) | collective-permute-done | bytes 1638432 | tf_op jit(solution)/shard_map/ppermute | solution.py:68
  92.2 1.8 %place.5 = (bf16[2048,1280]{1,0:T(8,128)(2,1)}, bf16[16,128]{1,0:T(8,128)(2,1)}) custom-call(bf16[10,64,1280]{2,1,0:T(8,128)(2,1)S(1)} %collective-permute-done.22.refs_0_, bf16[2048,1280]{1,0:T(8,128)(2,1)} %get-tuple-element.75.refs_1_), custom_call_target="tpu_custom_call", output_to_operand_aliasing={{0}: (1, {})} | custom-call | flops 1 | bytes 1 | tf_op jit(solution)/shard_map/place/pallas_call | solution.py:404
  (34 shorter events, 2.8 us)
Async XLA Ops:
  6.2 7.1 %collective-permute-start = (bf16[8,64,1280]{2,1,0:T(8,128)(2,1)S(1)}, bf16[8,64,1280]{2,1,0:T(8,128)(2,1)S(1)}, u32[]{:S(2)}, u32[]{:S(2)}) collective-permute-start(bf16[8,64,1280]{2,1,0:T(8,128)(2,1)S(1)} %get-tuple-element.42._), channel_id=1, source_target_pairs={{0,8},{8,0},{16,24},{24,16},{32,40},{40,32},{48,56},{56,48},{64,72... | collective-permute-start | bytes 3932168 | tf_op jit(solution)/shard_map/ppermute | solution.py:68
  11.1 6.7 %collective-permute-start.1 = (bf16[4,64,1280]{2,1,0:T(8,128)(2,1)S(1)}, bf16[4,64,1280]{2,1,0:T(8,128)(2,1)S(1)}, u32[]{:S(2)}, u32[]{:S(2)}) collective-permute-start(bf16[4,64,1280]{2,1,0:T(8,128)(2,1)S(1)} %get-tuple-element.47._), channel_id=1, source_target_pairs={{0,8},{8,0},{16,24},{24,16},{32,40},{40,32},{48,56},{56,48},{64,72... | collective-permute-start | bytes 1966088 | tf_op jit(solution)/shard_map/ppermute | solution.py:68
  12.7 9.6 %collective-permute-start.2 = (bf16[4,64,1280]{2,1,0:T(8,128)(2,1)S(1)}, bf16[4,64,1280]{2,1,0:T(8,128)(2,1)S(1)}, u32[]{:S(2)}, u32[]{:S(2)}) collective-permute-start(bf16[4,64,1280]{2,1,0:T(8,128)(2,1)S(1)} %get-tuple-element.49), channel_id=1, source_target_pairs={{0,8},{8,0},{16,24},{24,16},{32,40},{40,32},{48,56},{56,48},{64,72... | collective-permute-start | bytes 1966088 | tf_op jit(solution)/shard_map/ppermute | solution.py:68
  13.4 20.4 %collective-permute-start.6 = (bf16[4,64,1280]{2,1,0:T(8,128)(2,1)S(1)}, bf16[4,64,1280]{2,1,0:T(8,128)(2,1)S(1)}, u32[]{:S(2)}, u32[]{:S(2)}) collective-permute-start(bf16[4,64,1280]{2,1,0:T(8,128)(2,1)S(1)} %row_sum.1), channel_id=1, source_target_pairs={{0,64},{8,200},{16,80},{24,216},{32,96},{40,232},{48,112},{56,248}... | collective-permute-start | bytes 1966088 | tf_op jit(solution)/shard_map/ppermute | solution.py:68
  18.0 11.1 %collective-permute-start.3 = (bf16[2,64,1280]{2,1,0:T(8,128)(2,1)S(1)}, bf16[2,64,1280]{2,1,0:T(8,128)(2,1)S(1)}, u32[]{:S(2)}, u32[]{:S(2)}) collective-permute-start(bf16[2,64,1280]{2,1,0:T(8,128)(2,1)S(1)} %get-tuple-element.50), channel_id=1, source_target_pairs={{0,32},{8,40},{16,48},{24,56},{32,0},{40,8},{48,16},{56,24},{64,96... | collective-permute-start | bytes 983048 | tf_op jit(solution)/shard_map/ppermute | solution.py:68
  20.8 13.0 %collective-permute-start.4 = (bf16[2,64,1280]{2,1,0:T(8,128)(2,1)S(1)}, bf16[2,64,1280]{2,1,0:T(8,128)(2,1)S(1)}, u32[]{:S(2)}, u32[]{:S(2)}) collective-permute-start(bf16[2,64,1280]{2,1,0:T(8,128)(2,1)S(1)} %get-tuple-element.51), channel_id=1, source_target_pairs={{0,16},{8,56},{16,32},{24,8},{32,48},{40,24},{48,0},{56,40},{64,80... | collective-permute-start | bytes 983048 | tf_op jit(solution)/shard_map/ppermute | solution.py:68
  21.7 29.7 %copy-start = (f32[64,1280]{1,0:T(8,128)S(1)}, f32[64,1280]{1,0:T(8,128)}, u32[]{:S(2)}) copy-start(f32[64,1280]{1,0:T(8,128)} %refs_9_.1) | copy-start | bytes 983044
  21.7 29.7 %copy-start.1 = (f32[64,1280]{1,0:T(8,128)S(1)}, f32[64,1280]{1,0:T(8,128)}, u32[]{:S(2)}) copy-start(f32[64,1280]{1,0:T(8,128)} %refs_10_.1) | copy-start | bytes 983044
  21.7 29.7 %copy-start.2 = (f32[64,1280]{1,0:T(8,128)S(1)}, f32[64,1280]{1,0:T(8,128)}, u32[]{:S(2)}) copy-start(f32[64,1280]{1,0:T(8,128)} %refs_11_.1) | copy-start | bytes 983044
  21.7 12.2 %collective-permute-start.5 = (bf16[2,64,1280]{2,1,0:T(8,128)(2,1)S(1)}, bf16[2,64,1280]{2,1,0:T(8,128)(2,1)S(1)}, u32[]{:S(2)}, u32[]{:S(2)}) collective-permute-start(bf16[2,64,1280]{2,1,0:T(8,128)(2,1)S(1)} %get-tuple-element.52), channel_id=1, source_target_pairs={{0,48},{8,24},{16,0},{24,40},{32,16},{40,56},{48,32},{56,8},{64,11... | collective-permute-start | bytes 983048 | tf_op jit(solution)/shard_map/ppermute | solution.py:68
  34.3 9.0 %collective-permute-start.7 = (bf16[64,1280]{1,0:T(8,128)(2,1)S(1)}, bf16[64,1280]{1,0:T(8,128)(2,1)S(1)}, u32[]{:S(2)}, u32[]{:S(2)}) collective-permute-start(bf16[64,1280]{1,0:T(8,128)(2,1)S(1)} %get-tuple-element.54), channel_id=1, source_target_pairs={{0,192},{8,72},{16,208},{24,88},{32,224},{40,104},{48,240},{56,120... | collective-permute-start | bytes 491528 | tf_op jit(solution)/shard_map/ppermute | solution.py:68
  34.7 13.9 %collective-permute-start.8 = (bf16[64,1280]{1,0:T(8,128)(2,1)S(1)}, bf16[64,1280]{1,0:T(8,128)(2,1)S(1)}, u32[]{:S(2)}, u32[]{:S(2)}) collective-permute-start(bf16[64,1280]{1,0:T(8,128)(2,1)S(1)} %get-tuple-element.55), channel_id=1, source_target_pairs={{0,128},{8,136},{16,144},{24,152},{32,160},{40,168},{48,176},{56,1... | collective-permute-start | bytes 491528 | tf_op jit(solution)/shard_map/ppermute | solution.py:68
  39.6 9.0 %collective-permute-start.10 = (bf16[64,1280]{1,0:T(8,128)(2,1)S(1)}, bf16[64,1280]{1,0:T(8,128)(2,1)S(1)}, u32[]{:S(2)}, u32[]{:S(2)}) collective-permute-start(bf16[64,1280]{1,0:T(8,128)(2,1)S(1)} %get-tuple-element.57), channel_id=1, source_target_pairs={{0,16},{8,56},{16,32},{24,8},{32,48},{40,24},{48,0},{56,40},{64,80... | collective-permute-start | bytes 491528 | tf_op jit(solution)/shard_map/ppermute | solution.py:68
  42.0 6.5 %collective-permute-start.11 = (bf16[64,1280]{1,0:T(8,128)(2,1)S(1)}, bf16[64,1280]{1,0:T(8,128)(2,1)S(1)}, u32[]{:S(2)}, u32[]{:S(2)}) collective-permute-start(bf16[64,1280]{1,0:T(8,128)(2,1)S(1)} %get-tuple-element.58), channel_id=1, source_target_pairs={{0,48},{8,24},{16,0},{24,40},{32,16},{40,56},{48,32},{56,8},{64,11... | collective-permute-start | bytes 491528 | tf_op jit(solution)/shard_map/ppermute | solution.py:68
  42.0 9.4 %collective-permute-start.9 = (bf16[64,1280]{1,0:T(8,128)(2,1)S(1)}, bf16[64,1280]{1,0:T(8,128)(2,1)S(1)}, u32[]{:S(2)}, u32[]{:S(2)}) collective-permute-start(bf16[64,1280]{1,0:T(8,128)(2,1)S(1)} %get-tuple-element.56), channel_id=1, source_target_pairs={{0,32},{8,40},{16,48},{24,56},{32,0},{40,8},{48,16},{56,24},{64,96... | collective-permute-start | bytes 491528 | tf_op jit(solution)/shard_map/ppermute | solution.py:68
  52.2 10.1 %collective-permute-start.15 = (bf16[64,1280]{1,0:T(8,128)(2,1)S(1)}, bf16[64,1280]{1,0:T(8,128)(2,1)S(1)}, u32[]{:S(2)}, u32[]{:S(2)}) collective-permute-start(bf16[64,1280]{1,0:T(8,128)(2,1)S(1)} %get-tuple-element.61.w), channel_id=1, source_target_pairs={{0,128},{8,136},{16,144},{24,152},{32,160},{40,168},{48,176},{56,1... | collective-permute-start | bytes 491528 | tf_op jit(solution)/shard_map/ppermute | solution.py:68
  52.8 15.5 %collective-permute-start.16 = (bf16[64,1280]{1,0:T(8,128)(2,1)S(1)}, bf16[64,1280]{1,0:T(8,128)(2,1)S(1)}, u32[]{:S(2)}, u32[]{:S(2)}) collective-permute-start(bf16[64,1280]{1,0:T(8,128)(2,1)S(1)} %get-tuple-element.61.w), channel_id=1, source_target_pairs={{0,64},{8,200},{16,80},{24,216},{32,96},{40,232},{48,112},{56,248}... | collective-permute-start | bytes 491528 | tf_op jit(solution)/shard_map/ppermute | solution.py:68
  57.2 11.1 %collective-permute-start.12 = (bf16[64,1280]{1,0:T(8,128)(2,1)S(1)}, bf16[64,1280]{1,0:T(8,128)(2,1)S(1)}, u32[]{:S(2)}, u32[]{:S(2)}) collective-permute-start(bf16[64,1280]{1,0:T(8,128)(2,1)S(1)} %get-tuple-element.61.w), channel_id=1, source_target_pairs={{0,48},{8,24},{16,0},{24,40},{32,16},{40,56},{48,32},{56,8},{64,11... | collective-permute-start | bytes 491528 | tf_op jit(solution)/shard_map/ppermute | solution.py:68
  58.1 10.2 %collective-permute-start.13 = (bf16[64,1280]{1,0:T(8,128)(2,1)S(1)}, bf16[64,1280]{1,0:T(8,128)(2,1)S(1)}, u32[]{:S(2)}, u32[]{:S(2)}) collective-permute-start(bf16[64,1280]{1,0:T(8,128)(2,1)S(1)} %get-tuple-element.61.w), channel_id=1, source_target_pairs={{0,16},{8,56},{16,32},{24,8},{32,48},{40,24},{48,0},{56,40},{64,80... | collective-permute-start | bytes 491528 | tf_op jit(solution)/shard_map/ppermute | solution.py:68
  59.9 8.5 %collective-permute-start.14 = (bf16[64,1280]{1,0:T(8,128)(2,1)S(1)}, bf16[64,1280]{1,0:T(8,128)(2,1)S(1)}, u32[]{:S(2)}, u32[]{:S(2)}) collective-permute-start(bf16[64,1280]{1,0:T(8,128)(2,1)S(1)} %get-tuple-element.61.w), channel_id=1, source_target_pairs={{0,32},{8,40},{16,48},{24,56},{32,0},{40,8},{48,16},{56,24},{64,96... | collective-permute-start | bytes 491528 | tf_op jit(solution)/shard_map/ppermute | solution.py:68
  68.5 6.5 %collective-permute-start.17 = (bf16[6,64,1280]{2,1,0:T(8,128)(2,1)S(1)}, bf16[6,64,1280]{2,1,0:T(8,128)(2,1)S(1)}, u32[]{:S(2)}, u32[]{:S(2)}) collective-permute-start(bf16[6,64,1280]{2,1,0:T(8,128)(2,1)S(1)} %get-tuple-element.62.refs_0_), channel_id=1, source_target_pairs={{0,8},{8,0},{16,24},{24,16},{32,40},{40,32},{48,56},{56,48},{64,72... | collective-permute-start | bytes 2949128 | tf_op jit(solution)/shard_map/ppermute | solution.py:68
  70.1 18.3 %collective-permute-start.18 = (bf16[4,64,1280]{2,1,0:T(8,128)(2,1)S(1)}, bf16[4,64,1280]{2,1,0:T(8,128)(2,1)S(1)}, u32[]{:S(2)}, u32[]{:S(2)}) collective-permute-start(bf16[4,64,1280]{2,1,0:T(8,128)(2,1)S(1)} %get-tuple-element.71), channel_id=1, source_target_pairs={{0,192},{8,72},{16,208},{24,88},{32,224},{40,104},{48,240},{56,120... | collective-permute-start | bytes 1966088 | tf_op jit(solution)/shard_map/ppermute | solution.py:68
  70.2 8.6 %collective-permute-start.19 = (bf16[2,64,1280]{2,1,0:T(8,128)(2,1)S(1)}, bf16[2,64,1280]{2,1,0:T(8,128)(2,1)S(1)}, u32[]{:S(2)}, u32[]{:S(2)}) collective-permute-start(bf16[2,64,1280]{2,1,0:T(8,128)(2,1)S(1)} %get-tuple-element.72), channel_id=1, source_target_pairs={{0,32},{8,40},{16,48},{24,56},{32,0},{40,8},{48,16},{56,24},{64,96... | collective-permute-start | bytes 983048 | tf_op jit(solution)/shard_map/ppermute | solution.py:68
  72.3 16.0 %collective-permute-start.20 = (bf16[2,64,1280]{2,1,0:T(8,128)(2,1)S(1)}, bf16[2,64,1280]{2,1,0:T(8,128)(2,1)S(1)}, u32[]{:S(2)}, u32[]{:S(2)}) collective-permute-start(bf16[2,64,1280]{2,1,0:T(8,128)(2,1)S(1)} %get-tuple-element.72), channel_id=1, source_target_pairs={{0,48},{8,24},{16,0},{24,40},{32,16},{40,56},{48,32},{56,8},{64,11... | collective-permute-start | bytes 983048 | tf_op jit(solution)/shard_map/ppermute | solution.py:68
  72.4 16.0 %collective-permute-start.21 = (bf16[2,64,1280]{2,1,0:T(8,128)(2,1)S(1)}, bf16[2,64,1280]{2,1,0:T(8,128)(2,1)S(1)}, u32[]{:S(2)}, u32[]{:S(2)}) collective-permute-start(bf16[2,64,1280]{2,1,0:T(8,128)(2,1)S(1)} %get-tuple-element.72), channel_id=1, source_target_pairs={{0,16},{8,56},{16,32},{24,8},{32,48},{40,24},{48,0},{56,40},{64,80... | collective-permute-start | bytes 983048 | tf_op jit(solution)/shard_map/ppermute | solution.py:68
  88.5 3.7 %collective-permute-start.22 = (bf16[10,64,1280]{2,1,0:T(8,128)(2,1)S(1)}, bf16[10,64,1280]{2,1,0:T(8,128)(2,1)S(1)}, u32[]{:S(2)}, u32[]{:S(2)}) collective-permute-start(bf16[10,64,1280]{2,1,0:T(8,128)(2,1)S(1)} %join.1.refs_0_), channel_id=1, source_target_pairs={{0,8},{8,0},{16,24},{24,16},{32,40},{40,32},{48,56},{56,48},{64,72... | collective-permute-start | bytes 4915208 | tf_op jit(solution)/shard_map/ppermute | solution.py:68
